TPU v7x, 32 devices: a whole 2x2x4 slice. The times are simulated.
32 devices in a mesh: neur: 2 (over x), tm: 16 (over z, y, core).
Axes of the slice: x: 2, y: 2, z: 4, core: 2. Of those that a mesh axis runs over, the one named last changes fastest.
Arguments:
- counts: float32 [512, 8192], P('neur', 'tm'), may hold values from 200 to 10000
- motifs: float32 [512, 8, 128], P('neur'), may hold values from 0.2 to 5
- loadings: float32 [8, 8192], P(None, 'tm'), may hold values from 0.2 to 5
Outputs:
- new_motifs: float32 [512, 8, 128], P('neur')
- new_loadings: float32 [8, 8192], P(None, 'tm')
All inputs are finite; a program needn't handle non-finite values.
Results may differ from a plain program's by a relative error of at most 0.000071.
Values sent between devices are 32-bit elements; how exact they have to be, the bound alone decides.
No kernel may reach another device: no remote copies, remote signals or barrier semaphores. Data moves between devices by JAX's collectives and lax.ppermute only.
A program may use at most 64 MiB of HBM per device.

v0:
```python
import jax
import jax.numpy as jnp
from jax import lax
from jax.sharding import PartitionSpec as P


def shifted_2(value, axis, steps):
    count = lax.axis_size(axis)
    initial, last = (max(0, -steps), min(count, count - steps))
    return lax.ppermute(value, axis, [(source, source + steps) for source in range(initial, last)])


def skew_left(field, out_width):
    batch_size, lag_count, span_len = field.shape
    flat_rows = field.reshape(batch_size, lag_count * span_len)
    flat_rows = jnp.pad(flat_rows, ((0, 0), (0, lag_count)))
    return flat_rows.reshape(batch_size, lag_count, span_len + 1)[:, :, :out_width]


def toeplitz(extended, lag_count, out_width):
    stacked = jnp.broadcast_to(
        extended[:, None, :], (extended.shape[0], lag_count, extended.shape[1])
    )
    return skew_left(stacked, out_width)[:, ::-1, :]


def body(counts, motifs, loadings):
    highest = lax.Precision.HIGHEST
    rows_here, motif_count, lag_count = motifs.shape
    frames_here = loadings.shape[1]
    tail_cols = shifted_2(loadings[:, frames_here - lag_count :], "tm", 1)
    extended = jnp.concatenate([tail_cols[:, 1:], loadings], axis=1)
    shifted = toeplitz(extended, lag_count, frames_here).reshape(
        motif_count * lag_count, frames_here
    )
    motif_mat = motifs.reshape(rows_here, motif_count * lag_count)
    estimate = jnp.dot(motif_mat, shifted, precision=highest)
    ratio_field = counts / estimate
    denom_local = jnp.sum(shifted, axis=1).reshape(motif_count, lag_count)
    contract_rows = (((0,), (0,)), ((), ()))
    ahead_cols = shifted_2(ratio_field[:, :lag_count], "tm", -1)
    ratio_ext = jnp.concatenate([ratio_field, ahead_cols[:, : lag_count - 1]], axis=1)
    lagged = lax.dot_general(motif_mat, ratio_ext, contract_rows, precision=highest)
    numer_local = jnp.sum(
        skew_left(lagged.reshape(motif_count, lag_count, frames_here + lag_count - 1), frames_here),
        axis=1,
    )
    numer_h, motif_tot = lax.psum((numer_local, jnp.sum(motifs, axis=0)), "neur")
    total_frames = frames_here * lax.axis_size("tm")
    frame_global = lax.axis_index("tm") * frames_here + jnp.arange(frames_here, dtype=jnp.int32)
    lag_index = jnp.arange(lag_count, dtype=jnp.int32)
    valid = (lag_index[:, None] + frame_global[None, :] < total_frames).astype(jnp.float32)
    denom_h = jnp.dot(motif_tot, valid, precision=highest)
    new_loadings = loadings * numer_h / denom_h
    contract_frames = (((1,), (1,)), ((), ()))
    share_rows = rows_here // lax.axis_size("tm")
    numer_share = lax.psum_scatter(
        lax.dot_general(ratio_field, shifted, contract_frames, precision=highest),
        "tm",
        scatter_dimension=0,
        tiled=True,
    )
    denom_w = lax.psum(denom_local, "tm")
    motif_share = lax.dynamic_slice_in_dim(motifs, lax.axis_index("tm") * share_rows, share_rows, 0)
    updated_share = motif_share * numer_share.reshape(share_rows, motif_count, lag_count) / denom_w
    new_motifs = lax.all_gather(updated_share, "tm", axis=0, tiled=True)
    return (new_motifs, new_loadings)


def solution(mesh):
    in_specs = (P("neur", "tm"), P("neur", None, None), P(None, "tm"))
    out_specs = (P("neur", None, None), P(None, "tm"))
    return jax.shard_map(body, mesh=mesh, in_specs=in_specs, out_specs=out_specs, check_vma=False)
```

profile of v0, /device:TPU:0, one launch (start us, length us, event | category | flops | bytes accessed | tf_op | source)
XLA Modules:
  0.0 153.8 jit_solution(10008478696121770639)
XLA Ops:
  7.2 0.7 slice.18
  7.9 2.3 %collective-permute-start = (f32[8,128]{1,0:T(8,128)S(1)}, f32[8,128]{1,0:T(8,128)S(1)}, u32[]{:S(2)}, u32[]{:S(2)}) collective-permute-start(f32[8,128]{1,0:T(8,128)S(1)} %slice.18), channel_id=1, source_target_pairs={{0,1},{1,2},{2,3},{3,4},{4,5},{5,6},{6,7},{7,8},{8,9},{9,10},{10,1... | collective-permute-start | bytes 12296 | tf_op jit(solution)/shard_map/ppermute | solution.py:10
  10.3 2.0 %copy.13 = f32[256,512]{0,1:T(8,128)} copy(f32[256,512]{1,0:T(8,128)} %param.3) | data formatting | bytes 1048576 | tf_op args[0]
  12.3 0.1 slice.19
  12.4 0.8 pad_maximum_fusion
  13.2 0.2 broadcast_in_dim.2
  13.3 2.9 %reshape.31 = f32[8,81792]{1,0:T(8,128)} reshape(f32[8,128,639]{2,1,0:T(8,128)S(1)} %broadcast_in_dim.2) | data formatting | bytes 5234688 | tf_op jit(solution)/shard_map/reshape | solution.py:15
  16.2 1.9 %pad.7 = f32[8,81920]{1,0:T(8,128)S(1)} pad(f32[8,81792]{1,0:T(8,128)} %reshape.31, f32[]{:T(128)} %constant.5.clone.1), padding=0_0x0_128 | pad | bytes 5238788 | tf_op jit(solution)/shard_map/jit(_pad)/pad | solution.py:16
  18.2 0.5 copy.26
  18.7 1.6 %slice.24 = f32[8,128,512]{2,1,0:T(8,128)} slice(f32[8,128,640]{2,1,0:T(8,128)S(1)} %bitcast.32), slice={[0:8], [0:128], [0:512]} | slice | bytes 4194304 | tf_op jit(solution)/shard_map/slice | solution.py:17
  20.3 13.7 %rev.3 = f32[8,128,512]{2,1,0:T(8,128)S(1)} reverse(f32[8,128,512]{2,1,0:T(8,128)} %slice.24), dimensions={1} | reverse | bytes 4194304 | tf_op jit(solution)/shard_map/rev | solution.py:24
  34.1 4.5 %fusion = f32[256,512]{0,1:T(8,128)S(1)} fusion(f32[256,512]{0,1:T(8,128)} %copy.13, f32[8,128,512]{2,1,0:T(8,128)S(1)} %rev.3, f32[256,8,128]{2,1,0:T(8,128)S(1)} %copy-done), kind=kOutput, calls=%fused_computation.4 | convolution fusion | flops 1610743808 | bytes 4194304 | tf_op jit(solution)/shard_map/dot_general | solution.py:37
  38.6 0.8 copy-done.1
  39.3 4.6 %fusion.12 = f32[256,1024]{1,0:T(8,128)} fusion(f32[256,512]{0,1:T(8,128)S(1)} %fusion, f32[1024,512]{1,0:T(8,128)S(1)} %bitcast.28), kind=kOutput, calls=%fused_computation.21 | convolution fusion | flops 1610612736 | bytes 3670016 | tf_op jit(solution)/shard_map/dot_general | solution.py:58
  44.0 0.2 reduce_sum.27
  44.2 34.0 %psum.21 = f32[8,128]{1,0:T(8,128)S(1)} all-reduce(f32[8,128]{1,0:T(8,128)S(1)} %reduce_sum.27), channel_id=1, replica_groups=mesh['neur'=2,'tm'=16] {'tm'}, use_global_device_ids=true, to_apply=%region_2.3 | all-reduce | flops 1024 | bytes 8192 | tf_op jit(solution)/shard_map/psum | solution.py:63
  78.2 26.5 %reduce-scatter.2.cloned.1.call-done = f32[16,1024]{1,0:T(8,128)} async-done(((f32[256,1024]{1,0:T(8,128)}), f32[16,1024]{1,0:T(8,128)}) %reduce-scatter.2.cloned.1.call-update) | async-done | bytes 65552 | tf_op jit(solution)/shard_map/reduce_scatter | solution.py:57
  104.7 0.9 copy.17
  105.6 0.6 fusion.9
  106.3 0.9 slice.25
  107.2 1.5 collective-permute-start.1
  108.7 0.3 reduce_sum.29
  108.9 1.5 collective-permute-done.1
  110.4 3.7 %convolution_bitcast_fusion = f32[1024,639]{0,1:T(8,128)S(1)} fusion(f32[32,8,8,128]{3,2,1,0:T(8,128)} %bitcast.30, f32[256,127]{0,1:T(8,128)S(1)} %bitcast.33, f32[256,512]{0,1:T(8,128)} %copy-done.1), kind=kOutput, calls=%fused_computation.2 | convolution fusion | flops 2010283776 | bytes 4320256 | tf_op jit(solution)/shard_map/dot_general | solution.py:43
  114.2 2.1 %copy.14 = f32[1024,639]{1,0:T(8,128)} copy(f32[1024,639]{0,1:T(8,128)S(1)} %convolution_bitcast_fusion) | data formatting | bytes 5234688 | tf_op jit(solution)/shard_map/dot_general | solution.py:43
  116.3 3.1 %reshape_reshape.3 = f32[8,81792]{1,0:T(8,128)S(1)} reshape(f32[1024,639]{1,0:T(8,128)} %copy.14) | data formatting | bytes 5234688 | tf_op jit(solution)/shard_map/reshape;reshape | solution.py:15
  119.4 0.2 pad.8
  119.6 0.2 slice_reduce_fusion
  119.8 8.2 %all-reduce.2 = (f32[8,128]{1,0:T(8,128)S(1)}, f32[8,512]{1,0:T(8,128)S(1)}) all-reduce(f32[8,128]{1,0:T(8,128)S(1)} %reduce_sum.29, f32[8,512]{1,0:T(8,128)S(1)} %slice_reduce_fusion), channel_id=1, replica_groups=mesh['neur'=2,'tm'=16] {'neur'}, use_global_device_ids=true, to_apply=%region_6.7 | all-reduce | flops 5120 | bytes 40960 | tf_op jit(solution)/shard_map/psum | solution.py:48
  128.0 0.8 convolution_divide_fusion
  128.9 15.8 %all-gather.2.cloned.1.call-done = f32[256,8,128]{2,1,0:T(8,128)} async-done(((f32[16,8,128]{2,1,0:T(8,128)}), f32[256,8,128]{2,1,0:T(8,128)}) %all-gather.2.cloned.1.call-update) | async-done | bytes 1048592 | tf_op jit(solution)/shard_map/all_gather | solution.py:66
  144.7 2.3 %copy.28 = f32[256,8,128]{2,1,0:T(8,128)} copy(f32[256,8,128]{2,1,0:T(8,128)} %all-gather.2.cloned.1.call-done) | data formatting | bytes 2097152
  (11 shorter events, 0.1 us)
Async XLA Ops:
  7.2 97.6 %reduce-scatter.2.cloned.1.call-start = ((), (), s32[]{:S(2)}) async-start(), calls=%async_computation.1 | async-start | bytes 1114112 | tf_op jit(solution)/shard_map/reduce_scatter | solution.py:57
  7.9 4.4 %collective-permute-start = (f32[8,128]{1,0:T(8,128)S(1)}, f32[8,128]{1,0:T(8,128)S(1)}, u32[]{:S(2)}, u32[]{:S(2)}) collective-permute-start(f32[8,128]{1,0:T(8,128)S(1)} %slice.18), channel_id=1, source_target_pairs={{0,1},{1,2},{2,3},{3,4},{4,5},{5,6},{6,7},{7,8},{8,9},{9,10},{10,1... | collective-permute-start | bytes 12296 | tf_op jit(solution)/shard_map/ppermute | solution.py:10
  20.3 13.8 %copy-start = (f32[256,8,128]{2,1,0:T(8,128)S(1)}, f32[256,8,128]{2,1,0:T(8,128)}, u32[]{:S(2)}) copy-start(f32[256,8,128]{2,1,0:T(8,128)} %param.4) | copy-start | bytes 3145732
  38.6 0.8 copy-start.1
  44.0 100.7 %all-gather.2.cloned.1.call-start = ((), (), s32[]{:S(2)}) async-start(), calls=%async_computation.2 | async-start | bytes 1114112 | tf_op jit(solution)/shard_map/all_gather | solution.py:66
  107.2 3.2 %collective-permute-start.1 = (f32[256,128]{0,1:T(8,128)S(1)}, f32[256,128]{0,1:T(8,128)S(1)}, u32[]{:S(2)}, u32[]{:S(2)}) collective-permute-start(f32[256,128]{0,1:T(8,128)S(1)} %slice.25), channel_id=1, source_target_pairs={{1,0},{2,1},{3,2},{4,3},{5,4},{6,5},{7,6},{8,7},{9,8},{10,9},{11,1... | collective-permute-start | bytes 393224 | tf_op jit(solution)/shard_map/ppermute | solution.py:10
  119.4 8.6 %copy-start.2 = (f32[8,512]{1,0:T(8,128)S(1)}, f32[8,512]{1,0:T(8,128)}, u32[]{:S(2)}) copy-start(f32[8,512]{1,0:T(8,128)} %param.5) | copy-start | bytes 49156
Sparse Core Ops, SparseCore 0:
  44.1 60.5 reduce-scatter.1
  107.7 36.9 all-gather.1
where the time goes:
time: 155 us; the launch traced here: 154 us
  waiting for transfers between devices  43.9 us (28%)
  blocking collectives  42.2 us (27%)
  local copies, waits for them, and re-layouts  33.9 us (22%)
  between operations  14.2 us (9%)
  matrix products  13.6 us (9%)
  starting transfers between devices  3.9 us (3%)
  other arithmetic  2.11 us (1%)
    psum x1, blocking collectives, body(): denom_w = lax.psum(denom_local, 'tm')  34 us
    reduce_scatter x1, waiting for transfers between devices, body(): lax.psum_scatter(lax.dot_general(ratio_field, shifted, contract_frames, p...  26.5 us
    all_gather x1, waiting for transfers between devices, body(): new_motifs = lax.all_gather(updated_share, 'tm', axis=0, tiled=True)  15.8 us
    rev x1, local copies, waits for them, and re-layouts, toeplitz(): return skew_left(stacked, out_width)[:, ::-1, :]  13.7 us
    psum x1, blocking collectives, body(): lax.psum((numer_local, jnp.sum(motifs, axis=0)), 'neur')  8.25 us
    unnamed x10, local copies, waits for them, and re-layouts  6.45 us
    dot_general x1, matrix products, body(): lax.dot_general(ratio_field, shifted, contract_frames, precision=highest)  4.59 us
    dot_general x1, matrix products, body(): estimate = jnp.dot(motif_mat, shifted, precision=highest)  4.48 us
  transfers between devices with their start and end apart: 4, of which 3 were waited for; matrix products, arithmetic and copies ran while one was open for 9% of the time, Pallas kernels for 0%

commit v1 on v0

v1 whole, which is shorter than its diff:
```python
import jax
import jax.numpy as jnp
from jax import lax
from jax.experimental import pallas as pl
from jax.experimental.pallas import tpu as pltpu
from jax.sharding import PartitionSpec as P

F32, BF16 = jnp.float32, jnp.bfloat16
NN = (((1,), (0,)), ((), ()))
NT = (((1,), (1,)), ((), ()))
TN = (((0,), (0,)), ((), ()))
VMEM_LIMIT = 24 * 1024 * 1024


def split(x):
    high = x.astype(BF16)
    return high, (x - high.astype(F32)).astype(BF16)


def dot3(ah, al, bh, bl, dims):
    def dot(a, b):
        return lax.dot_general(a, b, dims, preferred_element_type=F32)

    return dot(ah, bh) + (dot(ah, bl) + dot(al, bh))


def toeplitz(row, lags):
    return pltpu.roll(jnp.broadcast_to(row, (lags, row.shape[1])), 0, 1, stride=1, stride_axis=0)


def vmem_call(kernel, out_shapes, scalars=0, name=None, flops=0):
    def call(*args):
        specs = [pl.BlockSpec(memory_space=pltpu.SMEM)] * scalars
        specs += [pl.BlockSpec(memory_space=pltpu.VMEM)] * (len(args) - scalars)
        moved = sum(a.size * a.dtype.itemsize for a in args)
        return pl.pallas_call(
            kernel,
            out_shape=out_shapes,
            in_specs=specs,
            out_specs=[pl.BlockSpec(memory_space=pltpu.VMEM)] * len(out_shapes),
            compiler_params=pltpu.CompilerParams(vmem_limit_bytes=VMEM_LIMIT),
            cost_estimate=pl.CostEstimate(flops=flops, bytes_accessed=moved, transcendentals=0),
            name=name,
        )(*args)

    return call


def body_kernel(counts_ref, motifs_ref, loads_ref, mh_ref, ml_ref, th_ref, tl_ref, rh_ref, rl_ref):
    rows = counts_ref.shape[0]
    motif_count = loads_ref.shape[0]
    lags = motifs_ref.shape[1]
    for k in range(motif_count):
        at = pl.ds(k * lags, lags)
        mh_ref[:, at], ml_ref[:, at] = split(motifs_ref[pl.ds(k, rows, stride=motif_count), :])
        th_ref[at, :], tl_ref[at, :] = split(toeplitz(loads_ref[pl.ds(k, 1), :], lags)[:, lags:])
    estimate = dot3(mh_ref[...], ml_ref[...], th_ref[...], tl_ref[...], NN)
    rh_ref[...], rl_ref[...] = split(counts_ref[:, lags:] / estimate)


def head_kernel(core_ref, tail_ref, counts_ref, loads_ref, mh_ref, ml_ref, th_ref, tl_ref, rh_ref, rl_ref,
                send_ref, keep_ref, fh_ref, fl_ref, hh, hl):
    rows = counts_ref.shape[0]
    motif_count = loads_ref.shape[0]
    lags = mh_ref.shape[1] // motif_count
    half = rows // 2
    frames = loads_ref.shape[1]
    for k in range(motif_count):
        at = pl.ds(k * lags, lags)
        row = jnp.concatenate([tail_ref[pl.ds(k, 1), frames - lags:], loads_ref[pl.ds(k, 1), :lags]], axis=1)
        hh[at, :], hl[at, :] = split(toeplitz(row, lags)[:, lags:])
    estimate = dot3(mh_ref[...], ml_ref[...], hh[...], hl[...], NN)
    head_h, head_l = split(counts_ref[:, :lags] / estimate)
    fh_ref[:, :lags], fl_ref[:, :lags] = head_h, head_l
    fh_ref[:, lags:], fl_ref[:, lags:] = rh_ref[...], rl_ref[...]
    core = core_ref[0]
    away, home = pl.ds(pl.multiple_of((1 - core) * half, half), half), pl.ds(pl.multiple_of(core * half, half), half)
    ones = jnp.ones((16, frames), BF16)
    xh = jnp.concatenate([fh_ref[away, :], fh_ref[home, :], ones], axis=0)
    xl = jnp.concatenate([fl_ref[away, :], fl_ref[home, :], jnp.zeros_like(ones)], axis=0)
    for k in range(motif_count):
        at = pl.ds(k * lags, lags)
        kh = jnp.concatenate([hh[at, :], th_ref[at, :]], axis=1)
        kl = jnp.concatenate([hl[at, :], tl_ref[at, :]], axis=1)
        numer = dot3(xh, xl, kh, kl, NT)
        send_ref[pl.ds(k, half, stride=motif_count), :] = numer[:half]
        keep_ref[pl.ds(k, half, stride=motif_count), :] = numer[half:rows]
        send_ref[pl.ds(half * motif_count + k, 1), :] = numer[rows:rows + 1]
        keep_ref[pl.ds(half * motif_count + k, 1), :] = numer[rows:rows + 1]


def fold_kernel(bit_ref, mine_ref, got_ref, send_ref, keep_ref):
    half = (mine_ref.shape[0] - 1) // 2
    bit = bit_ref[0]
    for out, place in ((send_ref, 1 - bit), (keep_ref, bit)):
        at = pl.ds(place * half, half)
        out[:half] = mine_ref[at] + got_ref[at]
        out[half:] = mine_ref[2 * half:] + got_ref[2 * half:]


def update_kernel(at_ref, mine_ref, got_ref, motifs_ref, out_ref):
    rows = out_ref.shape[0]
    denom = mine_ref[rows] + got_ref[rows]
    numer = mine_ref[:rows] + got_ref[:rows]
    out_ref[...] = motifs_ref[pl.ds(at_ref[0], rows)] * numer / denom[None]


def join_kernel(bit_ref, mine_ref, got_ref, out_ref):
    half = mine_ref.shape[0]
    bit = bit_ref[0]
    out_ref[pl.ds(bit * half, half)] = mine_ref[...]
    out_ref[pl.ds((1 - bit) * half, half)] = got_ref[...]


def lagged_kernel(mh_ref, ml_ref, fh_ref, fl_ref, motifs_ref, numer_ref, ahead_ref, total_ref):
    motif_count, frames = numer_ref.shape
    lags = mh_ref.shape[1] // motif_count
    width = frames + lags
    down = lax.broadcasted_iota(jnp.int32, (lags, lags), 0)
    across = lax.broadcasted_iota(jnp.int32, (lags, lags), 1)
    flip = (down + across == lags - 1).astype(BF16)
    for k in range(motif_count):
        at = pl.ds(k * lags, lags)
        ph, pw = (
            lax.dot_general(ref[:, at], flip, NN, preferred_element_type=F32).astype(BF16) for ref in (mh_ref, ml_ref)
        )
        lagged = dot3(ph, pw, fh_ref[...], fl_ref[...], TN)
        wide = jnp.concatenate([jnp.zeros((lags, lags), F32), lagged], axis=1)
        skewed = pltpu.roll(wide, width - (lags - 1), 1, stride=1, stride_axis=0)
        numer = jnp.sum(skewed, axis=0, keepdims=True)
        ahead_ref[pl.ds(k, 1), :] = numer[:, :lags]
        numer_ref[pl.ds(k, 1), :] = numer[:, lags:]
    total_ref[...] = jnp.sum(motifs_ref[...], axis=0)


def halo_kernel(numer_ref, ahead_ref, total_ref, out_ref):
    frames, lags = numer_ref.shape[1], ahead_ref.shape[1]
    out_ref[:, :frames - lags] = numer_ref[:, :frames - lags]
    out_ref[:, frames - lags:frames] = numer_ref[:, frames - lags:] + ahead_ref[...]
    out_ref[:, frames:] = total_ref[...]


def pair_kernel(mine_ref, got_ref, out_ref):
    out_ref[...] = mine_ref[...] + got_ref[...]


def loads_kernel(left_ref, mine_ref, got_ref, loads_ref, out_ref):
    frames = loads_ref.shape[1]
    lags = mine_ref.shape[1] - frames
    both = mine_ref[...] + got_ref[...]
    lag = lax.broadcasted_iota(jnp.int32, (lags, frames), 0)
    frame = lax.broadcasted_iota(jnp.int32, (lags, frames), 1)
    valid = (lag + frame < left_ref[0]).astype(F32)
    denom = lax.dot_general(both[:, frames:], valid, NN, precision=lax.Precision.HIGHEST, preferred_element_type=F32)
    out_ref[...] = loads_ref[...] * both[:, :frames] / denom


def body(counts, motifs, loadings):
    rows, motif_count, lags = motifs.shape
    frames = loadings.shape[1]
    ranks, me = lax.axis_size("tm"), lax.axis_index("tm")
    steps = ranks.bit_length() - 1
    assert ranks == 1 << steps and steps >= 3 and rows % ranks == 0

    def shape(*dims, dtype=F32):
        return jax.ShapeDtypeStruct(dims, dtype)

    orders = [[0, 1, 2, *range(3, steps)], [0, 2, 1, *range(3, steps)]]
    core = me & 1

    def bit(step):
        return jnp.where(core == 0, (me >> orders[0][step]) & 1, (me >> orders[1][step]) & 1).astype(jnp.int32)

    def swap(x, step):
        return lax.ppermute(x, "tm", [(i, i ^ (1 << orders[i & 1][step])) for i in range(ranks)])

    tail = lax.ppermute(loadings, "tm", [(i, i + 1) for i in range(ranks - 1)])
    flat = motifs.reshape(rows * motif_count, lags)
    depth = motif_count * lags
    macs = rows * depth * frames * 6
    mh, ml, th, tl, rh, rl = vmem_call(
        body_kernel,
        [shape(rows, depth, dtype=BF16)] * 2 + [shape(depth, frames - lags, dtype=BF16)] * 2
        + [shape(rows, frames - lags, dtype=BF16)] * 2,
        name="body", flops=macs,
    )(counts, flat, loadings)
    half = rows // 2
    send, keep, fh, fl = pl.pallas_call(
        head_kernel,
        out_shape=[shape((half + 1) * motif_count, lags)] * 2 + [shape(rows, frames, dtype=BF16)] * 2,
        in_specs=[pl.BlockSpec(memory_space=pltpu.SMEM)] + [pl.BlockSpec(memory_space=pltpu.VMEM)] * 9,
        out_specs=[pl.BlockSpec(memory_space=pltpu.VMEM)] * 4,
        scratch_shapes=[pltpu.VMEM((depth, lags), BF16)] * 2,
        compiler_params=pltpu.CompilerParams(vmem_limit_bytes=VMEM_LIMIT),
        name="head",
    )(core.reshape(1), tail, counts, loadings, mh, ml, th, tl, rh, rl)
    send = send.reshape(half + 1, motif_count, lags)
    keep = keep.reshape(half + 1, motif_count, lags)

    numer, ahead, total = vmem_call(
        lagged_kernel, [shape(motif_count, frames), shape(motif_count, lags), shape(motif_count, lags)],
        name="lagged", flops=macs,
    )(mh, ml, fh, fl, motifs)
    ahead = lax.ppermute(ahead, "tm", [(i, i - 1) for i in range(1, ranks)])
    (loads_part,) = vmem_call(halo_kernel, [shape(motif_count, frames + lags)], name="halo")(numer, ahead, total)

    own = bit(0) * half
    got = swap(send, 0)
    for step in range(1, steps - 1):
        half //= 2
        here = bit(step)
        send, keep = vmem_call(fold_kernel, [shape(half + 1, motif_count, lags)] * 2, 1, name="fold")(
            here.reshape(1), keep, got
        )
        own = own + here * half
        got = swap(send, step)
    (keep,) = vmem_call(pair_kernel, [shape(half + 1, motif_count, lags)], name="pair")(keep, got)
    got = swap(keep, steps - 1)
    (mine,) = vmem_call(update_kernel, [shape(half, motif_count, lags)], 1, name="update")(
        own.reshape(1), keep, got, motifs
    )
    for step in range(steps - 2, -1, -1):
        got = swap(mine, step)
        half *= 2
        (mine,) = vmem_call(join_kernel, [shape(half, motif_count, lags)], 1, name="join")(
            bit(step).reshape(1), mine, got
        )

    groups = lax.axis_size("neur")
    flips = groups.bit_length() - 1
    assert groups == 1 << flips
    for flip in range(flips):
        got = lax.ppermute(loads_part, "neur", [(i, i ^ (1 << flip)) for i in range(groups)])
        if flip < flips - 1:
            (loads_part,) = vmem_call(pair_kernel, [loads_part], name="pair")(loads_part, got)
    if flips == 0:
        got = jnp.zeros_like(loads_part)
    left = (ranks - me) * frames
    (new_loadings,) = vmem_call(loads_kernel, [shape(motif_count, frames)], 1, name="loads")(
        left.astype(jnp.int32).reshape(1), loads_part, got, loadings
    )
    return mine, new_loadings


def solution(mesh):
    in_specs = (P("neur", "tm"), P("neur", None, None), P(None, "tm"))
    out_specs = (P("neur", None, None), P(None, "tm"))
    return jax.shard_map(body, mesh=mesh, in_specs=in_specs, out_specs=out_specs, check_vma=False)
```

time: 155 us -> 65.6 us (0.42)
  blocking collectives: 42.2 us -> 0 us
  local copies, waits for them, and re-layouts: 33.9 us -> 7 us
  waiting for transfers between devices: 43.9 us -> 29.4 us
  matrix products: 13.6 us -> 0 us
  between operations: 14.2 us -> 0.74 us
  starting transfers between devices: 3.9 us -> 16.1 us
  Pallas kernels: 0 us -> 11.1 us
  other arithmetic: 2.11 us -> 0 us
    psum x2 -> x0, blocking collectives: 42.2 us -> none  [the longest x1 34 us: body(): denom_w = lax.psum(denom_local, 'tm')]
    ppermute x2 -> x10, waiting for transfers between devices: 1.48 us -> 29.4 us  [the longest x7 25.4 us: swap(): lax.ppermute(x, 'tm', [(i, i ^ 1 << orders[i & 1][step]) for i in range(r...]
    reduce_scatter x1 -> x0, waiting for transfers between devices: 26.5 us -> none  [body(): lax.psum_scatter(lax.dot_general(ratio_field, shifted, contract_frames, p...]
    all_gather x1 -> x0, waiting for transfers between devices: 15.8 us -> none  [body(): new_motifs = lax.all_gather(updated_share, 'tm', axis=0, tiled=True)]
    rev x1 -> x0, local copies, waits for them, and re-layouts: 13.7 us -> none  [toeplitz(): return skew_left(stacked, out_width)[:, ::-1, :]]
    dot_general x4 -> x0, matrix products: 13.6 us -> none  [the longest x1 4.59 us: body(): lax.dot_general(ratio_field, shifted, contract_frames, precision=highest)]
    ppermute x2 -> x10, starting transfers between devices: 3.82 us -> 16.1 us  [the longest x7 10.3 us: swap(): lax.ppermute(x, 'tm', [(i, i ^ 1 << orders[i & 1][step]) for i in range(r...]
    pallas_call x0 -> x12, Pallas kernels: none -> 11.1 us  [the longest x11 6.79 us: call(): pl.pallas_call(kernel, out_shape=out_shapes, in_specs=specs, out_specs=[p...]
  transfers between devices with their start and end apart: 4 -> 10, of which waited for: 3 -> 8; matrix products, arithmetic and copies ran while one was open for 9% -> 0% of each run, Pallas kernels for 0% -> 9%
where the time goes in v1:
time: 65.6 us; the launch traced here: 64.3 us
  waiting for transfers between devices  29.4 us (45%)
  starting transfers between devices  16.1 us (25%)
  Pallas kernels  11.1 us (17%)
  local copies, waits for them, and re-layouts  7 us (11%)
  between operations  0.74 us (1%)
    ppermute x7, waiting for transfers between devices, swap(): lax.ppermute(x, 'tm', [(i, i ^ 1 << orders[i & 1][step]) for i in range(r...  25.4 us
    ppermute x7, starting transfers between devices, swap(): lax.ppermute(x, 'tm', [(i, i ^ 1 << orders[i & 1][step]) for i in range(r...  10.3 us
    unnamed x28, local copies, waits for them, and re-layouts  7 us
    pallas_call x11, Pallas kernels, call(): pl.pallas_call(kernel, out_shape=out_shapes, in_specs=specs, out_specs=[p...  6.79 us
    pallas_call x1, Pallas kernels, body(): pl.pallas_call(head_kernel, out_shape=[shape((half + 1) * motif_count, la...  4.31 us
    ppermute x1, starting transfers between devices, body(): tail = lax.ppermute(loadings, 'tm', [(i, i + 1) for i in range(ranks - 1)])  2.97 us
    ppermute x1, waiting for transfers between devices, body(): lax.ppermute(loads_part, 'neur', [(i, i ^ 1 << flip) for i in range(group...  2.28 us
    ppermute x1, waiting for transfers between devices, body(): ahead = lax.ppermute(ahead, 'tm', [(i, i - 1) for i in range(1, ranks)])  1.76 us
  transfers between devices with their start and end apart: 10, of which 8 were waited for; matrix products, arithmetic and copies ran while one was open for 0% of the time, Pallas kernels for 9%

profile of v1, /device:TPU:0, one launch (start us, length us, event | category | flops | bytes accessed | tf_op | source)
XLA Modules:
  0.0 64.3 jit_solution(11427511834746204884)
XLA Ops:
  0.6 3.0 %collective-permute-start = (f32[8,512]{1,0:T(8,128)}, f32[8,512]{1,0:T(8,128)}, u32[]{:S(2)}, u32[]{:S(2)}) collective-permute-start(f32[8,512]{1,0:T(8,128)} %loads_ref.5), channel_id=1, source_target_pairs={{0,1},{1,2},{2,3},{3,4},{4,5},{5,6},{6,7},{7,8},{8,9},{9,10},{10,1... | collective-permute-start | bytes 49160 | tf_op jit(solution)/shard_map/ppermute | solution.py:177
  3.6 1.2 %copy-done = f32[256,8,128]{2,1,0:T(8,128)S(1)} copy-done((f32[256,8,128]{2,1,0:T(8,128)S(1)}, f32[256,8,128]{2,1,0:T(8,128)}, u32[]{:S(2)}) %copy-start) | copy-done | bytes 1048600
  4.8 1.0 %copy-done.2 = f32[256,512]{1,0:T(8,128)S(1)} copy-done((f32[256,512]{1,0:T(8,128)S(1)}, f32[256,512]{1,0:T(8,128)}, u32[]{:S(2)}) %copy-start.2) | copy-done | bytes 524312
  5.9 0.7 %copy-done.7 = f32[8,512]{1,0:T(8,128)S(1)} copy-done((f32[8,512]{1,0:T(8,128)S(1)}, f32[8,512]{1,0:T(8,128)}, u32[]{:S(2)}) %copy-start.7) | copy-done | bytes 16408
  6.6 1.6 %body.1 = (bf16[256,1024]{1,0:T(8,128)(2,1)S(1)}, bf16[256,1024]{1,0:T(8,128)(2,1)S(1)}, bf16[1024,384]{1,0:T(8,128)(2,1)S(1)}, bf16[1024,384]{1,0:T(8,128)(2,1)...) custom-call(f32[256,512]{1,0:T(8,128)S(1)} %copy-done.2, f32[2048,128]{1,0:T(8,128)S(1)} %bitcast.9, ...), custom_call_target="tpu_custom_call" | custom-call | flops 805306368 | bytes 1589248 | tf_op jit(solution)/shard_map/body/pallas_call | solution.py:36
  8.2 0.8 %copy-done.4 = bf16[256,1024]{1,0:T(8,128)(2,1)} copy-done((bf16[256,1024]{1,0:T(8,128)(2,1)}, bf16[256,1024]{1,0:T(8,128)(2,1)S(1)}, u32[]{:S(2)}) %copy-start.4) | copy-done | bytes 524312
  9.0 1.0 %copy-done.5 = bf16[256,1024]{1,0:T(8,128)(2,1)S(1)} copy-done((bf16[256,1024]{1,0:T(8,128)(2,1)S(1)}, bf16[256,1024]{1,0:T(8,128)(2,1)}, u32[]{:S(2)}) %copy-start.5) | copy-done | bytes 524312
  10.0 0.7 %copy-done.8 = f32[8,512]{1,0:T(8,128)S(1)} copy-done((f32[8,512]{1,0:T(8,128)S(1)}, f32[8,512]{1,0:T(8,128)}, u32[]{:S(2)}) %copy-start.8) | copy-done | bytes 16408
  10.7 4.3 %head.1 = (f32[1032,128]{1,0:T(8,128)}, f32[1032,128]{1,0:T(8,128)S(1)}, bf16[256,512]{1,0:T(8,128)(2,1)S(1)}, bf16[256,512]{1,0:T(8,128)(2,1)S(1)}) custom-call(s32[1]{0:T(128)} %bitcast.4.core_ref, f32[8,512]{1,0:T(8,128)} %collective-permute-done.tail_ref, f32[256,512]{1,0:T(8,128)S(1)} %copy-done.3, f32[8,512]{1,0:T(8,128)S(1)} %copy-done.8, ...), custom_call_target="tpu_custom_call" | custom-call | tf_op jit(solution)/shard_map/head/pallas_call | solution.py:188
  15.0 0.7 %copy-done.10 = bf16[256,512]{1,0:T(8,128)(2,1)} copy-done((bf16[256,512]{1,0:T(8,128)(2,1)}, bf16[256,512]{1,0:T(8,128)(2,1)S(1)}, u32[]{:S(2)}) %copy-start.10) | copy-done | bytes 262168
  15.8 0.7 %copy-done.12 = bf16[256,512]{1,0:T(8,128)(2,1)} copy-done((bf16[256,512]{1,0:T(8,128)(2,1)}, bf16[256,512]{1,0:T(8,128)(2,1)S(1)}, u32[]{:S(2)}) %copy-start.12) | copy-done | bytes 262168
  16.5 2.0 %collective-permute-start.1 = (f32[129,8,128]{2,1,0:T(8,128)}, f32[129,8,128]{2,1,0:T(8,128)S(1)}, u32[]{:S(2)}, u32[]{:S(2)}) collective-permute-start(f32[129,8,128]{2,1,0:T(8,128)} %bitcast.7), channel_id=1, source_target_pairs={{0,1},{1,0},{2,3},{3,2},{4,5},{5,4},{6,7},{7,6},{8,9},{9,8},{10,11... | collective-permute-start | bytes 1585160 | tf_op jit(solution)/shard_map/ppermute | solution.py:175
  18.5 1.8 %collective-permute-done.1.got_ref = f32[129,8,128]{2,1,0:T(8,128)S(1)} collective-permute-done((f32[129,8,128]{2,1,0:T(8,128)}, f32[129,8,128]{2,1,0:T(8,128)S(1)}, u32[]{:S(2)}, u32[]{:S(2)}) %collective-permute-start.1) | collective-permute-done | bytes 528416 | tf_op jit(solution)/shard_map/ppermute | solution.py:175
  20.2 0.1 fold.2
  20.3 1.6 %collective-permute-start.2 = (f32[65,8,128]{2,1,0:T(8,128)S(1)}, f32[65,8,128]{2,1,0:T(8,128)S(1)}, u32[]{:S(2)}, u32[]{:S(2)}) collective-permute-start(f32[65,8,128]{2,1,0:T(8,128)S(1)} %get-tuple-element.28), channel_id=1, source_target_pairs={{0,2},{1,5},{2,0},{3,7},{4,6},{5,1},{6,4},{7,3},{8,10},{9,13},{10,... | collective-permute-start | bytes 798728 | tf_op jit(solution)/shard_map/ppermute | solution.py:175
  21.9 4.9 %collective-permute-done.2.got_ref = f32[65,8,128]{2,1,0:T(8,128)S(1)} collective-permute-done((f32[65,8,128]{2,1,0:T(8,128)S(1)}, f32[65,8,128]{2,1,0:T(8,128)S(1)}, u32[]{:S(2)}, u32[]{:S(2)}) %collective-permute-start.2) | collective-permute-done | bytes 266272 | tf_op jit(solution)/shard_map/ppermute | solution.py:175
  26.8 1.6 %collective-permute-start.3 = (f32[33,8,128]{2,1,0:T(8,128)S(1)}, f32[33,8,128]{2,1,0:T(8,128)S(1)}, u32[]{:S(2)}, u32[]{:S(2)}) collective-permute-start(f32[33,8,128]{2,1,0:T(8,128)S(1)} %get-tuple-element.30), channel_id=1, source_target_pairs={{0,4},{1,3},{2,6},{3,1},{4,0},{5,7},{6,2},{7,5},{8,12},{9,11},{10,... | collective-permute-start | bytes 405512 | tf_op jit(solution)/shard_map/ppermute | solution.py:175
  28.5 3.4 %collective-permute-done.3.got_ref = f32[33,8,128]{2,1,0:T(8,128)S(1)} collective-permute-done((f32[33,8,128]{2,1,0:T(8,128)S(1)}, f32[33,8,128]{2,1,0:T(8,128)S(1)}, u32[]{:S(2)}, u32[]{:S(2)}) %collective-permute-start.3) | collective-permute-done | bytes 135200 | tf_op jit(solution)/shard_map/ppermute | solution.py:175
  31.9 2.7 %collective-permute-start.4 = (f32[33,8,128]{2,1,0:T(8,128)S(1)}, f32[33,8,128]{2,1,0:T(8,128)S(1)}, u32[]{:S(2)}, u32[]{:S(2)}) collective-permute-start(f32[33,8,128]{2,1,0:T(8,128)S(1)} %pair.1.mine_ref), channel_id=1, source_target_pairs={{0,8},{1,9},{2,10},{3,11},{4,12},{5,13},{6,14},{7,15},{8,0},{9,1},... | collective-permute-start | bytes 405512 | tf_op jit(solution)/shard_map/ppermute | solution.py:175
  34.6 5.1 %collective-permute-done.4.got_ref = f32[33,8,128]{2,1,0:T(8,128)S(1)} collective-permute-done((f32[33,8,128]{2,1,0:T(8,128)S(1)}, f32[33,8,128]{2,1,0:T(8,128)S(1)}, u32[]{:S(2)}, u32[]{:S(2)}) %collective-permute-start.4) | collective-permute-done | bytes 135200 | tf_op jit(solution)/shard_map/ppermute | solution.py:175
  39.7 0.7 %collective-permute-start.5 = (f32[32,8,128]{2,1,0:T(8,128)S(1)}, f32[32,8,128]{2,1,0:T(8,128)S(1)}, u32[]{:S(2)}, u32[]{:S(2)}) collective-permute-start(f32[32,8,128]{2,1,0:T(8,128)S(1)} %update.1.mine_ref), channel_id=1, source_target_pairs={{0,4},{1,3},{2,6},{3,1},{4,0},{5,7},{6,2},{7,5},{8,12},{9,11},{10,... | collective-permute-start | bytes 393224 | tf_op jit(solution)/shard_map/ppermute | solution.py:175
  40.4 5.4 %collective-permute-done.5.got_ref = f32[32,8,128]{2,1,0:T(8,128)S(1)} collective-permute-done((f32[32,8,128]{2,1,0:T(8,128)S(1)}, f32[32,8,128]{2,1,0:T(8,128)S(1)}, u32[]{:S(2)}, u32[]{:S(2)}) %collective-permute-start.5) | collective-permute-done | bytes 131104 | tf_op jit(solution)/shard_map/ppermute | solution.py:175
  45.9 1.6 %collective-permute-start.6 = (f32[64,8,128]{2,1,0:T(8,128)S(1)}, f32[64,8,128]{2,1,0:T(8,128)S(1)}, u32[]{:S(2)}, u32[]{:S(2)}) collective-permute-start(f32[64,8,128]{2,1,0:T(8,128)S(1)} %join.3.mine_ref), channel_id=1, source_target_pairs={{0,2},{1,5},{2,0},{3,7},{4,6},{5,1},{6,4},{7,3},{8,10},{9,13},{10,... | collective-permute-start | bytes 786440 | tf_op jit(solution)/shard_map/ppermute | solution.py:175
  47.4 4.8 %collective-permute-done.6.got_ref = f32[64,8,128]{2,1,0:T(8,128)S(1)} collective-permute-done((f32[64,8,128]{2,1,0:T(8,128)S(1)}, f32[64,8,128]{2,1,0:T(8,128)S(1)}, u32[]{:S(2)}, u32[]{:S(2)}) %collective-permute-start.6) | collective-permute-done | bytes 262176 | tf_op jit(solution)/shard_map/ppermute | solution.py:175
  52.3 0.1 collective-permute-start.7
  52.4 3.1 %lagged.1 = (f32[8,512]{1,0:T(8,128)S(1)}, f32[8,128]{1,0:T(8,128)S(1)}, f32[8,128]{1,0:T(8,128)S(1)}) custom-call(bf16[256,1024]{1,0:T(8,128)(2,1)S(1)} %get-tuple-element.19.mh_ref, bf16[256,1024]{1,0:T(8,128)(2,1)S(1)} %copy-done.6, bf16[256,512]{1,0:T(8,128)(2,1)S(1)} %copy-done.11, bf16[256,512]{1,0:T(8,128)(2,1)S(1)} %copy-done.13, ...), custom_call_target="tpu_custom_call" | custom-call | flops 805306368 | bytes 2621440 | tf_op jit(solution)/shard_map/lagged/pallas_call | solution.py:36
  55.5 1.3 %collective-permute-start.8 = (f32[8,128]{1,0:T(8,128)S(1)}, f32[8,128]{1,0:T(8,128)S(1)}, u32[]{:S(2)}, u32[]{:S(2)}) collective-permute-start(f32[8,128]{1,0:T(8,128)S(1)} %get-tuple-element.34), channel_id=1, source_target_pairs={{1,0},{2,1},{3,2},{4,3},{5,4},{6,5},{7,6},{8,7},{9,8},{10,9},{11,1... | collective-permute-start | bytes 12296 | tf_op jit(solution)/shard_map/ppermute | solution.py:204
  56.8 1.8 %collective-permute-done.8.ahead_ref = f32[8,128]{1,0:T(8,128)S(1)} collective-permute-done((f32[8,128]{1,0:T(8,128)S(1)}, f32[8,128]{1,0:T(8,128)S(1)}, u32[]{:S(2)}, u32[]{:S(2)}) %collective-permute-start.8) | collective-permute-done | bytes 4128 | tf_op jit(solution)/shard_map/ppermute | solution.py:204
  58.6 1.5 %collective-permute-start.9 = (f32[8,640]{1,0:T(8,128)S(1)}, f32[8,640]{1,0:T(8,128)S(1)}, u32[]{:S(2)}, u32[]{:S(2)}) collective-permute-start(f32[8,640]{1,0:T(8,128)S(1)} %halo.1.mine_ref), channel_id=1, source_target_pairs={{0,16},{16,0},{1,17},{17,1},{2,18},{18,2},{3,19},{19,3},{4,20},{20... | collective-permute-start | bytes 61448 | tf_op jit(solution)/shard_map/ppermute | solution.py:233
  60.1 2.3 %collective-permute-done.9.got_ref = f32[8,640]{1,0:T(8,128)S(1)} collective-permute-done((f32[8,640]{1,0:T(8,128)S(1)}, f32[8,640]{1,0:T(8,128)S(1)}, u32[]{:S(2)}, u32[]{:S(2)}) %collective-permute-start.9) | collective-permute-done | bytes 20512 | tf_op jit(solution)/shard_map/ppermute | solution.py:233
  62.4 0.9 %loads.1 = f32[8,512]{1,0:T(8,128)} custom-call(s32[1]{0:T(128)} %bitcast.8.left_ref, f32[8,640]{1,0:T(8,128)S(1)} %halo.1.mine_ref, f32[8,640]{1,0:T(8,128)S(1)} %collective-permute-done.9.got_ref, f32[8,512]{1,0:T(8,128)S(1)} %copy-done.9), custom_call_target="tpu_custom_call" | custom-call | bytes 57348 | tf_op jit(solution)/shard_map/loads/pallas_call | solution.py:36
  63.3 1.0 %join.5 = f32[256,8,128]{2,1,0:T(8,128)} custom-call(s32[1]{0:T(128)} %bitcast.bit_ref, f32[128,8,128]{2,1,0:T(8,128)S(1)} %join.4.mine_ref, f32[128,8,128]{2,1,0:T(8,128)S(1)} %collective-permute-done.7.got_ref), custom_call_target="tpu_custom_call" | custom-call | bytes 1048580 | tf_op jit(solution)/shard_map/join/pallas_call | solution.py:36
  (28 shorter events, 0.2 us)
Async XLA Ops:
  0.6 8.3 %collective-permute-start = (f32[8,512]{1,0:T(8,128)}, f32[8,512]{1,0:T(8,128)}, u32[]{:S(2)}, u32[]{:S(2)}) collective-permute-start(f32[8,512]{1,0:T(8,128)} %loads_ref.5), channel_id=1, source_target_pairs={{0,1},{1,2},{2,3},{3,4},{4,5},{5,6},{6,7},{7,8},{8,9},{9,10},{10,1... | collective-permute-start | bytes 49160 | tf_op jit(solution)/shard_map/ppermute | solution.py:177
  3.6 1.2 %copy-start = (f32[256,8,128]{2,1,0:T(8,128)S(1)}, f32[256,8,128]{2,1,0:T(8,128)}, u32[]{:S(2)}) copy-start(f32[256,8,128]{2,1,0:T(8,128)} %motifs_ref.3) | copy-start | bytes 3145732
  4.8 1.0 %copy-start.2 = (f32[256,512]{1,0:T(8,128)S(1)}, f32[256,512]{1,0:T(8,128)}, u32[]{:S(2)}) copy-start(f32[256,512]{1,0:T(8,128)} %counts_ref.3) | copy-start | bytes 1572868
  5.9 0.7 %copy-start.7 = (f32[8,512]{1,0:T(8,128)S(1)}, f32[8,512]{1,0:T(8,128)}, u32[]{:S(2)}) copy-start(f32[8,512]{1,0:T(8,128)} %loads_ref.5) | copy-start | bytes 49156
  6.6 2.4 %copy-start.3 = (f32[256,512]{1,0:T(8,128)S(1)}, f32[256,512]{1,0:T(8,128)}, u32[]{:S(2)}) copy-start(f32[256,512]{1,0:T(8,128)} %counts_ref.3) | copy-start | bytes 1572868
  8.2 0.8 %copy-start.4 = (bf16[256,1024]{1,0:T(8,128)(2,1)}, bf16[256,1024]{1,0:T(8,128)(2,1)S(1)}, u32[]{:S(2)}) copy-start(bf16[256,1024]{1,0:T(8,128)(2,1)S(1)} %get-tuple-element.20.ml_ref) | copy-start | bytes 1572868
  9.0 1.0 %copy-start.5 = (bf16[256,1024]{1,0:T(8,128)(2,1)S(1)}, bf16[256,1024]{1,0:T(8,128)(2,1)}, u32[]{:S(2)}) copy-start(bf16[256,1024]{1,0:T(8,128)(2,1)} %copy-done.4) | copy-start | bytes 1572868
  10.0 0.7 %copy-start.8 = (f32[8,512]{1,0:T(8,128)S(1)}, f32[8,512]{1,0:T(8,128)}, u32[]{:S(2)}) copy-start(f32[8,512]{1,0:T(8,128)} %loads_ref.5) | copy-start | bytes 49156
  15.0 0.7 %copy-start.10 = (bf16[256,512]{1,0:T(8,128)(2,1)}, bf16[256,512]{1,0:T(8,128)(2,1)S(1)}, u32[]{:S(2)}) copy-start(bf16[256,512]{1,0:T(8,128)(2,1)S(1)} %get-tuple-element.31.fh_ref) | copy-start | bytes 786436
  15.8 0.7 %copy-start.12 = (bf16[256,512]{1,0:T(8,128)(2,1)}, bf16[256,512]{1,0:T(8,128)(2,1)S(1)}, u32[]{:S(2)}) copy-start(bf16[256,512]{1,0:T(8,128)(2,1)S(1)} %get-tuple-element.32.fl_ref) | copy-start | bytes 786436
  16.5 23.2 %copy-start.1 = (f32[256,8,128]{2,1,0:T(8,128)S(1)}, f32[256,8,128]{2,1,0:T(8,128)}, u32[]{:S(2)}) copy-start(f32[256,8,128]{2,1,0:T(8,128)} %motifs_ref.3) | copy-start | bytes 3145732
  16.5 3.8 %collective-permute-start.1 = (f32[129,8,128]{2,1,0:T(8,128)}, f32[129,8,128]{2,1,0:T(8,128)S(1)}, u32[]{:S(2)}, u32[]{:S(2)}) collective-permute-start(f32[129,8,128]{2,1,0:T(8,128)} %bitcast.7), channel_id=1, source_target_pairs={{0,1},{1,0},{2,3},{3,2},{4,5},{5,4},{6,7},{7,6},{8,9},{9,8},{10,11... | collective-permute-start | bytes 1585160 | tf_op jit(solution)/shard_map/ppermute | solution.py:175
  20.3 6.5 %collective-permute-start.2 = (f32[65,8,128]{2,1,0:T(8,128)S(1)}, f32[65,8,128]{2,1,0:T(8,128)S(1)}, u32[]{:S(2)}, u32[]{:S(2)}) collective-permute-start(f32[65,8,128]{2,1,0:T(8,128)S(1)} %get-tuple-element.28), channel_id=1, source_target_pairs={{0,2},{1,5},{2,0},{3,7},{4,6},{5,1},{6,4},{7,3},{8,10},{9,13},{10,... | collective-permute-start | bytes 798728 | tf_op jit(solution)/shard_map/ppermute | solution.py:175
  26.8 5.1 %collective-permute-start.3 = (f32[33,8,128]{2,1,0:T(8,128)S(1)}, f32[33,8,128]{2,1,0:T(8,128)S(1)}, u32[]{:S(2)}, u32[]{:S(2)}) collective-permute-start(f32[33,8,128]{2,1,0:T(8,128)S(1)} %get-tuple-element.30), channel_id=1, source_target_pairs={{0,4},{1,3},{2,6},{3,1},{4,0},{5,7},{6,2},{7,5},{8,12},{9,11},{10,... | collective-permute-start | bytes 405512 | tf_op jit(solution)/shard_map/ppermute | solution.py:175
  31.9 7.7 %collective-permute-start.4 = (f32[33,8,128]{2,1,0:T(8,128)S(1)}, f32[33,8,128]{2,1,0:T(8,128)S(1)}, u32[]{:S(2)}, u32[]{:S(2)}) collective-permute-start(f32[33,8,128]{2,1,0:T(8,128)S(1)} %pair.1.mine_ref), channel_id=1, source_target_pairs={{0,8},{1,9},{2,10},{3,11},{4,12},{5,13},{6,14},{7,15},{8,0},{9,1},... | collective-permute-start | bytes 405512 | tf_op jit(solution)/shard_map/ppermute | solution.py:175
  39.7 6.1 %collective-permute-start.5 = (f32[32,8,128]{2,1,0:T(8,128)S(1)}, f32[32,8,128]{2,1,0:T(8,128)S(1)}, u32[]{:S(2)}, u32[]{:S(2)}) collective-permute-start(f32[32,8,128]{2,1,0:T(8,128)S(1)} %update.1.mine_ref), channel_id=1, source_target_pairs={{0,4},{1,3},{2,6},{3,1},{4,0},{5,7},{6,2},{7,5},{8,12},{9,11},{10,... | collective-permute-start | bytes 393224 | tf_op jit(solution)/shard_map/ppermute | solution.py:175
  45.8 6.6 %copy-start.6 = (bf16[256,1024]{1,0:T(8,128)(2,1)S(1)}, bf16[256,1024]{1,0:T(8,128)(2,1)}, u32[]{:S(2)}) copy-start(bf16[256,1024]{1,0:T(8,128)(2,1)} %copy-done.4) | copy-start | bytes 1572868
  45.8 6.6 %copy-start.11 = (bf16[256,512]{1,0:T(8,128)(2,1)S(1)}, bf16[256,512]{1,0:T(8,128)(2,1)}, u32[]{:S(2)}) copy-start(bf16[256,512]{1,0:T(8,128)(2,1)} %copy-done.10) | copy-start | bytes 786436
  45.8 6.6 %copy-start.13 = (bf16[256,512]{1,0:T(8,128)(2,1)S(1)}, bf16[256,512]{1,0:T(8,128)(2,1)}, u32[]{:S(2)}) copy-start(bf16[256,512]{1,0:T(8,128)(2,1)} %copy-done.12) | copy-start | bytes 786436
  45.9 6.4 %collective-permute-start.6 = (f32[64,8,128]{2,1,0:T(8,128)S(1)}, f32[64,8,128]{2,1,0:T(8,128)S(1)}, u32[]{:S(2)}, u32[]{:S(2)}) collective-permute-start(f32[64,8,128]{2,1,0:T(8,128)S(1)} %join.3.mine_ref), channel_id=1, source_target_pairs={{0,2},{1,5},{2,0},{3,7},{4,6},{5,1},{6,4},{7,3},{8,10},{9,13},{10,... | collective-permute-start | bytes 786440 | tf_op jit(solution)/shard_map/ppermute | solution.py:175
  52.3 10.9 %collective-permute-start.7 = (f32[128,8,128]{2,1,0:T(8,128)S(1)}, f32[128,8,128]{2,1,0:T(8,128)S(1)}, u32[]{:S(2)}, u32[]{:S(2)}) collective-permute-start(f32[128,8,128]{2,1,0:T(8,128)S(1)} %join.4.mine_ref), channel_id=1, source_target_pairs={{0,1},{1,0},{2,3},{3,2},{4,5},{5,4},{6,7},{7,6},{8,9},{9,8},{10,11... | collective-permute-start | bytes 1572872 | tf_op jit(solution)/shard_map/ppermute | solution.py:175
  55.5 3.1 %collective-permute-start.8 = (f32[8,128]{1,0:T(8,128)S(1)}, f32[8,128]{1,0:T(8,128)S(1)}, u32[]{:S(2)}, u32[]{:S(2)}) collective-permute-start(f32[8,128]{1,0:T(8,128)S(1)} %get-tuple-element.34), channel_id=1, source_target_pairs={{1,0},{2,1},{3,2},{4,3},{5,4},{6,5},{7,6},{8,7},{9,8},{10,9},{11,1... | collective-permute-start | bytes 12296 | tf_op jit(solution)/shard_map/ppermute | solution.py:204
  58.6 3.8 %copy-start.9 = (f32[8,512]{1,0:T(8,128)S(1)}, f32[8,512]{1,0:T(8,128)}, u32[]{:S(2)}) copy-start(f32[8,512]{1,0:T(8,128)} %loads_ref.5) | copy-start | bytes 49156
  58.6 3.8 %collective-permute-start.9 = (f32[8,640]{1,0:T(8,128)S(1)}, f32[8,640]{1,0:T(8,128)S(1)}, u32[]{:S(2)}, u32[]{:S(2)}) collective-permute-start(f32[8,640]{1,0:T(8,128)S(1)} %halo.1.mine_ref), channel_id=1, source_target_pairs={{0,16},{16,0},{1,17},{17,1},{2,18},{18,2},{3,19},{19,3},{4,20},{20... | collective-permute-start | bytes 61448 | tf_op jit(solution)/shard_map/ppermute | solution.py:233

commit v2 on v0

v2 whole, which is shorter than its diff:
```python
import functools

import jax
import jax.numpy as jnp
from jax import lax
from jax.experimental import pallas as pl
from jax.experimental.pallas import tpu as pltpu
from jax.sharding import PartitionSpec as P

F32, BF16 = jnp.float32, jnp.bfloat16
NN = (((1,), (0,)), ((), ()))
NT = (((1,), (1,)), ((), ()))
TN = (((0,), (0,)), ((), ()))
MIB = 1024 * 1024
BODY_LIMIT = 20
ONES = 16
CHUNKS = 2


def split(x):
    high = x.astype(BF16)
    return high, (x - high.astype(F32)).astype(BF16)


def dot3(ah, al, bh, bl, dims):
    def dot(a, b):
        return lax.dot_general(a, b, dims, preferred_element_type=F32)

    return dot(ah, bh) + (dot(ah, bl) + dot(al, bh))


def toeplitz(row, lags):
    return pltpu.roll(jnp.broadcast_to(row, (lags, row.shape[1])), 0, 1, stride=1, stride_axis=0)


def place(me, step, steps):
    first, second = (order(core, steps)[step] for core in range(2))
    return jnp.where(me & 1 == 0, (me >> first) & 1, (me >> second) & 1)


def order(core, steps):
    return [0, 2, 1, *range(3, steps)] if core else list(range(steps))


def call(kernel, out_shapes, *args, limit=4, spaces=None, outs=None, scratch=(), aliases=None, flops=0, moved=0):
    spaces = spaces or [pltpu.VMEM] * (len(args) - 1)
    outs = outs or [pltpu.VMEM] * len(out_shapes)
    return pl.pallas_call(
        kernel,
        out_shape=out_shapes,
        in_specs=[pl.BlockSpec(memory_space=space) for space in [pltpu.SMEM, *spaces]],
        out_specs=[pl.BlockSpec(memory_space=space) for space in outs],
        scratch_shapes=list(scratch),
        input_output_aliases=aliases or {},
        compiler_params=pltpu.CompilerParams(vmem_limit_bytes=int(limit * MIB)),
        cost_estimate=pl.CostEstimate(flops=flops, bytes_accessed=moved, transcendentals=0),
        name=getattr(kernel, "func", kernel).__name__,
    )(*args)


def body_kernel(me_ref, counts_hbm, motifs_hbm, loads_hbm, mh_ref, ml_ref, rh_ref, rl_ref, numer_ref, counts_ref,
                loads_ref, total_ref, motifs_ref, rest_ref, th, tl, sems):
    rows, frames = counts_hbm.shape
    motif_count = loads_ref.shape[0]
    lags = counts_ref.shape[1]
    copies = [
        pltpu.make_async_copy(loads_hbm, loads_ref, sems.at[0]),
        pltpu.make_async_copy(motifs_hbm, motifs_ref, sems.at[1]),
        pltpu.make_async_copy(counts_hbm.at[:, pl.ds(lags, frames - lags)], rest_ref, sems.at[2]),
        pltpu.make_async_copy(counts_hbm.at[:, pl.ds(0, lags)], counts_ref, sems.at[3]),
    ]
    for copy in copies:
        copy.start()
    copies[0].wait()
    for k in range(motif_count):
        at = pl.ds(k * lags, lags)
        th[at, :], tl[at, :] = split(toeplitz(loads_ref[pl.ds(k, 1), :], lags)[:, lags:])
    copies[1].wait()
    for k in range(motif_count):
        at = pl.ds(k * lags, lags)
        mh_ref[:, at], ml_ref[:, at] = split(motifs_ref[pl.ds(k, rows, stride=motif_count), :])
    estimate = dot3(mh_ref[...], ml_ref[...], th[...], tl[...], NN)
    copies[2].wait()
    rh_ref[...], rl_ref[...] = split(rest_ref[...] / estimate)
    ones = jnp.ones((ONES, frames - lags), BF16)
    xh = jnp.concatenate([rh_ref[...], ones], axis=0)
    xl = jnp.concatenate([rl_ref[...], jnp.zeros_like(ones)], axis=0)
    for k in range(0, motif_count, 2):
        at = pl.ds(k * lags, 2 * lags)
        numer_ref[:, at] = dot3(xh, xl, th[at, :], tl[at, :], NT)
    total_ref[...] = jnp.sum(motifs_ref[...].reshape(rows, motif_count, lags), axis=0)
    copies[3].wait()


def numer_rows(numer, motif_count, out_ref, count):
    lags = out_ref.shape[-1]
    for k in range(motif_count):
        out_ref[pl.ds(k, count, stride=motif_count), :] = numer[:count, k * lags:(k + 1) * lags]


def head_kernel(chunks, me_ref, tail_ref, counts_ref, loads_ref, mh_ref, ml_ref, numer_ref, *refs):
    *send_refs, fh_ref, fl_ref, hh_ref, hl_ref, denom_ref = refs
    rows, lags = counts_ref.shape
    motif_count, frames = loads_ref.shape
    for k in range(motif_count):
        at = pl.ds(k * lags, lags)
        row = jnp.concatenate([tail_ref[pl.ds(k, 1), frames - lags:], loads_ref[pl.ds(k, 1), :lags]], axis=1)
        hh_ref[at, :], hl_ref[at, :] = split(toeplitz(row, lags)[:, lags:])
    estimate = dot3(mh_ref[...], ml_ref[...], hh_ref[...], hl_ref[...], NN)
    fh_ref[...], fl_ref[...] = split(counts_ref[...] / estimate)
    half = rows // chunks // 2
    away = [pl.ds(pl.multiple_of((2 * c + 1 - (me_ref[0] & 1)) * half, half), half) for c in range(chunks)]
    ones = jnp.ones((ONES, lags), BF16)
    xh = jnp.concatenate([*(fh_ref[at, :] for at in away), ones], axis=0)
    xl = jnp.concatenate([*(fl_ref[at, :] for at in away), jnp.zeros_like(ones)], axis=0)
    for k in range(0, motif_count, 2):
        at = pl.ds(k * lags, 2 * lags)
        numer = dot3(xh, xl, hh_ref[at, :], hl_ref[at, :], NT)
        for j in range(2):
            there, here = pl.ds((k + j) * lags, lags), slice(j * lags, (j + 1) * lags)
            for c in range(chunks):
                send_refs[c][pl.ds(k + j, half, stride=motif_count), :] = (
                    numer[c * half:(c + 1) * half, here] + numer_ref[away[c], there]
                )
            denom = numer[chunks * half:chunks * half + 1, here] + numer_ref[pl.ds(rows, 1), there]
            send_refs[0][pl.ds(half * motif_count + k + j, 1), :] = denom
            denom_ref[pl.ds(k + j, 1), :] = denom


def home_kernel(chunks, me_ref, fh_ref, fl_ref, hh_ref, hl_ref, denom_ref, numer_ref, *keep_refs):
    rows, lags = fh_ref.shape
    motif_count = denom_ref.shape[0]
    half = rows // chunks // 2
    home = [pl.ds(pl.multiple_of((2 * c + (me_ref[0] & 1)) * half, half), half) for c in range(chunks)]
    xh = jnp.concatenate([fh_ref[at, :] for at in home], axis=0)
    xl = jnp.concatenate([fl_ref[at, :] for at in home], axis=0)
    for k in range(0, motif_count, 2):
        at = pl.ds(k * lags, 2 * lags)
        numer = dot3(xh, xl, hh_ref[at, :], hl_ref[at, :], NT)
        for j in range(2):
            there, here = pl.ds((k + j) * lags, lags), slice(j * lags, (j + 1) * lags)
            for c in range(chunks):
                keep_refs[c][pl.ds(k + j, half, stride=motif_count), :] = (
                    numer[c * half:(c + 1) * half, here] + numer_ref[home[c], there]
                )
    keep_refs[0][pl.ds(half * motif_count, motif_count), :] = denom_ref[...]


def fold_kernel(step, steps, half, me_ref, mine_ref, got_ref, send_ref, keep_ref):
    bit = place(me_ref[0], step, steps)
    for out, part in ((send_ref, 1 - bit), (keep_ref, bit)):
        at = pl.ds(part * half, half)
        out[:half] = mine_ref[at] + got_ref[at]
        if out.shape[0] > half:
            out[half:] = mine_ref[2 * half:] + got_ref[2 * half:]


def pair_kernel(me_ref, mine_ref, got_ref, out_ref):
    out_ref[...] = mine_ref[...] + got_ref[...]


def update_kernel(chunk, steps, me_ref, mine_ref, got_ref, denom_ref, motifs_ref, out_ref, *denom_out):
    rows = out_ref.shape[0]
    at, size = chunk, rows << (steps - 1)
    at = chunk * size
    for step in range(steps - 1):
        size //= 2
        at = at + place(me_ref[0], step, steps) * size
    numer = mine_ref[:rows] + got_ref[:rows]
    if denom_out:
        denom = mine_ref[rows] + got_ref[rows]
        denom_out[0][...] = denom
    else:
        denom = denom_ref[...]
    out_ref[...] = motifs_ref[pl.ds(at, rows)] * numer / denom[None]


def join_kernel(step, steps, me_ref, mine_ref, got_ref, out_ref):
    half = mine_ref.shape[0]
    bit = place(me_ref[0], step, steps)
    out_ref[pl.ds(bit * half, half)] = mine_ref[...]
    out_ref[pl.ds((1 - bit) * half, half)] = got_ref[...]


def store_kernel(parts, me_ref, *refs):
    blocks, out_hbm, sems = refs[:len(parts)], refs[-2], refs[-1]
    core = me_ref[0] & 1
    copies = []
    for i, ((at, own), block) in enumerate(zip(parts, blocks)):
        rows = block.shape[0]
        at = at + (core if own else 1 - core) * rows
        copies.append(pltpu.make_async_copy(block, out_hbm.at[pl.ds(at, rows)], sems.at[i]))
    for copy in copies:
        copy.start()
    for copy in copies:
        copy.wait()


def lagged_kernel(me_ref, mh_ref, ml_ref, fh_ref, fl_ref, rh_ref, rl_ref, numer_ref, ahead_ref, ph, pw):
    motif_count, frames = numer_ref.shape
    lags = ahead_ref.shape[1]
    width = frames + lags
    down = lax.broadcasted_iota(jnp.int32, (lags, lags), 0)
    across = lax.broadcasted_iota(jnp.int32, (lags, lags), 1)
    flip = (down + across == lags - 1).astype(BF16)
    xh = jnp.concatenate([fh_ref[...], rh_ref[...]], axis=1)
    xl = jnp.concatenate([fl_ref[...], rl_ref[...]], axis=1)
    for k in range(motif_count):
        at = pl.ds(k * lags, lags)
        for ref, out in ((mh_ref, ph), (ml_ref, pw)):
            out[:, at] = lax.dot_general(ref[:, at], flip, NN, preferred_element_type=F32).astype(BF16)
    for k in range(0, motif_count, 4):
        at = pl.ds(k * lags, 4 * lags)
        lagged = dot3(ph[:, at], pw[:, at], xh, xl, TN)
        for j in range(4):
            wide = jnp.concatenate([jnp.zeros((lags, lags), F32), lagged[j * lags:(j + 1) * lags]], axis=1)
            skewed = pltpu.roll(wide, width - (lags - 1), 1, stride=1, stride_axis=0)
            numer = jnp.sum(skewed, axis=0, keepdims=True)
            ahead_ref[pl.ds(k + j, 1), :] = numer[:, :lags]
            numer_ref[pl.ds(k + j, 1), :] = numer[:, lags:]


def halo_kernel(me_ref, numer_ref, ahead_ref, total_ref, out_ref):
    frames, lags = numer_ref.shape[1], ahead_ref.shape[1]
    out_ref[:, :frames - lags] = numer_ref[:, :frames - lags]
    out_ref[:, frames - lags:frames] = numer_ref[:, frames - lags:] + ahead_ref[...]
    out_ref[:, frames:] = total_ref[...]


def loads_kernel(ranks, me_ref, mine_ref, got_ref, loads_ref, out_ref):
    frames = loads_ref.shape[1]
    lags = mine_ref.shape[1] - frames
    both = mine_ref[...] + got_ref[...]
    left = (ranks - me_ref[0]) * frames
    lag = lax.broadcasted_iota(jnp.int32, (lags, frames), 0)
    frame = lax.broadcasted_iota(jnp.int32, (lags, frames), 1)
    valid = (lag + frame < left).astype(F32)
    denom = lax.dot_general(both[:, frames:], valid, NN, precision=lax.Precision.HIGHEST, preferred_element_type=F32)
    out_ref[...] = loads_ref[...] * both[:, :frames] / denom


def body(counts, motifs, loadings):
    rows, motif_count, lags = motifs.shape
    frames = loadings.shape[1]
    ranks, groups = lax.axis_size("tm"), lax.axis_size("neur")
    steps, flips = ranks.bit_length() - 1, groups.bit_length() - 1
    assert ranks == 1 << steps and groups == 1 << flips and steps >= 3 and rows % (ranks * CHUNKS) == 0

    def shape(*dims, dtype=F32):
        return jax.ShapeDtypeStruct(dims, dtype)

    def swap(x, step):
        return lax.ppermute(x, "tm", [(i, i ^ (1 << order(i & 1, steps)[step])) for i in range(ranks)])

    me = lax.axis_index("tm").astype(jnp.int32).reshape(1)
    tail = lax.ppermute(loadings, "tm", [(i, i + 1) for i in range(ranks - 1)])
    flat = motifs.reshape(rows * motif_count, lags)
    depth, rest = motif_count * lags, frames - lags
    macs = rows * depth * frames * 3
    mh, ml, rh, rl, numer, head_counts, own_loads, total = call(
        body_kernel,
        [shape(rows, depth, dtype=BF16)] * 2 + [shape(rows, rest, dtype=BF16)] * 2
        + [shape(rows + ONES, depth), shape(rows, lags), shape(motif_count, frames), shape(motif_count, lags)],
        me, *(pltpu.with_memory_space_constraint(x, pltpu.HBM) for x in (counts, flat, loadings)),
        spaces=[pltpu.HBM] * 3,
        scratch=[pltpu.VMEM((rows * motif_count, lags), F32), pltpu.VMEM((rows, rest), F32)]
        + [pltpu.VMEM((depth, rest), BF16)] * 2 + [pltpu.SemaphoreType.DMA((4,))],
        limit=BODY_LIMIT, flops=4 * macs,
    )
    half = rows // CHUNKS // 2
    sizes = [half + 1] + [half] * (CHUNKS - 1)
    parts = [shape(size * motif_count, lags) for size in sizes]
    *send, fh, fl, hh, hl, denom = call(
        functools.partial(head_kernel, CHUNKS),
        parts + [shape(rows, lags, dtype=BF16)] * 2 + [shape(depth, lags, dtype=BF16)] * 2 + [shape(motif_count, lags)],
        me, tail, head_counts, own_loads, mh, ml, numer, limit=6,
    )

    def cube(x):
        return x.reshape(-1, motif_count, lags)

    got = [swap(cube(x), 0) for x in send]
    keep = call(
        functools.partial(home_kernel, CHUNKS), parts, me, fh, fl, hh, hl, denom, numer, limit=6, flops=macs // 4
    )
    keep = [cube(x) for x in keep]
    part, ahead = call(
        lagged_kernel, [shape(motif_count, frames), shape(motif_count, lags)], me, mh, ml, fh, fl, rh, rl,
        scratch=[pltpu.VMEM((rows, depth), BF16)] * 2, limit=8, flops=2 * macs,
    )

    for step in range(1, steps - 1):
        half //= 2
        for c in range(CHUNKS):
            sums = [shape(half + (c == 0), motif_count, lags)] * 2
            send[c], keep[c] = call(
                functools.partial(fold_kernel, step, steps, half), sums, me, keep[c], got[c]
            )
            got[c] = swap(send[c], step)
        if step == 1:
            got[0], part, ahead = lax.optimization_barrier((got[0], part, ahead))
        if step == 2:
            ahead = lax.ppermute(ahead, "tm", [(i, i - 1) for i in range(1, ranks)])
            (part,) = call(halo_kernel, [shape(motif_count, frames + lags)], me, part, ahead, total)
            got[0], part = lax.optimization_barrier((got[0], part))
    for c in range(CHUNKS):
        (keep[c],) = call(pair_kernel, [shape(half + (c == 0), motif_count, lags)], me, keep[c], got[c])
        got[c] = swap(keep[c], steps - 1)
    other = jnp.zeros_like(part)
    for flip in range(flips):
        if flip:
            (part,) = call(pair_kernel, [part], me, part, other)
        other = lax.ppermute(part, "neur", [(i, i ^ (1 << flip)) for i in range(groups)])
    (new_loadings,) = call(
        functools.partial(loads_kernel, ranks), [shape(motif_count, frames)], me, part, other, own_loads
    )
    got[0], new_loadings = lax.optimization_barrier((got[0], new_loadings))
    mine = [None] * CHUNKS
    for c in range(CHUNKS):
        mine[c], *more = call(
            functools.partial(update_kernel, c, steps), [shape(half, motif_count, lags)] + [shape(motif_count, lags)] * (c == 0),
            me, keep[c], got[c], denom, motifs,
        )
        if more:
            denom = more[0]
    for step in range(steps - 2, 0, -1):
        for c in range(CHUNKS):
            got[c] = swap(mine[c], step)
        half *= 2
        for c in range(CHUNKS):
            (mine[c],) = call(
                functools.partial(join_kernel, step, steps), [shape(half, motif_count, lags)], me, mine[c], got[c]
            )
    out = None
    waiting = []
    for c in range(CHUNKS):
        got[c] = swap(mine[c], 0)
        waiting.append(((c * half * 2, True), mine[c]))
        out = store(me, out, motifs, waiting)
        waiting = [((c * half * 2, False), got[c])]
    return store(me, out, motifs, waiting), new_loadings


def store(me, out, like, waiting):
    places, blocks = zip(*waiting)
    given = [] if out is None else [out]
    (out,) = call(
        functools.partial(store_kernel, places), [jax.ShapeDtypeStruct(like.shape, F32)], me, *blocks, *given,
        spaces=[pltpu.VMEM] * len(blocks) + [pltpu.HBM] * len(given), outs=[pltpu.HBM],
        scratch=[pltpu.SemaphoreType.DMA((len(blocks),))], aliases={len(blocks) + 1: 0} if given else None,
    )
    return out


def solution(mesh):
    in_specs = (P("neur", "tm"), P("neur", None, None), P(None, "tm"))
    out_specs = (P("neur", None, None), P(None, "tm"))
    return jax.shard_map(body, mesh=mesh, in_specs=in_specs, out_specs=out_specs, check_vma=False)
```

time: 155 us -> 45.8 us (0.30)
  blocking collectives: 42.2 us -> 0 us
  local copies, waits for them, and re-layouts: 33.9 us -> 0.01 us
  waiting for transfers between devices: 43.9 us -> 13.5 us
  starting transfers between devices: 3.9 us -> 21 us
  matrix products: 13.6 us -> 0 us
  between operations: 14.2 us -> 0.81 us
  Pallas kernels: 0 us -> 10.2 us
  other arithmetic: 2.11 us -> 0 us
    psum x2 -> x0, blocking collectives: 42.2 us -> none  [the longest x1 34 us: body(): denom_w = lax.psum(denom_local, 'tm')]
    reduce_scatter x1 -> x0, waiting for transfers between devices: 26.5 us -> none  [body(): lax.psum_scatter(lax.dot_general(ratio_field, shifted, contract_frames, p...]
    ppermute x2 -> x17, starting transfers between devices: 3.82 us -> 21 us  [the longest x14 15.9 us: swap(): lax.ppermute(x, 'tm', [(i, i ^ 1 << order(i & 1, steps)[step]) for i in r...]
    all_gather x1 -> x0, waiting for transfers between devices: 15.8 us -> none  [body(): new_motifs = lax.all_gather(updated_share, 'tm', axis=0, tiled=True)]
    rev x1 -> x0, local copies, waits for them, and re-layouts: 13.7 us -> none  [toeplitz(): return skew_left(stacked, out_width)[:, ::-1, :]]
    dot_general x4 -> x0, matrix products: 13.6 us -> none  [the longest x1 4.59 us: body(): lax.dot_general(ratio_field, shifted, contract_frames, precision=highest)]
    ppermute x2 -> x17, waiting for transfers between devices: 1.48 us -> 13.5 us  [the longest x14 9.3 us: swap(): lax.ppermute(x, 'tm', [(i, i ^ 1 << order(i & 1, steps)[step]) for i in r...]
    pallas_call x0 -> x21, Pallas kernels: none -> 10.2 us  [call(): pl.pallas_call(kernel, out_shape=out_shapes, in_specs=[pl.BlockSpec(memor...]
  transfers between devices with their start and end apart: 4 -> 17, of which waited for: 3 -> 8; matrix products, arithmetic and copies ran while one was open for 9% -> 0% of each run, Pallas kernels for 0% -> 18%
where the time goes in v2:
time: 45.8 us; the launch traced here: 45.5 us
  starting transfers between devices  21 us (46%)
  waiting for transfers between devices  13.5 us (29%)
  Pallas kernels  10.2 us (22%)
  between operations  0.81 us (2%)
    ppermute x14, starting transfers between devices, swap(): lax.ppermute(x, 'tm', [(i, i ^ 1 << order(i & 1, steps)[step]) for i in r...  15.9 us
    pallas_call x21, Pallas kernels, call(): pl.pallas_call(kernel, out_shape=out_shapes, in_specs=[pl.BlockSpec(memor...  10.2 us
    ppermute x14, waiting for transfers between devices, swap(): lax.ppermute(x, 'tm', [(i, i ^ 1 << order(i & 1, steps)[step]) for i in r...  9.3 us
    ppermute x1, waiting for transfers between devices, body(): lax.ppermute(part, 'neur', [(i, i ^ 1 << flip) for i in range(groups)])  2.44 us
    ppermute x1, starting transfers between devices, body(): tail = lax.ppermute(loadings, 'tm', [(i, i + 1) for i in range(ranks - 1)])  2.36 us
    ppermute x1, waiting for transfers between devices, body(): ahead = lax.ppermute(ahead, 'tm', [(i, i - 1) for i in range(1, ranks)])  1.76 us
    ppermute x1, starting transfers between devices, body(): lax.ppermute(part, 'neur', [(i, i ^ 1 << flip) for i in range(groups)])  1.49 us
    ppermute x1, starting transfers between devices, body(): ahead = lax.ppermute(ahead, 'tm', [(i, i - 1) for i in range(1, ranks)])  1.28 us
  transfers between devices with their start and end apart: 17, of which 8 were waited for; matrix products, arithmetic and copies ran while one was open for 0% of the time, Pallas kernels for 18%

profile of v2, /device:TPU:0, one launch (start us, length us, event | category | flops | bytes accessed | tf_op | source)
XLA Modules:
  0.0 45.5 jit_solution(13263273255325147257)
XLA Ops:
  0.6 2.4 %collective-permute-start = (f32[8,512]{1,0:T(8,128)}, f32[8,512]{1,0:T(8,128)S(1)}, u32[]{:S(2)}, u32[]{:S(2)}) collective-permute-start(f32[8,512]{1,0:T(8,128)} %loads_hbm.1), channel_id=1, source_target_pairs={{0,1},{1,2},{2,3},{3,4},{4,5},{5,6},{6,7},{7,8},{8,9},{9,10},{10,1... | collective-permute-start | bytes 49160 | tf_op jit(solution)/shard_map/ppermute | solution.py:256
  3.0 3.6 %body_kernel.1 = (bf16[256,1024]{1,0:T(8,128)(2,1)S(1)}, bf16[256,1024]{1,0:T(8,128)(2,1)S(1)}, bf16[256,384]{1,0:T(8,128)(2,1)S(1)}, bf16[256,384]{1,0:T(8,128)...) custom-call(s32[1]{0:T(128)} %bitcast.me_ref, ...), custom_call_target="tpu_custom_call" | custom-call | flops 1610612736 | tf_op jit(solution)/shard_map/body_kernel/pallas_call | solution.py:48
  6.6 1.3 %head_kernel.1 = (f32[520,128]{1,0:T(8,128)S(1)}, f32[512,128]{1,0:T(8,128)S(1)}, bf16[256,128]{1,0:T(8,128)(2,1)S(1)}, bf16[256,128]{1,0:T(8,128)(2,1)S(1)}, bf...) custom-call(s32[1]{0:T(128)} %bitcast.me_ref, ...), custom_call_target="tpu_custom_call" | custom-call | tf_op jit(solution)/shard_map/head_kernel/pallas_call | solution.py:48
  7.9 2.7 %collective-permute-start.5 = (f32[65,8,128]{2,1,0:T(8,128)S(1)}, f32[65,8,128]{2,1,0:T(8,128)S(1)}, u32[]{:S(2)}, u32[]{:S(2)}) collective-permute-start(f32[65,8,128]{2,1,0:T(8,128)S(1)} %bitcast.9), channel_id=1, source_target_pairs={{0,1},{1,0},{2,3},{3,2},{4,5},{5,4},{6,7},{7,6},{8,9},{9,8},{10,11... | collective-permute-start | bytes 798728 | tf_op jit(solution)/shard_map/ppermute | solution.py:253
  10.6 0.1 collective-permute-start.1
  10.7 0.4 home_kernel.1
  11.1 0.7 %collective-permute-done.5.got_ref = f32[65,8,128]{2,1,0:T(8,128)S(1)} collective-permute-done((f32[65,8,128]{2,1,0:T(8,128)S(1)}, f32[65,8,128]{2,1,0:T(8,128)S(1)}, u32[]{:S(2)}, u32[]{:S(2)}) %collective-permute-start.5) | collective-permute-done | bytes 266272 | tf_op jit(solution)/shard_map/ppermute | solution.py:253
  11.8 1.6 %collective-permute-start.6 = (f32[33,8,128]{2,1,0:T(8,128)S(1)}, f32[33,8,128]{2,1,0:T(8,128)S(1)}, u32[]{:S(2)}, u32[]{:S(2)}) collective-permute-start(f32[33,8,128]{2,1,0:T(8,128)S(1)} %get-tuple-element.57), channel_id=1, source_target_pairs={{0,2},{1,5},{2,0},{3,7},{4,6},{5,1},{6,4},{7,3},{8,10},{9,13},{10,... | collective-permute-start | bytes 405512 | tf_op jit(solution)/shard_map/ppermute | solution.py:253
  13.4 0.6 %collective-permute-start.2 = (f32[32,8,128]{2,1,0:T(8,128)S(1)}, f32[32,8,128]{2,1,0:T(8,128)S(1)}, u32[]{:S(2)}, u32[]{:S(2)}) collective-permute-start(f32[32,8,128]{2,1,0:T(8,128)S(1)} %get-tuple-element.51), channel_id=1, source_target_pairs={{0,2},{1,5},{2,0},{3,7},{4,6},{5,1},{6,4},{7,3},{8,10},{9,13},{10,... | collective-permute-start | bytes 393224 | tf_op jit(solution)/shard_map/ppermute | solution.py:253
  14.0 1.6 %lagged_kernel.1 = (f32[8,512]{1,0:T(8,128)S(1)}, f32[8,128]{1,0:T(8,128)S(1)}) custom-call(s32[1]{0:T(128)} %bitcast.me_ref, bf16[256,1024]{1,0:T(8,128)(2,1)S(1)} %get-tuple-element.40.mh_ref, bf16[256,1024]{1,0:T(8,128)(2,1)S(1)} %get-tuple-element.41.ml_ref, bf16[256,128]{1,0:T(8,128)(2,1)S(1)} %get-tuple-element.43.fh_ref, ...), custom_call_target="tpu_custom_call" | custom-call | flops 805306368 | tf_op jit(solution)/shard_map/lagged_kernel/pallas_call | solution.py:48
  15.6 1.3 %collective-permute-done.6.got_ref = f32[33,8,128]{2,1,0:T(8,128)S(1)} collective-permute-done((f32[33,8,128]{2,1,0:T(8,128)S(1)}, f32[33,8,128]{2,1,0:T(8,128)S(1)}, u32[]{:S(2)}, u32[]{:S(2)}) %collective-permute-start.6) | collective-permute-done | bytes 135200 | tf_op jit(solution)/shard_map/ppermute | solution.py:253
  16.9 1.6 %collective-permute-start.7 = (f32[17,8,128]{2,1,0:T(8,128)S(1)}, f32[17,8,128]{2,1,0:T(8,128)S(1)}, u32[]{:S(2)}, u32[]{:S(2)}) collective-permute-start(f32[17,8,128]{2,1,0:T(8,128)S(1)} %get-tuple-element.64), channel_id=1, source_target_pairs={{0,4},{1,3},{2,6},{3,1},{4,0},{5,7},{6,2},{7,5},{8,12},{9,11},{10,... | collective-permute-start | bytes 208904 | tf_op jit(solution)/shard_map/ppermute | solution.py:253
  18.6 1.6 %collective-permute-start.3 = (f32[16,8,128]{2,1,0:T(8,128)S(1)}, f32[16,8,128]{2,1,0:T(8,128)S(1)}, u32[]{:S(2)}, u32[]{:S(2)}) collective-permute-start(f32[16,8,128]{2,1,0:T(8,128)S(1)} %get-tuple-element.53), channel_id=1, source_target_pairs={{0,4},{1,3},{2,6},{3,1},{4,0},{5,7},{6,2},{7,5},{8,12},{9,11},{10,... | collective-permute-start | bytes 196616 | tf_op jit(solution)/shard_map/ppermute | solution.py:253
  20.1 1.3 %collective-permute-start.8 = (f32[8,128]{1,0:T(8,128)S(1)}, f32[8,128]{1,0:T(8,128)S(1)}, u32[]{:S(2)}, u32[]{:S(2)}) collective-permute-start(f32[8,128]{1,0:T(8,128)S(1)} %get-tuple-element.66), channel_id=1, source_target_pairs={{1,0},{2,1},{3,2},{4,3},{5,4},{6,5},{7,6},{8,7},{9,8},{10,9},{11,1... | collective-permute-start | bytes 12296 | tf_op jit(solution)/shard_map/ppermute | solution.py:303
  21.4 1.8 %collective-permute-done.8.ahead_ref = f32[8,128]{1,0:T(8,128)S(1)} collective-permute-done((f32[8,128]{1,0:T(8,128)S(1)}, f32[8,128]{1,0:T(8,128)S(1)}, u32[]{:S(2)}, u32[]{:S(2)}) %collective-permute-start.8) | collective-permute-done | bytes 4128 | tf_op jit(solution)/shard_map/ppermute | solution.py:303
  23.2 2.7 %collective-permute-start.9 = (f32[17,8,128]{2,1,0:T(8,128)S(1)}, f32[17,8,128]{2,1,0:T(8,128)S(1)}, u32[]{:S(2)}, u32[]{:S(2)}) collective-permute-start(f32[17,8,128]{2,1,0:T(8,128)S(1)} %pair_kernel.3.mine_ref), channel_id=1, source_target_pairs={{0,8},{1,9},{2,10},{3,11},{4,12},{5,13},{6,14},{7,15},{8,0},{9,1},... | collective-permute-start | bytes 208904 | tf_op jit(solution)/shard_map/ppermute | solution.py:253
  25.9 0.4 collective-permute-start.4
  26.3 1.5 %collective-permute-start.10 = (f32[8,640]{1,0:T(8,128)S(1)}, f32[8,640]{1,0:T(8,128)S(1)}, u32[]{:S(2)}, u32[]{:S(2)}) collective-permute-start(f32[8,640]{1,0:T(8,128)S(1)} %halo_kernel.1.mine_ref), channel_id=1, source_target_pairs={{0,16},{16,0},{1,17},{17,1},{2,18},{18,2},{3,19},{19,3},{4,20},{20... | collective-permute-start | bytes 61448 | tf_op jit(solution)/shard_map/ppermute | solution.py:313
  27.8 2.4 %collective-permute-done.10.got_ref = f32[8,640]{1,0:T(8,128)S(1)} collective-permute-done((f32[8,640]{1,0:T(8,128)S(1)}, f32[8,640]{1,0:T(8,128)S(1)}, u32[]{:S(2)}, u32[]{:S(2)}) %collective-permute-start.10) | collective-permute-done | bytes 20512 | tf_op jit(solution)/shard_map/ppermute | solution.py:313
  30.2 0.9 %loads_kernel.1 = f32[8,512]{1,0:T(8,128)} custom-call(s32[1]{0:T(128)} %bitcast.me_ref, f32[8,640]{1,0:T(8,128)S(1)} %halo_kernel.1.mine_ref, f32[8,640]{1,0:T(8,128)S(1)} %collective-permute-done.10.got_ref, f32[8,512]{1,0:T(8,128)S(1)} %get-tuple-element.39.loads_ref), custom_call_target="tpu_custom_call" | custom-call | tf_op jit(solution)/shard_map/loads_kernel/pallas_call | solution.py:48
  31.1 0.7 %collective-permute-start.14 = (f32[16,8,128]{2,1,0:T(8,128)S(1)}, f32[16,8,128]{2,1,0:T(8,128)S(1)}, u32[]{:S(2)}, u32[]{:S(2)}) collective-permute-start(f32[16,8,128]{2,1,0:T(8,128)S(1)} %get-tuple-element.72.mine_ref), channel_id=1, source_target_pairs={{0,4},{1,3},{2,6},{3,1},{4,0},{5,7},{6,2},{7,5},{8,12},{9,11},{10,... | collective-permute-start | bytes 196616 | tf_op jit(solution)/shard_map/ppermute | solution.py:253
  31.8 1.4 %collective-permute-done.4.got_ref = f32[16,8,128]{2,1,0:T(8,128)S(1)} collective-permute-done((f32[16,8,128]{2,1,0:T(8,128)S(1)}, f32[16,8,128]{2,1,0:T(8,128)S(1)}, u32[]{:S(2)}, u32[]{:S(2)}) %collective-permute-start.4) | collective-permute-done | bytes 65568 | tf_op jit(solution)/shard_map/ppermute | solution.py:253
  33.2 0.1 collective-permute-start.11
  33.3 2.1 %collective-permute-done.14.got_ref = f32[16,8,128]{2,1,0:T(8,128)S(1)} collective-permute-done((f32[16,8,128]{2,1,0:T(8,128)S(1)}, f32[16,8,128]{2,1,0:T(8,128)S(1)}, u32[]{:S(2)}, u32[]{:S(2)}) %collective-permute-start.14) | collective-permute-done | bytes 65568 | tf_op jit(solution)/shard_map/ppermute | solution.py:253
  35.5 2.6 %collective-permute-start.15 = (f32[32,8,128]{2,1,0:T(8,128)S(1)}, f32[32,8,128]{2,1,0:T(8,128)S(1)}, u32[]{:S(2)}, u32[]{:S(2)}) collective-permute-start(f32[32,8,128]{2,1,0:T(8,128)S(1)} %join_kernel.6.mine_ref), channel_id=1, source_target_pairs={{0,2},{1,5},{2,0},{3,7},{4,6},{5,1},{6,4},{7,3},{8,10},{9,13},{10,... | collective-permute-start | bytes 393224 | tf_op jit(solution)/shard_map/ppermute | solution.py:253
  38.1 1.2 %collective-permute-start.12 = (f32[32,8,128]{2,1,0:T(8,128)S(1)}, f32[32,8,128]{2,1,0:T(8,128)S(1)}, u32[]{:S(2)}, u32[]{:S(2)}) collective-permute-start(f32[32,8,128]{2,1,0:T(8,128)S(1)} %join_kernel.4.mine_ref), channel_id=1, source_target_pairs={{0,2},{1,5},{2,0},{3,7},{4,6},{5,1},{6,4},{7,3},{8,10},{9,13},{10,... | collective-permute-start | bytes 393224 | tf_op jit(solution)/shard_map/ppermute | solution.py:253
  39.3 1.8 %collective-permute-done.15.got_ref = f32[32,8,128]{2,1,0:T(8,128)S(1)} collective-permute-done((f32[32,8,128]{2,1,0:T(8,128)S(1)}, f32[32,8,128]{2,1,0:T(8,128)S(1)}, u32[]{:S(2)}, u32[]{:S(2)}) %collective-permute-start.15) | collective-permute-done | bytes 131104 | tf_op jit(solution)/shard_map/ppermute | solution.py:253
  41.0 0.1 collective-permute-start.16
  41.1 2.0 %collective-permute-done.12.got_ref = f32[32,8,128]{2,1,0:T(8,128)S(1)} collective-permute-done((f32[32,8,128]{2,1,0:T(8,128)S(1)}, f32[32,8,128]{2,1,0:T(8,128)S(1)}, u32[]{:S(2)}, u32[]{:S(2)}) %collective-permute-start.12) | collective-permute-done | bytes 131104 | tf_op jit(solution)/shard_map/ppermute | solution.py:253
  43.2 0.7 %store_kernel.3.refs_2_ = f32[256,8,128]{2,1,0:T(8,128)} custom-call(s32[1]{0:T(128)} %bitcast.me_ref, f32[64,8,128]{2,1,0:T(8,128)S(1)} %join_kernel.7.refs_0_), custom_call_target="tpu_custom_call" | custom-call | tf_op jit(solution)/shard_map/store_kernel/pallas_call | solution.py:48
  44.0 0.8 %store_kernel.4.refs_1_ = f32[256,8,128]{2,1,0:T(8,128)} custom-call(s32[1]{0:T(128)} %bitcast.me_ref, f32[64,8,128]{2,1,0:T(8,128)S(1)} %collective-permute-done.16.refs_0_, f32[64,8,128]{2,1,0:T(8,128)S(1)} %join_kernel.5.refs_1_, f32[256,8,128]{2,1,0:T(8,128)} %store_kernel.3.refs_2_), custom_call_target="tpu_custom_call", output_to_operand_aliasing={{}: (3, {})} | custom-call | tf_op jit(solution)/shard_map/store_kernel/pallas_call | solution.py:48
  44.8 0.7 %store_kernel.5 = f32[256,8,128]{2,1,0:T(8,128)} custom-call(s32[1]{0:T(128)} %bitcast.me_ref, f32[64,8,128]{2,1,0:T(8,128)S(1)} %collective-permute-done.13.refs_0_, f32[256,8,128]{2,1,0:T(8,128)} %store_kernel.4.refs_1_), custom_call_target="tpu_custom_call", output_to_operand_aliasing={{}: (2, {})} | custom-call | tf_op jit(solution)/shard_map/store_kernel/pallas_call | solution.py:48
  (25 shorter events, 0.3 us)
Async XLA Ops:
  0.6 6.0 %collective-permute-start = (f32[8,512]{1,0:T(8,128)}, f32[8,512]{1,0:T(8,128)S(1)}, u32[]{:S(2)}, u32[]{:S(2)}) collective-permute-start(f32[8,512]{1,0:T(8,128)} %loads_hbm.1), channel_id=1, source_target_pairs={{0,1},{1,2},{2,3},{3,4},{4,5},{5,6},{6,7},{7,8},{8,9},{9,10},{10,1... | collective-permute-start | bytes 49160 | tf_op jit(solution)/shard_map/ppermute | solution.py:256
  7.9 3.9 %collective-permute-start.5 = (f32[65,8,128]{2,1,0:T(8,128)S(1)}, f32[65,8,128]{2,1,0:T(8,128)S(1)}, u32[]{:S(2)}, u32[]{:S(2)}) collective-permute-start(f32[65,8,128]{2,1,0:T(8,128)S(1)} %bitcast.9), channel_id=1, source_target_pairs={{0,1},{1,0},{2,3},{3,2},{4,5},{5,4},{6,7},{7,6},{8,9},{9,8},{10,11... | collective-permute-start | bytes 798728 | tf_op jit(solution)/shard_map/ppermute | solution.py:253
  10.6 2.8 %collective-permute-start.1 = (f32[64,8,128]{2,1,0:T(8,128)S(1)}, f32[64,8,128]{2,1,0:T(8,128)S(1)}, u32[]{:S(2)}, u32[]{:S(2)}) collective-permute-start(f32[64,8,128]{2,1,0:T(8,128)S(1)} %bitcast.10), channel_id=1, source_target_pairs={{0,1},{1,0},{2,3},{3,2},{4,5},{5,4},{6,7},{7,6},{8,9},{9,8},{10,11... | collective-permute-start | bytes 786440 | tf_op jit(solution)/shard_map/ppermute | solution.py:253
  11.8 5.1 %collective-permute-start.6 = (f32[33,8,128]{2,1,0:T(8,128)S(1)}, f32[33,8,128]{2,1,0:T(8,128)S(1)}, u32[]{:S(2)}, u32[]{:S(2)}) collective-permute-start(f32[33,8,128]{2,1,0:T(8,128)S(1)} %get-tuple-element.57), channel_id=1, source_target_pairs={{0,2},{1,5},{2,0},{3,7},{4,6},{5,1},{6,4},{7,3},{8,10},{9,13},{10,... | collective-permute-start | bytes 405512 | tf_op jit(solution)/shard_map/ppermute | solution.py:253
  13.4 5.1 %collective-permute-start.2 = (f32[32,8,128]{2,1,0:T(8,128)S(1)}, f32[32,8,128]{2,1,0:T(8,128)S(1)}, u32[]{:S(2)}, u32[]{:S(2)}) collective-permute-start(f32[32,8,128]{2,1,0:T(8,128)S(1)} %get-tuple-element.51), channel_id=1, source_target_pairs={{0,2},{1,5},{2,0},{3,7},{4,6},{5,1},{6,4},{7,3},{8,10},{9,13},{10,... | collective-permute-start | bytes 393224 | tf_op jit(solution)/shard_map/ppermute | solution.py:253
  15.6 15.5 %copy-start = (f32[256,8,128]{2,1,0:T(8,128)S(1)}, f32[256,8,128]{2,1,0:T(8,128)}, u32[]{:S(2)}) copy-start(f32[256,8,128]{2,1,0:T(8,128)} %motifs_ref.3) | copy-start | bytes 3145732
  16.9 6.3 %collective-permute-start.7 = (f32[17,8,128]{2,1,0:T(8,128)S(1)}, f32[17,8,128]{2,1,0:T(8,128)S(1)}, u32[]{:S(2)}, u32[]{:S(2)}) collective-permute-start(f32[17,8,128]{2,1,0:T(8,128)S(1)} %get-tuple-element.64), channel_id=1, source_target_pairs={{0,4},{1,3},{2,6},{3,1},{4,0},{5,7},{6,2},{7,5},{8,12},{9,11},{10,... | collective-permute-start | bytes 208904 | tf_op jit(solution)/shard_map/ppermute | solution.py:253
  18.6 7.3 %collective-permute-start.3 = (f32[16,8,128]{2,1,0:T(8,128)S(1)}, f32[16,8,128]{2,1,0:T(8,128)S(1)}, u32[]{:S(2)}, u32[]{:S(2)}) collective-permute-start(f32[16,8,128]{2,1,0:T(8,128)S(1)} %get-tuple-element.53), channel_id=1, source_target_pairs={{0,4},{1,3},{2,6},{3,1},{4,0},{5,7},{6,2},{7,5},{8,12},{9,11},{10,... | collective-permute-start | bytes 196616 | tf_op jit(solution)/shard_map/ppermute | solution.py:253
  20.1 3.0 %collective-permute-start.8 = (f32[8,128]{1,0:T(8,128)S(1)}, f32[8,128]{1,0:T(8,128)S(1)}, u32[]{:S(2)}, u32[]{:S(2)}) collective-permute-start(f32[8,128]{1,0:T(8,128)S(1)} %get-tuple-element.66), channel_id=1, source_target_pairs={{1,0},{2,1},{3,2},{4,3},{5,4},{6,5},{7,6},{8,7},{9,8},{10,9},{11,1... | collective-permute-start | bytes 12296 | tf_op jit(solution)/shard_map/ppermute | solution.py:303
  23.2 7.9 %collective-permute-start.9 = (f32[17,8,128]{2,1,0:T(8,128)S(1)}, f32[17,8,128]{2,1,0:T(8,128)S(1)}, u32[]{:S(2)}, u32[]{:S(2)}) collective-permute-start(f32[17,8,128]{2,1,0:T(8,128)S(1)} %pair_kernel.3.mine_ref), channel_id=1, source_target_pairs={{0,8},{1,9},{2,10},{3,11},{4,12},{5,13},{6,14},{7,15},{8,0},{9,1},... | collective-permute-start | bytes 208904 | tf_op jit(solution)/shard_map/ppermute | solution.py:253
  25.9 7.4 %collective-permute-start.4 = (f32[16,8,128]{2,1,0:T(8,128)S(1)}, f32[16,8,128]{2,1,0:T(8,128)S(1)}, u32[]{:S(2)}, u32[]{:S(2)}) collective-permute-start(f32[16,8,128]{2,1,0:T(8,128)S(1)} %pair_kernel.2.mine_ref), channel_id=1, source_target_pairs={{0,8},{1,9},{2,10},{3,11},{4,12},{5,13},{6,14},{7,15},{8,0},{9,1},... | collective-permute-start | bytes 196616 | tf_op jit(solution)/shard_map/ppermute | solution.py:253
  26.3 3.9 %collective-permute-start.10 = (f32[8,640]{1,0:T(8,128)S(1)}, f32[8,640]{1,0:T(8,128)S(1)}, u32[]{:S(2)}, u32[]{:S(2)}) collective-permute-start(f32[8,640]{1,0:T(8,128)S(1)} %halo_kernel.1.mine_ref), channel_id=1, source_target_pairs={{0,16},{16,0},{1,17},{17,1},{2,18},{18,2},{3,19},{19,3},{4,20},{20... | collective-permute-start | bytes 61448 | tf_op jit(solution)/shard_map/ppermute | solution.py:313
  31.1 4.3 %collective-permute-start.14 = (f32[16,8,128]{2,1,0:T(8,128)S(1)}, f32[16,8,128]{2,1,0:T(8,128)S(1)}, u32[]{:S(2)}, u32[]{:S(2)}) collective-permute-start(f32[16,8,128]{2,1,0:T(8,128)S(1)} %get-tuple-element.72.mine_ref), channel_id=1, source_target_pairs={{0,4},{1,3},{2,6},{3,1},{4,0},{5,7},{6,2},{7,5},{8,12},{9,11},{10,... | collective-permute-start | bytes 196616 | tf_op jit(solution)/shard_map/ppermute | solution.py:253
  33.2 4.8 %collective-permute-start.11 = (f32[16,8,128]{2,1,0:T(8,128)S(1)}, f32[16,8,128]{2,1,0:T(8,128)S(1)}, u32[]{:S(2)}, u32[]{:S(2)}) collective-permute-start(f32[16,8,128]{2,1,0:T(8,128)S(1)} %update_kernel.3.mine_ref), channel_id=1, source_target_pairs={{0,4},{1,3},{2,6},{3,1},{4,0},{5,7},{6,2},{7,5},{8,12},{9,11},{10,... | collective-permute-start | bytes 196616 | tf_op jit(solution)/shard_map/ppermute | solution.py:253
  35.5 5.6 %collective-permute-start.15 = (f32[32,8,128]{2,1,0:T(8,128)S(1)}, f32[32,8,128]{2,1,0:T(8,128)S(1)}, u32[]{:S(2)}, u32[]{:S(2)}) collective-permute-start(f32[32,8,128]{2,1,0:T(8,128)S(1)} %join_kernel.6.mine_ref), channel_id=1, source_target_pairs={{0,2},{1,5},{2,0},{3,7},{4,6},{5,1},{6,4},{7,3},{8,10},{9,13},{10,... | collective-permute-start | bytes 393224 | tf_op jit(solution)/shard_map/ppermute | solution.py:253
  38.1 5.0 %collective-permute-start.12 = (f32[32,8,128]{2,1,0:T(8,128)S(1)}, f32[32,8,128]{2,1,0:T(8,128)S(1)}, u32[]{:S(2)}, u32[]{:S(2)}) collective-permute-start(f32[32,8,128]{2,1,0:T(8,128)S(1)} %join_kernel.4.mine_ref), channel_id=1, source_target_pairs={{0,2},{1,5},{2,0},{3,7},{4,6},{5,1},{6,4},{7,3},{8,10},{9,13},{10,... | collective-permute-start | bytes 393224 | tf_op jit(solution)/shard_map/ppermute | solution.py:253
  41.0 2.9 %collective-permute-start.16 = (f32[64,8,128]{2,1,0:T(8,128)S(1)}, f32[64,8,128]{2,1,0:T(8,128)S(1)}, u32[]{:S(2)}, u32[]{:S(2)}) collective-permute-start(f32[64,8,128]{2,1,0:T(8,128)S(1)} %join_kernel.7.refs_0_), channel_id=1, source_target_pairs={{0,1},{1,0},{2,3},{3,2},{4,5},{5,4},{6,7},{7,6},{8,9},{9,8},{10,11... | collective-permute-start | bytes 786440 | tf_op jit(solution)/shard_map/ppermute | solution.py:253
  43.1 1.6 %collective-permute-start.13 = (f32[64,8,128]{2,1,0:T(8,128)S(1)}, f32[64,8,128]{2,1,0:T(8,128)S(1)}, u32[]{:S(2)}, u32[]{:S(2)}) collective-permute-start(f32[64,8,128]{2,1,0:T(8,128)S(1)} %join_kernel.5.refs_1_), channel_id=1, source_target_pairs={{0,1},{1,0},{2,3},{3,2},{4,5},{5,4},{6,7},{7,6},{8,9},{9,8},{10,11... | collective-permute-start | bytes 786440 | tf_op jit(solution)/shard_map/ppermute | solution.py:253

commit v3 on v2

v3 whole, which is shorter than its diff:
```python
import functools
import math

import jax
import jax.numpy as jnp
from jax import lax
from jax.experimental import pallas as pl
from jax.experimental.pallas import tpu as pltpu
from jax.sharding import PartitionSpec as P

F32, BF16 = jnp.float32, jnp.bfloat16
NN = (((1,), (0,)), ((), ()))
NT = (((1,), (1,)), ((), ()))
TN = (((0,), (0,)), ((), ()))
MIB = 1024 * 1024
BODY_LIMIT = 20
ONES = 16
LOADS_AFTER = 0
PARTS = (1, 1)


def split(x):
    high = x.astype(BF16)
    return high, (x - high.astype(F32)).astype(BF16)


def dot3(ah, al, bh, bl, dims):
    def dot(a, b):
        return lax.dot_general(a, b, dims, preferred_element_type=F32)

    return dot(ah, bh) + (dot(ah, bl) + dot(al, bh))


def toeplitz(row, lags):
    return pltpu.roll(jnp.broadcast_to(row, (lags, row.shape[1])), 0, 1, stride=1, stride_axis=0)


def place(me, step, steps):
    first, second = (order(core, steps)[step] for core in range(2))
    return jnp.where(me & 1 == 0, (me >> first) & 1, (me >> second) & 1)


def order(core, steps):
    return [0, 2, 1, *range(3, steps)] if core else list(range(steps))


class Chain:
    def __init__(self, me):
        self.me, self.token = me, None

    def __call__(self, kernel, out_shapes, *args, limit=4, spaces=None, outs=None, scratch=(), aliases=None, flops=0,
                 order=True):
        spaces = spaces or [pltpu.VMEM] * len(args)
        outs = outs or [pltpu.VMEM] * len(out_shapes)
        aliases, tokens = dict(aliases or {}), []
        if order and self.token is not None:
            tokens = [self.token]
            aliases[len(args) + 1] = len(out_shapes)
        given, results = 1 + len(args), len(out_shapes)

        def run(*refs):
            inputs, rest = refs[:given], refs[given + len(tokens):]
            kernel(*inputs, *rest[:results], *rest[results + len(tokens):])

        made = pl.pallas_call(
            run,
            out_shape=[*out_shapes, *(jax.ShapeDtypeStruct(t.shape, t.dtype) for t in tokens)],
            in_specs=[pl.BlockSpec(memory_space=space) for space in [pltpu.SMEM, *spaces, *[pltpu.VMEM] * len(tokens)]],
            out_specs=[pl.BlockSpec(memory_space=space) for space in [*outs, *[pltpu.VMEM] * len(tokens)]],
            scratch_shapes=list(scratch),
            input_output_aliases=aliases,
            compiler_params=pltpu.CompilerParams(vmem_limit_bytes=int(limit * MIB)),
            cost_estimate=pl.CostEstimate(flops=flops, bytes_accessed=0, transcendentals=0),
            name=getattr(kernel, "func", kernel).__name__,
        )(self.me, *args, *tokens)
        if tokens:
            self.token = made[-1]
        return made[:results]


def body_kernel(me_ref, counts_hbm, motifs_hbm, loads_hbm, mh_ref, ml_ref, rh_ref, rl_ref, numer_ref, counts_ref,
                loads_ref, total_ref, motifs_ref, rest_ref, th, tl, sems):
    rows, frames = counts_hbm.shape
    motif_count = loads_ref.shape[0]
    lags = counts_ref.shape[1]
    copies = [
        pltpu.make_async_copy(loads_hbm, loads_ref, sems.at[0]),
        pltpu.make_async_copy(motifs_hbm, motifs_ref, sems.at[1]),
        pltpu.make_async_copy(counts_hbm.at[:, pl.ds(lags, frames - lags)], rest_ref, sems.at[2]),
        pltpu.make_async_copy(counts_hbm.at[:, pl.ds(0, lags)], counts_ref, sems.at[3]),
    ]
    for copy in copies:
        copy.start()
    copies[0].wait()
    for k in range(motif_count):
        at = pl.ds(k * lags, lags)
        th[at, :], tl[at, :] = split(toeplitz(loads_ref[pl.ds(k, 1), :], lags)[:, lags:])
    copies[1].wait()
    for k in range(motif_count):
        at = pl.ds(k * lags, lags)
        mh_ref[:, at], ml_ref[:, at] = split(motifs_ref[pl.ds(k, rows, stride=motif_count), :])
    estimate = dot3(mh_ref[...], ml_ref[...], th[...], tl[...], NN)
    copies[2].wait()
    rh_ref[...], rl_ref[...] = split(rest_ref[...] / estimate)
    ones = jnp.ones((ONES, frames - lags), BF16)
    xh = jnp.concatenate([rh_ref[...], ones], axis=0)
    xl = jnp.concatenate([rl_ref[...], jnp.zeros_like(ones)], axis=0)
    for k in range(0, motif_count, 2):
        at = pl.ds(k * lags, 2 * lags)
        numer_ref[:, at] = dot3(xh, xl, th[at, :], tl[at, :], NT)
    total_ref[...] = jnp.sum(motifs_ref[...].reshape(rows, motif_count, lags), axis=0)
    copies[3].wait()


def numer_rows(numer, motif_count, out_ref, count):
    lags = out_ref.shape[-1]
    for k in range(motif_count):
        out_ref[pl.ds(k, count, stride=motif_count), :] = numer[:count, k * lags:(k + 1) * lags]


def blocks(sizes, core):
    at = [sum(sizes[:c]) for c in range(len(sizes))]
    step = math.gcd(*sizes) // 2
    return [pl.ds(pl.multiple_of(first + core * (size // 2), step), size // 2) for first, size in zip(at, sizes)]


def slabs(numer, sizes):
    return [numer[sum(sizes[:c]) // 2:sum(sizes[:c + 1]) // 2] for c in range(len(sizes))]


def head_kernel(sizes, me_ref, tail_ref, counts_ref, loads_ref, mh_ref, ml_ref, numer_ref, *refs):
    *send_refs, fh_ref, fl_ref, hh_ref, hl_ref, denom_ref = refs
    rows, lags = counts_ref.shape
    motif_count, frames = loads_ref.shape
    for k in range(motif_count):
        at = pl.ds(k * lags, lags)
        row = jnp.concatenate([tail_ref[pl.ds(k, 1), frames - lags:], loads_ref[pl.ds(k, 1), :lags]], axis=1)
        hh_ref[at, :], hl_ref[at, :] = split(toeplitz(row, lags)[:, lags:])
    estimate = dot3(mh_ref[...], ml_ref[...], hh_ref[...], hl_ref[...], NN)
    fh_ref[...], fl_ref[...] = split(counts_ref[...] / estimate)
    away = blocks(sizes, 1 - (me_ref[0] & 1))
    ones = jnp.ones((ONES, lags), BF16)
    xh = jnp.concatenate([*(fh_ref[at, :] for at in away), ones], axis=0)
    xl = jnp.concatenate([*(fl_ref[at, :] for at in away), jnp.zeros_like(ones)], axis=0)
    for k in range(0, motif_count, 2):
        at = pl.ds(k * lags, 2 * lags)
        numer = dot3(xh, xl, hh_ref[at, :], hl_ref[at, :], NT)
        for j in range(2):
            there, here = pl.ds((k + j) * lags, lags), slice(j * lags, (j + 1) * lags)
            for ref, at, slab in zip(send_refs, away, slabs(numer, sizes)):
                ref[pl.ds(k + j, at.size, stride=motif_count), :] = slab[:, here] + numer_ref[at, there]
            denom = numer[rows // 2:rows // 2 + 1, here] + numer_ref[pl.ds(rows, 1), there]
            send_refs[0][pl.ds(away[0].size * motif_count + k + j, 1), :] = denom
            denom_ref[pl.ds(k + j, 1), :] = denom


def home_kernel(sizes, me_ref, fh_ref, fl_ref, hh_ref, hl_ref, denom_ref, numer_ref, *keep_refs):
    rows, lags = fh_ref.shape
    motif_count = denom_ref.shape[0]
    home = blocks(sizes, me_ref[0] & 1)
    xh = jnp.concatenate([fh_ref[at, :] for at in home], axis=0)
    xl = jnp.concatenate([fl_ref[at, :] for at in home], axis=0)
    for k in range(0, motif_count, 2):
        at = pl.ds(k * lags, 2 * lags)
        numer = dot3(xh, xl, hh_ref[at, :], hl_ref[at, :], NT)
        for j in range(2):
            there, here = pl.ds((k + j) * lags, lags), slice(j * lags, (j + 1) * lags)
            for ref, at, slab in zip(keep_refs, home, slabs(numer, sizes)):
                ref[pl.ds(k + j, at.size, stride=motif_count), :] = slab[:, here] + numer_ref[at, there]
    keep_refs[0][pl.ds(home[0].size * motif_count, motif_count), :] = denom_ref[...]


def fold_kernel(step, steps, half, me_ref, mine_ref, got_ref, send_ref, keep_ref):
    bit = place(me_ref[0], step, steps)
    for out, part in ((send_ref, 1 - bit), (keep_ref, bit)):
        at = pl.ds(part * half, half)
        out[:half] = mine_ref[at] + got_ref[at]
        if out.shape[0] > half:
            out[half:] = mine_ref[2 * half:] + got_ref[2 * half:]


def pair_kernel(me_ref, mine_ref, got_ref, out_ref):
    out_ref[...] = mine_ref[...] + got_ref[...]


def pair_row_kernel(me_ref, mine_ref, got_ref, row_ref, out_ref):
    rows = mine_ref.shape[0]
    out_ref[:rows] = mine_ref[...] + got_ref[...]
    out_ref[rows] = row_ref[...]


def carry(me, bit, mine, got):
    return jnp.where(me & ((1 << bit) - 1) == 0, got, mine)


def carry_bit(me, step, steps):
    first, second = (order(core, steps)[step] for core in range(2))
    return jnp.where(me & 1 == 0, first, second)


def update_kernel(first, size, steps, me_ref, mine_ref, got_ref, denom_ref, motifs_ref, out_ref, *denom_out):
    rows, at, me = size >> (steps - 1), first, me_ref[0]
    for step in range(steps - 1):
        size //= 2
        at = at + place(me, step, steps) * size
    numer = mine_ref[:rows] + got_ref[:rows]
    if denom_out:
        denom = mine_ref[rows] + got_ref[rows]
        denom_out[0][...] = denom
        out_ref[rows] = carry(me, steps - 1, mine_ref[rows + 1], got_ref[rows + 1])
    else:
        denom = denom_ref[...]
    out_ref[:rows] = motifs_ref[pl.ds(at, rows)] * numer / denom[None]


def join_kernel(step, steps, half, me_ref, mine_ref, got_ref, out_ref):
    me = me_ref[0]
    bit = place(me, step, steps)
    out_ref[pl.ds(bit * half, half)] = mine_ref[:half]
    out_ref[pl.ds((1 - bit) * half, half)] = got_ref[:half]
    if mine_ref.shape[0] > half:
        out_ref[2 * half] = carry(me, carry_bit(me, step, steps), mine_ref[half], got_ref[half])


def store_kernel(parts, row_at, ranks, me_ref, *refs):
    refs, sems = refs[:-1], refs[-1]
    core = me_ref[0] & 1
    copies = []
    out_hbm = refs[-1] if row_at is None else refs[-3]
    for i, ((at, rows, own), block) in enumerate(zip(parts, refs)):
        at = at + (core if own else 1 - core) * rows
        copies.append(pltpu.make_async_copy(block.at[pl.ds(0, rows)], out_hbm.at[pl.ds(at, rows)], sems.at[i]))
    for copy in copies:
        copy.start()
    if row_at is not None:
        block, (numer_ref, scale_ref) = refs[0], refs[len(parts):len(parts) + 2]
        loads_hbm, loads_ref = refs[-2:]
        frames, lags = numer_ref.shape[1], block.shape[-1]
        rest = frames - lags
        ahead = jnp.where(me_ref[0] == ranks - 1, 0.0, block[row_at])
        loads_ref[:, :rest] = scale_ref[:, :rest] * numer_ref[:, :rest]
        loads_ref[:, rest:] = scale_ref[:, rest:] * (numer_ref[:, rest:] + ahead)
        copies.append(pltpu.make_async_copy(loads_ref, loads_hbm, sems.at[len(parts)]))
        copies[-1].start()
    for copy in copies:
        copy.wait()


def lagged_kernel(me_ref, mh_ref, ml_ref, fh_ref, fl_ref, rh_ref, rl_ref, total_ref, out_ref, ph, pw):
    motif_count, lags = total_ref.shape
    frames = out_ref.shape[1] - 2 * lags
    width = frames + lags
    down = lax.broadcasted_iota(jnp.int32, (lags, lags), 0)
    across = lax.broadcasted_iota(jnp.int32, (lags, lags), 1)
    flip = (down + across == lags - 1).astype(BF16)
    xh = jnp.concatenate([fh_ref[...], rh_ref[...]], axis=1)
    xl = jnp.concatenate([fl_ref[...], rl_ref[...]], axis=1)
    for k in range(motif_count):
        at = pl.ds(k * lags, lags)
        for ref, out in ((mh_ref, ph), (ml_ref, pw)):
            out[:, at] = lax.dot_general(ref[:, at], flip, NN, preferred_element_type=F32).astype(BF16)
    for k in range(0, motif_count, 4):
        at = pl.ds(k * lags, 4 * lags)
        lagged = dot3(ph[:, at], pw[:, at], xh, xl, TN)
        for j in range(4):
            wide = jnp.concatenate([jnp.zeros((lags, lags), F32), lagged[j * lags:(j + 1) * lags]], axis=1)
            skewed = pltpu.roll(wide, width - (lags - 1), 1, stride=1, stride_axis=0)
            numer = jnp.sum(skewed, axis=0, keepdims=True)
            out_ref[pl.ds(k + j, 1), :frames] = numer[:, lags:]
            out_ref[pl.ds(k + j, 1), frames:width] = numer[:, :lags]
    out_ref[:, width:] = total_ref[...]


def loads_kernel(ranks, me_ref, mine_ref, got_ref, loads_ref, ahead_ref, numer_ref, scale_ref):
    frames, lags = loads_ref.shape[1], ahead_ref.shape[1]
    both = mine_ref[...] + got_ref[...]
    numer_ref[...] = both[:, :frames]
    ahead_ref[...] = both[:, frames:frames + lags]
    left = (ranks - me_ref[0]) * frames
    lag = lax.broadcasted_iota(jnp.int32, (lags, frames), 0)
    frame = lax.broadcasted_iota(jnp.int32, (lags, frames), 1)
    valid = (lag + frame < left).astype(F32)
    total = both[:, frames + lags:]
    denom = lax.dot_general(total, valid, NN, precision=lax.Precision.HIGHEST, preferred_element_type=F32)
    scale_ref[...] = loads_ref[...] / denom


def body(counts, motifs, loadings):
    rows, motif_count, lags = motifs.shape
    frames = loadings.shape[1]
    ranks, groups = lax.axis_size("tm"), lax.axis_size("neur")
    steps, flips = ranks.bit_length() - 1, groups.bit_length() - 1
    assert ranks == 1 << steps and groups == 1 << flips and steps >= 3

    def shape(*dims, dtype=F32):
        return jax.ShapeDtypeStruct(dims, dtype)

    def swap(x, step):
        return lax.ppermute(x, "tm", [(i, i ^ (1 << order(i & 1, steps)[step])) for i in range(ranks)])

    call = Chain(lax.axis_index("tm").astype(jnp.int32).reshape(1))
    tail = lax.ppermute(loadings, "tm", [(i, i + 1) for i in range(ranks - 1)])
    flat = motifs.reshape(rows * motif_count, lags)
    depth, rest = motif_count * lags, frames - lags
    macs = rows * depth * frames * 3
    mh, ml, rh, rl, numer, head_counts, own_loads, total = call(
        body_kernel,
        [shape(rows, depth, dtype=BF16)] * 2 + [shape(rows, rest, dtype=BF16)] * 2
        + [shape(rows + ONES, depth), shape(rows, lags), shape(motif_count, frames), shape(motif_count, lags)],
        *(pltpu.with_memory_space_constraint(x, pltpu.HBM) for x in (counts, flat, loadings)),
        spaces=[pltpu.HBM] * 3,
        scratch=[pltpu.VMEM((rows * motif_count, lags), F32), pltpu.VMEM((rows, rest), F32)]
        + [pltpu.VMEM((depth, rest), BF16)] * 2 + [pltpu.SemaphoreType.DMA((4,))],
        limit=BODY_LIMIT, flops=4 * macs,
    )
    sizes = [rows * share // sum(PARTS) for share in PARTS]
    assert sum(sizes) == rows and all(size % (ranks // 2) == 0 for size in sizes)
    chunks = range(len(sizes))
    half = [size // 2 for size in sizes]
    extra = [int(c == 0) for c in chunks]
    parts = [shape((half[c] + extra[c]) * motif_count, lags) for c in chunks]
    *send, fh, fl, hh, hl, denom = call(
        functools.partial(head_kernel, sizes),
        parts + [shape(rows, lags, dtype=BF16)] * 2 + [shape(depth, lags, dtype=BF16)] * 2 + [shape(motif_count, lags)],
        tail, head_counts, own_loads, mh, ml, numer, limit=6,
    )

    call.token = denom

    def cube(x):
        return x.reshape(-1, motif_count, lags)

    def cubes(count):
        return shape(count, motif_count, lags)

    got = [swap(cube(x), 0) for x in send]
    keep = call(
        functools.partial(home_kernel, sizes), parts, fh, fl, hh, hl, denom, numer, limit=6, flops=macs // 4
    )
    keep = [cube(x) for x in keep]
    (part,) = call(
        lagged_kernel, [shape(motif_count, frames + 2 * lags)], mh, ml, fh, fl, rh, rl, total,
        scratch=[pltpu.VMEM((rows, depth), BF16)] * 2, limit=8, flops=2 * macs,
    )
    other = jnp.zeros_like(part)
    for flip in range(flips):
        if flip:
            (part,) = call(pair_kernel, [part], part, other, order=False)
        other = lax.ppermute(part, "neur", [(i, i ^ (1 << flip)) for i in range(groups)])
    for step in range(1, steps - 1):
        for c in chunks:
            half[c] //= 2
            send[c], keep[c] = call(
                functools.partial(fold_kernel, step, steps, half[c]), [cubes(half[c] + extra[c])] * 2, keep[c], got[c]
            )
            got[c] = swap(send[c], step)
            if step == 2 and c == LOADS_AFTER:
                ahead, numer, scale = call(
                    functools.partial(loads_kernel, ranks), [shape(motif_count, lags)] + [shape(motif_count, frames)] * 2,
                    part, other, own_loads,
                )
    for c in chunks:
        if c == 0:
            (keep[c],) = call(pair_row_kernel, [cubes(half[c] + 2)], keep[c], got[c], ahead)
        else:
            (keep[c],) = call(pair_kernel, [cubes(half[c])], keep[c], got[c])
        got[c] = swap(keep[c], steps - 1)
    mine = [None for c in chunks]
    for c in chunks:
        mine[c], *more = call(
            functools.partial(update_kernel, sum(sizes[:c]), sizes[c], steps),
            [cubes(half[c] + extra[c])] + [shape(motif_count, lags)] * extra[c], keep[c], got[c], denom, motifs,
        )
        if more:
            denom = more[0]
        got[c] = swap(mine[c], steps - 2)
    out, new_loadings, waiting = None, None, []
    for step in range(steps - 2, 0, -1):
        for c in chunks:
            (mine[c],) = call(
                functools.partial(join_kernel, step, steps, half[c]), [cubes(2 * half[c] + extra[c])], mine[c], got[c]
            )
            half[c] *= 2
            got[c] = swap(mine[c], step - 1)
            if step == 1:
                waiting.append((sum(sizes[:c]), half[c], True, mine[c]))
                out, new_loadings = store(call, out, new_loadings, rows, waiting, numer, scale, ranks)
                waiting = [(sum(sizes[:c]), half[c], False, got[c])]
    out, new_loadings = store(call, out, new_loadings, rows, waiting, numer, scale, ranks)
    return out, new_loadings


def store(call, out, new_loadings, rows, waiting, numer, scale, ranks):
    waiting = sorted(waiting, key=lambda block: block[2])
    first, half, own, block = waiting[0]
    brings = first == 0 and not own
    given = [block for *_, block in waiting] + [numer, scale] * brings
    spaces = [pltpu.VMEM] * len(given)
    results = [jax.ShapeDtypeStruct((rows, *block.shape[1:]), F32)] + [jax.ShapeDtypeStruct(numer.shape, F32)] * brings
    aliases = {}
    if out is not None:
        given.append(out)
        spaces.append(pltpu.HBM)
        aliases = {len(given): 0}
    out, *more = call(
        functools.partial(store_kernel, [place[:3] for place in waiting], half if brings else None, ranks),
        results, *given, spaces=spaces, outs=[pltpu.HBM] * len(results), aliases=aliases,
        scratch=[pltpu.VMEM(numer.shape, F32)] * brings + [pltpu.SemaphoreType.DMA((3,))],
    )
    return out, more[0] if brings else new_loadings


def solution(mesh):
    in_specs = (P("neur", "tm"), P("neur", None, None), P(None, "tm"))
    out_specs = (P("neur", None, None), P(None, "tm"))
    return jax.shard_map(body, mesh=mesh, in_specs=in_specs, out_specs=out_specs, check_vma=False)
```

time: 45.8 us -> 43.9 us (0.959)
  waiting for transfers between devices: 13.5 us -> 12.1 us
  Pallas kernels: 10.2 us -> 9.64 us
    ppermute x14, waiting for transfers between devices: 9.3 us -> 12.1 us  [swap(): lax.ppermute(x, 'tm', [(i, i ^ 1 << order(i & 1, steps)[step]) for i in r...]
    ppermute x1, waiting for transfers between devices: 2.44 us -> 0.01 us  [body(): lax.ppermute(part, 'neur', [(i, i ^ 1 << flip) for i in range(groups)])]
    ppermute x1 -> x0, waiting for transfers between devices: 1.76 us -> none  [body(): ahead = lax.ppermute(ahead, 'tm', [(i, i - 1) for i in range(1, ranks)])]
    ppermute x14, starting transfers between devices: 15.9 us -> 17.3 us  [swap(): lax.ppermute(x, 'tm', [(i, i ^ 1 << order(i & 1, steps)[step]) for i in r...]
    ppermute x1 -> x0, starting transfers between devices: 1.28 us -> none  [body(): ahead = lax.ppermute(ahead, 'tm', [(i, i - 1) for i in range(1, ranks)])]
    pallas_call x21 -> x20, Pallas kernels: 10.2 us -> 9.64 us  [__call__(): pl.pallas_call(run, out_shape=[*out_shapes, *(jax.ShapeDtypeStruct(t.shap...]
  transfers between devices with their start and end apart: 17 -> 16, of which waited for: 8 -> 8; matrix products, arithmetic and copies ran while one was open for 0% -> 0% of each run, Pallas kernels for 18% -> 17%
where the time goes in v3:
time: 43.9 us; the launch traced here: 43.7 us
  starting transfers between devices  21.2 us (48%)
  waiting for transfers between devices  12.1 us (28%)
  Pallas kernels  9.64 us (22%)
  between operations  0.8 us (2%)
    ppermute x14, starting transfers between devices, swap(): lax.ppermute(x, 'tm', [(i, i ^ 1 << order(i & 1, steps)[step]) for i in r...  17.3 us
    ppermute x14, waiting for transfers between devices, swap(): lax.ppermute(x, 'tm', [(i, i ^ 1 << order(i & 1, steps)[step]) for i in r...  12.1 us
    pallas_call x20, Pallas kernels, __call__(): pl.pallas_call(run, out_shape=[*out_shapes, *(jax.ShapeDtypeStruct(t.shap...  9.64 us
    ppermute x1, starting transfers between devices, body(): tail = lax.ppermute(loadings, 'tm', [(i, i + 1) for i in range(ranks - 1)])  2.36 us
    ppermute x1, starting transfers between devices, body(): lax.ppermute(part, 'neur', [(i, i ^ 1 << flip) for i in range(groups)])  1.51 us
  transfers between devices with their start and end apart: 16, of which 8 were waited for; matrix products, arithmetic and copies ran while one was open for 0% of the time, Pallas kernels for 17%

profile of v3, /device:TPU:0, one launch (start us, length us, event | category | flops | bytes accessed | tf_op | source)
XLA Modules:
  0.0 43.7 jit_solution(17631572156947934349)
XLA Ops:
  0.6 2.4 %collective-permute-start = (f32[8,512]{1,0:T(8,128)}, f32[8,512]{1,0:T(8,128)S(1)}, u32[]{:S(2)}, u32[]{:S(2)}) collective-permute-start(f32[8,512]{1,0:T(8,128)} %refs_3_.1), channel_id=1, source_target_pairs={{0,1},{1,2},{2,3},{3,4},{4,5},{5,6},{6,7},{7,8},{8,9},{9,10},{10,1... | collective-permute-start | bytes 49160 | tf_op jit(solution)/shard_map/ppermute | solution.py:302
  3.0 3.6 %body_kernel.1 = (bf16[256,1024]{1,0:T(8,128)(2,1)S(1)}, bf16[256,1024]{1,0:T(8,128)(2,1)S(1)}, bf16[256,384]{1,0:T(8,128)(2,1)S(1)}, bf16[256,384]{1,0:T(8,128)...) custom-call(s32[1]{0:T(128)} %bitcast.refs_0_, ...), custom_call_target="tpu_custom_call" | custom-call | flops 1610612736 | tf_op jit(solution)/shard_map/body_kernel/pallas_call | solution.py:65
  6.6 1.3 %head_kernel.1 = (f32[520,128]{1,0:T(8,128)S(1)}, f32[512,128]{1,0:T(8,128)S(1)}, bf16[256,128]{1,0:T(8,128)(2,1)S(1)}, bf16[256,128]{1,0:T(8,128)(2,1)S(1)}, bf...) custom-call(s32[1]{0:T(128)} %bitcast.refs_0_, ...), custom_call_target="tpu_custom_call" | custom-call | tf_op jit(solution)/shard_map/head_kernel/pallas_call | solution.py:65
  7.9 2.7 %collective-permute-start.2 = (f32[65,8,128]{2,1,0:T(8,128)S(1)}, f32[65,8,128]{2,1,0:T(8,128)S(1)}, u32[]{:S(2)}, u32[]{:S(2)}) collective-permute-start(f32[65,8,128]{2,1,0:T(8,128)S(1)} %bitcast.9), channel_id=1, source_target_pairs={{0,1},{1,0},{2,3},{3,2},{4,5},{5,4},{6,7},{7,6},{8,9},{9,8},{10,11... | collective-permute-start | bytes 798728 | tf_op jit(solution)/shard_map/ppermute | solution.py:299
  10.6 0.1 collective-permute-start.1
  10.7 0.4 home_kernel.1
  11.1 1.6 %lagged_kernel.1 = (f32[8,768]{1,0:T(8,128)S(1)}, f32[8,128]{1,0:T(8,128)S(1)}) custom-call(s32[1]{0:T(128)} %bitcast.refs_0_, bf16[256,1024]{1,0:T(8,128)(2,1)S(1)} %get-tuple-element.63.refs_4_.refs_1_, bf16[256,1024]{1,0:T(8,128)(2,1)S(1)} %get-tuple-element.64.refs_5_.refs_2_, ...), custom_call_target="tpu_custom_call", output_to_operand_aliasing={{1}: (8, {})} | custom-call | flops 805306368 | tf_op jit(solution)/shard_map/lagged_kernel/pallas_call | solution.py:65
  12.7 1.6 %collective-permute-start.5 = (f32[33,8,128]{2,1,0:T(8,128)S(1)}, f32[33,8,128]{2,1,0:T(8,128)S(1)}, u32[]{:S(2)}, u32[]{:S(2)}) collective-permute-start(f32[33,8,128]{2,1,0:T(8,128)S(1)} %get-tuple-element.85), channel_id=1, source_target_pairs={{0,2},{1,5},{2,0},{3,7},{4,6},{5,1},{6,4},{7,3},{8,10},{9,13},{10,... | collective-permute-start | bytes 405512 | tf_op jit(solution)/shard_map/ppermute | solution.py:299
  14.3 0.6 %collective-permute-start.3 = (f32[32,8,128]{2,1,0:T(8,128)S(1)}, f32[32,8,128]{2,1,0:T(8,128)S(1)}, u32[]{:S(2)}, u32[]{:S(2)}) collective-permute-start(f32[32,8,128]{2,1,0:T(8,128)S(1)} %get-tuple-element.82), channel_id=1, source_target_pairs={{0,2},{1,5},{2,0},{3,7},{4,6},{5,1},{6,4},{7,3},{8,10},{9,13},{10,... | collective-permute-start | bytes 393224 | tf_op jit(solution)/shard_map/ppermute | solution.py:299
  14.9 1.5 %collective-permute-start.4 = (f32[8,768]{1,0:T(8,128)S(1)}, f32[8,768]{1,0:T(8,128)S(1)}, u32[]{:S(2)}, u32[]{:S(2)}) collective-permute-start(f32[8,768]{1,0:T(8,128)S(1)} %get-tuple-element.83.refs_1_), channel_id=1, source_target_pairs={{0,16},{16,0},{1,17},{17,1},{2,18},{18,2},{3,19},{19,3},{4,20},{20... | collective-permute-start | bytes 73736 | tf_op jit(solution)/shard_map/ppermute | solution.py:349
  16.4 1.4 %collective-permute-done.5.refs_2_ = f32[33,8,128]{2,1,0:T(8,128)S(1)} collective-permute-done((f32[33,8,128]{2,1,0:T(8,128)S(1)}, f32[33,8,128]{2,1,0:T(8,128)S(1)}, u32[]{:S(2)}, u32[]{:S(2)}) %collective-permute-start.5) | collective-permute-done | bytes 135200 | tf_op jit(solution)/shard_map/ppermute | solution.py:299
  17.8 1.6 %collective-permute-start.7 = (f32[17,8,128]{2,1,0:T(8,128)S(1)}, f32[17,8,128]{2,1,0:T(8,128)S(1)}, u32[]{:S(2)}, u32[]{:S(2)}) collective-permute-start(f32[17,8,128]{2,1,0:T(8,128)S(1)} %get-tuple-element.92), channel_id=1, source_target_pairs={{0,4},{1,3},{2,6},{3,1},{4,0},{5,7},{6,2},{7,5},{8,12},{9,11},{10,... | collective-permute-start | bytes 208904 | tf_op jit(solution)/shard_map/ppermute | solution.py:299
  19.5 0.3 loads_kernel.1
  19.8 1.3 %collective-permute-start.6 = (f32[16,8,128]{2,1,0:T(8,128)S(1)}, f32[16,8,128]{2,1,0:T(8,128)S(1)}, u32[]{:S(2)}, u32[]{:S(2)}) collective-permute-start(f32[16,8,128]{2,1,0:T(8,128)S(1)} %get-tuple-element.90), channel_id=1, source_target_pairs={{0,4},{1,3},{2,6},{3,1},{4,0},{5,7},{6,2},{7,5},{8,12},{9,11},{10,... | collective-permute-start | bytes 196616 | tf_op jit(solution)/shard_map/ppermute | solution.py:299
  21.1 1.2 %collective-permute-done.7.refs_2_ = f32[17,8,128]{2,1,0:T(8,128)S(1)} collective-permute-done((f32[17,8,128]{2,1,0:T(8,128)S(1)}, f32[17,8,128]{2,1,0:T(8,128)S(1)}, u32[]{:S(2)}, u32[]{:S(2)}) %collective-permute-start.7) | collective-permute-done | bytes 69664 | tf_op jit(solution)/shard_map/ppermute | solution.py:299
  22.2 2.6 %collective-permute-start.9 = (f32[18,8,128]{2,1,0:T(8,128)S(1)}, f32[18,8,128]{2,1,0:T(8,128)S(1)}, u32[]{:S(2)}, u32[]{:S(2)}) collective-permute-start(f32[18,8,128]{2,1,0:T(8,128)S(1)} %get-tuple-element.97.refs_1_), channel_id=1, source_target_pairs={{0,8},{1,9},{2,10},{3,11},{4,12},{5,13},{6,14},{7,15},{8,0},{9,1},... | collective-permute-start | bytes 221192 | tf_op jit(solution)/shard_map/ppermute | solution.py:299
  24.9 2.5 %collective-permute-start.8 = (f32[16,8,128]{2,1,0:T(8,128)S(1)}, f32[16,8,128]{2,1,0:T(8,128)S(1)}, u32[]{:S(2)}, u32[]{:S(2)}) collective-permute-start(f32[16,8,128]{2,1,0:T(8,128)S(1)} %get-tuple-element.96.refs_1_), channel_id=1, source_target_pairs={{0,8},{1,9},{2,10},{3,11},{4,12},{5,13},{6,14},{7,15},{8,0},{9,1},... | collective-permute-start | bytes 196616 | tf_op jit(solution)/shard_map/ppermute | solution.py:299
  27.3 2.2 %collective-permute-done.9.refs_2_ = f32[18,8,128]{2,1,0:T(8,128)S(1)} collective-permute-done((f32[18,8,128]{2,1,0:T(8,128)S(1)}, f32[18,8,128]{2,1,0:T(8,128)S(1)}, u32[]{:S(2)}, u32[]{:S(2)}) %collective-permute-start.9) | collective-permute-done | bytes 73760 | tf_op jit(solution)/shard_map/ppermute | solution.py:299
  29.6 0.3 collective-permute-start.11
  29.9 0.4 collective-permute-done.8.refs_2_
  30.3 1.5 %collective-permute-start.10 = (f32[16,8,128]{2,1,0:T(8,128)S(1)}, f32[16,8,128]{2,1,0:T(8,128)S(1)}, u32[]{:S(2)}, u32[]{:S(2)}) collective-permute-start(f32[16,8,128]{2,1,0:T(8,128)S(1)} %get-tuple-element.101.refs_1_), channel_id=1, source_target_pairs={{0,4},{1,3},{2,6},{3,1},{4,0},{5,7},{6,2},{7,5},{8,12},{9,11},{10,... | collective-permute-start | bytes 196616 | tf_op jit(solution)/shard_map/ppermute | solution.py:299
  31.8 2.7 %collective-permute-done.11.refs_2_ = f32[17,8,128]{2,1,0:T(8,128)S(1)} collective-permute-done((f32[17,8,128]{2,1,0:T(8,128)S(1)}, f32[17,8,128]{2,1,0:T(8,128)S(1)}, u32[]{:S(2)}, u32[]{:S(2)}) %collective-permute-start.11) | collective-permute-done | bytes 69664 | tf_op jit(solution)/shard_map/ppermute | solution.py:299
  34.5 1.8 %collective-permute-start.13 = (f32[33,8,128]{2,1,0:T(8,128)S(1)}, f32[33,8,128]{2,1,0:T(8,128)S(1)}, u32[]{:S(2)}, u32[]{:S(2)}) collective-permute-start(f32[33,8,128]{2,1,0:T(8,128)S(1)} %get-tuple-element.106.refs_1_), channel_id=1, source_target_pairs={{0,2},{1,5},{2,0},{3,7},{4,6},{5,1},{6,4},{7,3},{8,10},{9,13},{10,... | collective-permute-start | bytes 405512 | tf_op jit(solution)/shard_map/ppermute | solution.py:299
  36.3 0.7 %collective-permute-start.12 = (f32[32,8,128]{2,1,0:T(8,128)S(1)}, f32[32,8,128]{2,1,0:T(8,128)S(1)}, u32[]{:S(2)}, u32[]{:S(2)}) collective-permute-start(f32[32,8,128]{2,1,0:T(8,128)S(1)} %get-tuple-element.105.refs_1_), channel_id=1, source_target_pairs={{0,2},{1,5},{2,0},{3,7},{4,6},{5,1},{6,4},{7,3},{8,10},{9,13},{10,... | collective-permute-start | bytes 393224 | tf_op jit(solution)/shard_map/ppermute | solution.py:299
  37.0 2.6 %collective-permute-done.13.refs_2_ = f32[33,8,128]{2,1,0:T(8,128)S(1)} collective-permute-done((f32[33,8,128]{2,1,0:T(8,128)S(1)}, f32[33,8,128]{2,1,0:T(8,128)S(1)}, u32[]{:S(2)}, u32[]{:S(2)}) %collective-permute-start.13) | collective-permute-done | bytes 135200 | tf_op jit(solution)/shard_map/ppermute | solution.py:299
  39.6 0.1 collective-permute-start.15
  39.7 0.7 %store_kernel.3 = (f32[256,8,128]{2,1,0:T(8,128)}, f32[8,128]{1,0:T(8,128)S(1)}) custom-call(s32[1]{0:T(128)} %bitcast.refs_0_, f32[65,8,128]{2,1,0:T(8,128)S(1)} %get-tuple-element.108.refs_1_, f32[8,128]{1,0:T(8,128)S(1)} %get-tuple-element.109.refs_2_), custom_call_target="tpu_custom_call", output_to_operand_aliasing={{1}: (2, {})} | custom-call | tf_op jit(solution)/shard_map/store_kernel/pallas_call | solution.py:65
  40.4 0.9 %collective-permute-done.12.refs_2_ = f32[32,8,128]{2,1,0:T(8,128)S(1)} collective-permute-done((f32[32,8,128]{2,1,0:T(8,128)S(1)}, f32[32,8,128]{2,1,0:T(8,128)S(1)}, u32[]{:S(2)}, u32[]{:S(2)}) %collective-permute-start.12) | collective-permute-done | bytes 131104 | tf_op jit(solution)/shard_map/ppermute | solution.py:299
  41.4 0.1 collective-permute-start.14
  41.4 0.8 %store_kernel.4 = (f32[256,8,128]{2,1,0:T(8,128)}, f32[8,512]{1,0:T(8,128)}, f32[8,128]{1,0:T(8,128)S(1)}) custom-call(s32[1]{0:T(128)} %bitcast.refs_0_, f32[65,8,128]{2,1,0:T(8,128)S(1)} %collective-permute-done.15.refs_1_, f32[64,8,128]{2,1,0:T(8,128)S(1)} %get-tuple-element.111.refs_2_, ...), custom_call_target="tpu_custom_call", output_to_operand_aliasing={{0}: (5, {}), {2}: (6, {})} | custom-call | tf_op jit(solution)/shard_map/store_kernel/pallas_call | solution.py:65
  42.3 0.7 %collective-permute-done.14.refs_1_ = f32[64,8,128]{2,1,0:T(8,128)S(1)} collective-permute-done((f32[64,8,128]{2,1,0:T(8,128)S(1)}, f32[64,8,128]{2,1,0:T(8,128)S(1)}, u32[]{:S(2)}, u32[]{:S(2)}) %collective-permute-start.14) | collective-permute-done | bytes 262176 | tf_op jit(solution)/shard_map/ppermute | solution.py:299
  43.0 0.7 %store_kernel.5 = (f32[256,8,128]{2,1,0:T(8,128)}, f32[8,128]{1,0:T(8,128)S(1)}) custom-call(s32[1]{0:T(128)} %bitcast.refs_0_, f32[64,8,128]{2,1,0:T(8,128)S(1)} %collective-permute-done.14.refs_1_, f32[256,8,128]{2,1,0:T(8,128)} %get-tuple-element.116.refs_2_, f32[8,128]{1,0:T(8,128)S(1)} %get-tuple-element.117.refs_3_), custom_call_target="tpu_custom_call", output_to_operand_aliasing={{0}: (2, {}), {1}: (3, {})} | custom-call | tf_op jit(solution)/shard_map/store_kernel/pallas_call | solution.py:65
  (23 shorter events, 0.3 us)
Async XLA Ops:
  0.6 6.0 %collective-permute-start = (f32[8,512]{1,0:T(8,128)}, f32[8,512]{1,0:T(8,128)S(1)}, u32[]{:S(2)}, u32[]{:S(2)}) collective-permute-start(f32[8,512]{1,0:T(8,128)} %refs_3_.1), channel_id=1, source_target_pairs={{0,1},{1,2},{2,3},{3,4},{4,5},{5,6},{6,7},{7,8},{8,9},{9,10},{10,1... | collective-permute-start | bytes 49160 | tf_op jit(solution)/shard_map/ppermute | solution.py:302
  7.9 4.8 %collective-permute-start.2 = (f32[65,8,128]{2,1,0:T(8,128)S(1)}, f32[65,8,128]{2,1,0:T(8,128)S(1)}, u32[]{:S(2)}, u32[]{:S(2)}) collective-permute-start(f32[65,8,128]{2,1,0:T(8,128)S(1)} %bitcast.9), channel_id=1, source_target_pairs={{0,1},{1,0},{2,3},{3,2},{4,5},{5,4},{6,7},{7,6},{8,9},{9,8},{10,11... | collective-permute-start | bytes 798728 | tf_op jit(solution)/shard_map/ppermute | solution.py:299
  10.6 3.7 %collective-permute-start.1 = (f32[64,8,128]{2,1,0:T(8,128)S(1)}, f32[64,8,128]{2,1,0:T(8,128)S(1)}, u32[]{:S(2)}, u32[]{:S(2)}) collective-permute-start(f32[64,8,128]{2,1,0:T(8,128)S(1)} %bitcast.10), channel_id=1, source_target_pairs={{0,1},{1,0},{2,3},{3,2},{4,5},{5,4},{6,7},{7,6},{8,9},{9,8},{10,11... | collective-permute-start | bytes 786440 | tf_op jit(solution)/shard_map/ppermute | solution.py:299
  12.7 16.9 %copy-start = (f32[256,8,128]{2,1,0:T(8,128)S(1)}, f32[256,8,128]{2,1,0:T(8,128)}, u32[]{:S(2)}) copy-start(f32[256,8,128]{2,1,0:T(8,128)} %refs_4_.3) | copy-start | bytes 3145732
  12.7 5.1 %collective-permute-start.5 = (f32[33,8,128]{2,1,0:T(8,128)S(1)}, f32[33,8,128]{2,1,0:T(8,128)S(1)}, u32[]{:S(2)}, u32[]{:S(2)}) collective-permute-start(f32[33,8,128]{2,1,0:T(8,128)S(1)} %get-tuple-element.85), channel_id=1, source_target_pairs={{0,2},{1,5},{2,0},{3,7},{4,6},{5,1},{6,4},{7,3},{8,10},{9,13},{10,... | collective-permute-start | bytes 405512 | tf_op jit(solution)/shard_map/ppermute | solution.py:299
  14.3 5.4 %collective-permute-start.3 = (f32[32,8,128]{2,1,0:T(8,128)S(1)}, f32[32,8,128]{2,1,0:T(8,128)S(1)}, u32[]{:S(2)}, u32[]{:S(2)}) collective-permute-start(f32[32,8,128]{2,1,0:T(8,128)S(1)} %get-tuple-element.82), channel_id=1, source_target_pairs={{0,2},{1,5},{2,0},{3,7},{4,6},{5,1},{6,4},{7,3},{8,10},{9,13},{10,... | collective-permute-start | bytes 393224 | tf_op jit(solution)/shard_map/ppermute | solution.py:299
  14.9 4.5 %collective-permute-start.4 = (f32[8,768]{1,0:T(8,128)S(1)}, f32[8,768]{1,0:T(8,128)S(1)}, u32[]{:S(2)}, u32[]{:S(2)}) collective-permute-start(f32[8,768]{1,0:T(8,128)S(1)} %get-tuple-element.83.refs_1_), channel_id=1, source_target_pairs={{0,16},{16,0},{1,17},{17,1},{2,18},{18,2},{3,19},{19,3},{4,20},{20... | collective-permute-start | bytes 73736 | tf_op jit(solution)/shard_map/ppermute | solution.py:349
  17.8 4.4 %collective-permute-start.7 = (f32[17,8,128]{2,1,0:T(8,128)S(1)}, f32[17,8,128]{2,1,0:T(8,128)S(1)}, u32[]{:S(2)}, u32[]{:S(2)}) collective-permute-start(f32[17,8,128]{2,1,0:T(8,128)S(1)} %get-tuple-element.92), channel_id=1, source_target_pairs={{0,4},{1,3},{2,6},{3,1},{4,0},{5,7},{6,2},{7,5},{8,12},{9,11},{10,... | collective-permute-start | bytes 208904 | tf_op jit(solution)/shard_map/ppermute | solution.py:299
  19.8 5.1 %collective-permute-start.6 = (f32[16,8,128]{2,1,0:T(8,128)S(1)}, f32[16,8,128]{2,1,0:T(8,128)S(1)}, u32[]{:S(2)}, u32[]{:S(2)}) collective-permute-start(f32[16,8,128]{2,1,0:T(8,128)S(1)} %get-tuple-element.90), channel_id=1, source_target_pairs={{0,4},{1,3},{2,6},{3,1},{4,0},{5,7},{6,2},{7,5},{8,12},{9,11},{10,... | collective-permute-start | bytes 196616 | tf_op jit(solution)/shard_map/ppermute | solution.py:299
  22.2 7.4 %collective-permute-start.9 = (f32[18,8,128]{2,1,0:T(8,128)S(1)}, f32[18,8,128]{2,1,0:T(8,128)S(1)}, u32[]{:S(2)}, u32[]{:S(2)}) collective-permute-start(f32[18,8,128]{2,1,0:T(8,128)S(1)} %get-tuple-element.97.refs_1_), channel_id=1, source_target_pairs={{0,8},{1,9},{2,10},{3,11},{4,12},{5,13},{6,14},{7,15},{8,0},{9,1},... | collective-permute-start | bytes 221192 | tf_op jit(solution)/shard_map/ppermute | solution.py:299
  24.9 5.4 %collective-permute-start.8 = (f32[16,8,128]{2,1,0:T(8,128)S(1)}, f32[16,8,128]{2,1,0:T(8,128)S(1)}, u32[]{:S(2)}, u32[]{:S(2)}) collective-permute-start(f32[16,8,128]{2,1,0:T(8,128)S(1)} %get-tuple-element.96.refs_1_), channel_id=1, source_target_pairs={{0,8},{1,9},{2,10},{3,11},{4,12},{5,13},{6,14},{7,15},{8,0},{9,1},... | collective-permute-start | bytes 196616 | tf_op jit(solution)/shard_map/ppermute | solution.py:299
  29.6 4.9 %collective-permute-start.11 = (f32[17,8,128]{2,1,0:T(8,128)S(1)}, f32[17,8,128]{2,1,0:T(8,128)S(1)}, u32[]{:S(2)}, u32[]{:S(2)}) collective-permute-start(f32[17,8,128]{2,1,0:T(8,128)S(1)} %get-tuple-element.102.refs_1_), channel_id=1, source_target_pairs={{0,4},{1,3},{2,6},{3,1},{4,0},{5,7},{6,2},{7,5},{8,12},{9,11},{10,... | collective-permute-start | bytes 208904 | tf_op jit(solution)/shard_map/ppermute | solution.py:299
  30.3 6.0 %collective-permute-start.10 = (f32[16,8,128]{2,1,0:T(8,128)S(1)}, f32[16,8,128]{2,1,0:T(8,128)S(1)}, u32[]{:S(2)}, u32[]{:S(2)}) collective-permute-start(f32[16,8,128]{2,1,0:T(8,128)S(1)} %get-tuple-element.101.refs_1_), channel_id=1, source_target_pairs={{0,4},{1,3},{2,6},{3,1},{4,0},{5,7},{6,2},{7,5},{8,12},{9,11},{10,... | collective-permute-start | bytes 196616 | tf_op jit(solution)/shard_map/ppermute | solution.py:299
  34.5 5.1 %collective-permute-start.13 = (f32[33,8,128]{2,1,0:T(8,128)S(1)}, f32[33,8,128]{2,1,0:T(8,128)S(1)}, u32[]{:S(2)}, u32[]{:S(2)}) collective-permute-start(f32[33,8,128]{2,1,0:T(8,128)S(1)} %get-tuple-element.106.refs_1_), channel_id=1, source_target_pairs={{0,2},{1,5},{2,0},{3,7},{4,6},{5,1},{6,4},{7,3},{8,10},{9,13},{10,... | collective-permute-start | bytes 405512 | tf_op jit(solution)/shard_map/ppermute | solution.py:299
  36.3 5.0 %collective-permute-start.12 = (f32[32,8,128]{2,1,0:T(8,128)S(1)}, f32[32,8,128]{2,1,0:T(8,128)S(1)}, u32[]{:S(2)}, u32[]{:S(2)}) collective-permute-start(f32[32,8,128]{2,1,0:T(8,128)S(1)} %get-tuple-element.105.refs_1_), channel_id=1, source_target_pairs={{0,2},{1,5},{2,0},{3,7},{4,6},{5,1},{6,4},{7,3},{8,10},{9,13},{10,... | collective-permute-start | bytes 393224 | tf_op jit(solution)/shard_map/ppermute | solution.py:299
  39.6 1.8 %collective-permute-start.15 = (f32[65,8,128]{2,1,0:T(8,128)S(1)}, f32[65,8,128]{2,1,0:T(8,128)S(1)}, u32[]{:S(2)}, u32[]{:S(2)}) collective-permute-start(f32[65,8,128]{2,1,0:T(8,128)S(1)} %get-tuple-element.108.refs_1_), channel_id=1, source_target_pairs={{0,1},{1,0},{2,3},{3,2},{4,5},{5,4},{6,7},{7,6},{8,9},{9,8},{10,11... | collective-permute-start | bytes 798728 | tf_op jit(solution)/shard_map/ppermute | solution.py:299
  41.4 1.6 %collective-permute-start.14 = (f32[64,8,128]{2,1,0:T(8,128)S(1)}, f32[64,8,128]{2,1,0:T(8,128)S(1)}, u32[]{:S(2)}, u32[]{:S(2)}) collective-permute-start(f32[64,8,128]{2,1,0:T(8,128)S(1)} %get-tuple-element.111.refs_2_), channel_id=1, source_target_pairs={{0,1},{1,0},{2,3},{3,2},{4,5},{5,4},{6,7},{7,6},{8,9},{9,8},{10,11... | collective-permute-start | bytes 786440 | tf_op jit(solution)/shard_map/ppermute | solution.py:299

commit v4 on v3

--- a/solution.py
+++ b/solution.py
@@ -134,7 +134,8 @@
     motif_count, frames = loads_ref.shape
     for k in range(motif_count):
         at = pl.ds(k * lags, lags)
-        row = jnp.concatenate([tail_ref[pl.ds(k, 1), frames - lags:], loads_ref[pl.ds(k, 1), :lags]], axis=1)
+        tail = jnp.where(me_ref[0] == 0, 0.0, tail_ref[pl.ds(k, 1), frames - lags:])
+        row = jnp.concatenate([tail, loads_ref[pl.ds(k, 1), :lags]], axis=1)
         hh_ref[at, :], hl_ref[at, :] = split(toeplitz(row, lags)[:, lags:])
     estimate = dot3(mh_ref[...], ml_ref[...], hh_ref[...], hl_ref[...], NN)
     fh_ref[...], fl_ref[...] = split(counts_ref[...] / estimate)
@@ -299,7 +300,7 @@
         return lax.ppermute(x, "tm", [(i, i ^ (1 << order(i & 1, steps)[step])) for i in range(ranks)])
 
     call = Chain(lax.axis_index("tm").astype(jnp.int32).reshape(1))
-    tail = lax.ppermute(loadings, "tm", [(i, i + 1) for i in range(ranks - 1)])
+    tail = lax.ppermute(loadings, "tm", [(i, (i + 1) % ranks) for i in range(ranks)])
     flat = motifs.reshape(rows * motif_count, lags)
     depth, rest = motif_count * lags, frames - lags
     macs = rows * depth * frames * 3

time: 43.9 us -> 42.5 us (0.968)
  starting transfers between devices: 21.2 us -> 15.3 us
  waiting for transfers between devices: 12.1 us -> 16.5 us
    ppermute x14, starting transfers between devices: 17.3 us -> 12.9 us  [swap(): lax.ppermute(x, 'tm', [(i, i ^ 1 << order(i & 1, steps)[step]) for i in r...]
    ppermute x1, waiting for transfers between devices: 0.01 us -> 3.05 us  [body(): lax.ppermute(loadings, 'tm', [(i, (i + 1) % ranks) for i in range(ranks)])]
    ppermute x1, starting transfers between devices: 2.36 us -> 0.5 us  [body(): lax.ppermute(loadings, 'tm', [(i, (i + 1) % ranks) for i in range(ranks)])]
    ppermute x14, waiting for transfers between devices: 12.1 us -> 13.4 us  [swap(): lax.ppermute(x, 'tm', [(i, i ^ 1 << order(i & 1, steps)[step]) for i in r...]
  transfers between devices with their start and end apart: 16 -> 16, of which waited for: 8 -> 11; matrix products, arithmetic and copies ran while one was open for 0% -> 0% of each run, Pallas kernels for 17% -> 18%
where the time goes in v4:
time: 42.5 us; the launch traced here: 42.3 us
  waiting for transfers between devices  16.5 us (39%)
  starting transfers between devices  15.3 us (36%)
  Pallas kernels  9.63 us (23%)
  between operations  0.78 us (2%)
    ppermute x14, waiting for transfers between devices, swap(): lax.ppermute(x, 'tm', [(i, i ^ 1 << order(i & 1, steps)[step]) for i in r...  13.4 us
    ppermute x14, starting transfers between devices, swap(): lax.ppermute(x, 'tm', [(i, i ^ 1 << order(i & 1, steps)[step]) for i in r...  12.9 us
    pallas_call x20, Pallas kernels, __call__(): pl.pallas_call(run, out_shape=[*out_shapes, *(jax.ShapeDtypeStruct(t.shap...  9.63 us
    ppermute x1, waiting for transfers between devices, body(): lax.ppermute(loadings, 'tm', [(i, (i + 1) % ranks) for i in range(ranks)])  3.05 us
    ppermute x1, starting transfers between devices, body(): lax.ppermute(part, 'neur', [(i, i ^ 1 << flip) for i in range(groups)])  1.92 us
  transfers between devices with their start and end apart: 16, of which 11 were waited for; matrix products, arithmetic and copies ran while one was open for 0% of the time, Pallas kernels for 18%

profile of v4, /device:TPU:0, one launch (start us, length us, event | category | flops | bytes accessed | tf_op | source)
XLA Modules:
  0.0 42.3 jit_solution(6828885313034338827)
XLA Ops:
  0.6 0.5 %collective-permute-start = (f32[8,512]{1,0:T(8,128)}, f32[8,512]{1,0:T(8,128)S(1)}, u32[]{:S(2)}, u32[]{:S(2)}) collective-permute-start(f32[8,512]{1,0:T(8,128)} %refs_3_.1), channel_id=1, source_target_pairs={{0,1},{1,2},{2,3},{3,4},{4,5},{5,6},{6,7},{7,8},{8,9},{9,10},{10,1... | collective-permute-start | bytes 49160 | tf_op jit(solution)/shard_map/ppermute | solution.py:303
  1.1 3.6 %body_kernel.1 = (bf16[256,1024]{1,0:T(8,128)(2,1)S(1)}, bf16[256,1024]{1,0:T(8,128)(2,1)S(1)}, bf16[256,384]{1,0:T(8,128)(2,1)S(1)}, bf16[256,384]{1,0:T(8,128)...) custom-call(s32[1]{0:T(128)} %bitcast.refs_0_, ...), custom_call_target="tpu_custom_call" | custom-call | flops 1610612736 | tf_op jit(solution)/shard_map/body_kernel/pallas_call | solution.py:65
  4.7 3.0 %collective-permute-done.refs_1_ = f32[8,512]{1,0:T(8,128)S(1)} collective-permute-done((f32[8,512]{1,0:T(8,128)}, f32[8,512]{1,0:T(8,128)S(1)}, u32[]{:S(2)}, u32[]{:S(2)}) %collective-permute-start) | collective-permute-done | bytes 16416 | tf_op jit(solution)/shard_map/ppermute | solution.py:303
  7.8 1.3 %head_kernel.1 = (f32[520,128]{1,0:T(8,128)S(1)}, f32[512,128]{1,0:T(8,128)S(1)}, bf16[256,128]{1,0:T(8,128)(2,1)S(1)}, bf16[256,128]{1,0:T(8,128)(2,1)S(1)}, bf...) custom-call(s32[1]{0:T(128)} %bitcast.refs_0_, ...), custom_call_target="tpu_custom_call" | custom-call | tf_op jit(solution)/shard_map/head_kernel/pallas_call | solution.py:65
  9.2 0.5 %collective-permute-start.1 = (f32[64,8,128]{2,1,0:T(8,128)S(1)}, f32[64,8,128]{2,1,0:T(8,128)S(1)}, u32[]{:S(2)}, u32[]{:S(2)}) collective-permute-start(f32[64,8,128]{2,1,0:T(8,128)S(1)} %bitcast.10), channel_id=1, source_target_pairs={{0,1},{1,0},{2,3},{3,2},{4,5},{5,4},{6,7},{7,6},{8,9},{9,8},{10,11... | collective-permute-start | bytes 786440 | tf_op jit(solution)/shard_map/ppermute | solution.py:300
  9.7 0.4 home_kernel.1
  10.0 1.6 %lagged_kernel.1 = (f32[8,768]{1,0:T(8,128)S(1)}, f32[8,128]{1,0:T(8,128)S(1)}) custom-call(s32[1]{0:T(128)} %bitcast.refs_0_, bf16[256,1024]{1,0:T(8,128)(2,1)S(1)} %get-tuple-element.63.refs_4_.refs_1_, bf16[256,1024]{1,0:T(8,128)(2,1)S(1)} %get-tuple-element.64.refs_5_.refs_2_, ...), custom_call_target="tpu_custom_call", output_to_operand_aliasing={{1}: (8, {})} | custom-call | flops 805306368 | tf_op jit(solution)/shard_map/lagged_kernel/pallas_call | solution.py:65
  11.7 0.8 %collective-permute-start.5 = (f32[33,8,128]{2,1,0:T(8,128)S(1)}, f32[33,8,128]{2,1,0:T(8,128)S(1)}, u32[]{:S(2)}, u32[]{:S(2)}) collective-permute-start(f32[33,8,128]{2,1,0:T(8,128)S(1)} %get-tuple-element.85), channel_id=1, source_target_pairs={{0,2},{1,5},{2,0},{3,7},{4,6},{5,1},{6,4},{7,3},{8,10},{9,13},{10,... | collective-permute-start | bytes 405512 | tf_op jit(solution)/shard_map/ppermute | solution.py:300
  12.5 1.4 %collective-permute-start.3 = (f32[32,8,128]{2,1,0:T(8,128)S(1)}, f32[32,8,128]{2,1,0:T(8,128)S(1)}, u32[]{:S(2)}, u32[]{:S(2)}) collective-permute-start(f32[32,8,128]{2,1,0:T(8,128)S(1)} %get-tuple-element.82), channel_id=1, source_target_pairs={{0,2},{1,5},{2,0},{3,7},{4,6},{5,1},{6,4},{7,3},{8,10},{9,13},{10,... | collective-permute-start | bytes 393224 | tf_op jit(solution)/shard_map/ppermute | solution.py:300
  13.9 1.9 %collective-permute-start.4 = (f32[8,768]{1,0:T(8,128)S(1)}, f32[8,768]{1,0:T(8,128)S(1)}, u32[]{:S(2)}, u32[]{:S(2)}) collective-permute-start(f32[8,768]{1,0:T(8,128)S(1)} %get-tuple-element.83.refs_1_), channel_id=1, source_target_pairs={{0,16},{16,0},{1,17},{17,1},{2,18},{18,2},{3,19},{19,3},{4,20},{20... | collective-permute-start | bytes 73736 | tf_op jit(solution)/shard_map/ppermute | solution.py:350
  15.8 1.0 %collective-permute-done.5.refs_2_ = f32[33,8,128]{2,1,0:T(8,128)S(1)} collective-permute-done((f32[33,8,128]{2,1,0:T(8,128)S(1)}, f32[33,8,128]{2,1,0:T(8,128)S(1)}, u32[]{:S(2)}, u32[]{:S(2)}) %collective-permute-start.5) | collective-permute-done | bytes 135200 | tf_op jit(solution)/shard_map/ppermute | solution.py:300
  16.8 0.8 %collective-permute-start.7 = (f32[17,8,128]{2,1,0:T(8,128)S(1)}, f32[17,8,128]{2,1,0:T(8,128)S(1)}, u32[]{:S(2)}, u32[]{:S(2)}) collective-permute-start(f32[17,8,128]{2,1,0:T(8,128)S(1)} %get-tuple-element.92), channel_id=1, source_target_pairs={{0,4},{1,3},{2,6},{3,1},{4,0},{5,7},{6,2},{7,5},{8,12},{9,11},{10,... | collective-permute-start | bytes 208904 | tf_op jit(solution)/shard_map/ppermute | solution.py:300
  17.6 0.1 collective-permute-done.4.refs_2_
  17.7 0.3 loads_kernel.1
  18.0 0.2 collective-permute-done.3.refs_2_
  18.2 1.1 %collective-permute-start.6 = (f32[16,8,128]{2,1,0:T(8,128)S(1)}, f32[16,8,128]{2,1,0:T(8,128)S(1)}, u32[]{:S(2)}, u32[]{:S(2)}) collective-permute-start(f32[16,8,128]{2,1,0:T(8,128)S(1)} %get-tuple-element.90), channel_id=1, source_target_pairs={{0,4},{1,3},{2,6},{3,1},{4,0},{5,7},{6,2},{7,5},{8,12},{9,11},{10,... | collective-permute-start | bytes 196616 | tf_op jit(solution)/shard_map/ppermute | solution.py:300
  19.3 1.9 %collective-permute-done.7.refs_2_ = f32[17,8,128]{2,1,0:T(8,128)S(1)} collective-permute-done((f32[17,8,128]{2,1,0:T(8,128)S(1)}, f32[17,8,128]{2,1,0:T(8,128)S(1)}, u32[]{:S(2)}, u32[]{:S(2)}) %collective-permute-start.7) | collective-permute-done | bytes 69664 | tf_op jit(solution)/shard_map/ppermute | solution.py:300
  21.2 1.8 %collective-permute-start.9 = (f32[18,8,128]{2,1,0:T(8,128)S(1)}, f32[18,8,128]{2,1,0:T(8,128)S(1)}, u32[]{:S(2)}, u32[]{:S(2)}) collective-permute-start(f32[18,8,128]{2,1,0:T(8,128)S(1)} %get-tuple-element.97.refs_1_), channel_id=1, source_target_pairs={{0,8},{1,9},{2,10},{3,11},{4,12},{5,13},{6,14},{7,15},{8,0},{9,1},... | collective-permute-start | bytes 221192 | tf_op jit(solution)/shard_map/ppermute | solution.py:300
  23.0 2.5 %collective-permute-start.8 = (f32[16,8,128]{2,1,0:T(8,128)S(1)}, f32[16,8,128]{2,1,0:T(8,128)S(1)}, u32[]{:S(2)}, u32[]{:S(2)}) collective-permute-start(f32[16,8,128]{2,1,0:T(8,128)S(1)} %get-tuple-element.96.refs_1_), channel_id=1, source_target_pairs={{0,8},{1,9},{2,10},{3,11},{4,12},{5,13},{6,14},{7,15},{8,0},{9,1},... | collective-permute-start | bytes 196616 | tf_op jit(solution)/shard_map/ppermute | solution.py:300
  25.5 2.5 %collective-permute-done.9.refs_2_ = f32[18,8,128]{2,1,0:T(8,128)S(1)} collective-permute-done((f32[18,8,128]{2,1,0:T(8,128)S(1)}, f32[18,8,128]{2,1,0:T(8,128)S(1)}, u32[]{:S(2)}, u32[]{:S(2)}) %collective-permute-start.9) | collective-permute-done | bytes 73760 | tf_op jit(solution)/shard_map/ppermute | solution.py:300
  28.0 0.1 collective-permute-start.11
  28.1 1.3 %collective-permute-done.8.refs_2_ = f32[16,8,128]{2,1,0:T(8,128)S(1)} collective-permute-done((f32[16,8,128]{2,1,0:T(8,128)S(1)}, f32[16,8,128]{2,1,0:T(8,128)S(1)}, u32[]{:S(2)}, u32[]{:S(2)}) %collective-permute-start.8) | collective-permute-done | bytes 65568 | tf_op jit(solution)/shard_map/ppermute | solution.py:300
  29.4 0.8 %collective-permute-start.10 = (f32[16,8,128]{2,1,0:T(8,128)S(1)}, f32[16,8,128]{2,1,0:T(8,128)S(1)}, u32[]{:S(2)}, u32[]{:S(2)}) collective-permute-start(f32[16,8,128]{2,1,0:T(8,128)S(1)} %get-tuple-element.101.refs_1_), channel_id=1, source_target_pairs={{0,4},{1,3},{2,6},{3,1},{4,0},{5,7},{6,2},{7,5},{8,12},{9,11},{10,... | collective-permute-start | bytes 196616 | tf_op jit(solution)/shard_map/ppermute | solution.py:300
  30.2 2.3 %collective-permute-done.11.refs_2_ = f32[17,8,128]{2,1,0:T(8,128)S(1)} collective-permute-done((f32[17,8,128]{2,1,0:T(8,128)S(1)}, f32[17,8,128]{2,1,0:T(8,128)S(1)}, u32[]{:S(2)}, u32[]{:S(2)}) %collective-permute-start.11) | collective-permute-done | bytes 69664 | tf_op jit(solution)/shard_map/ppermute | solution.py:300
  32.5 2.3 %collective-permute-start.13 = (f32[33,8,128]{2,1,0:T(8,128)S(1)}, f32[33,8,128]{2,1,0:T(8,128)S(1)}, u32[]{:S(2)}, u32[]{:S(2)}) collective-permute-start(f32[33,8,128]{2,1,0:T(8,128)S(1)} %get-tuple-element.106.refs_1_), channel_id=1, source_target_pairs={{0,2},{1,5},{2,0},{3,7},{4,6},{5,1},{6,4},{7,3},{8,10},{9,13},{10,... | collective-permute-start | bytes 405512 | tf_op jit(solution)/shard_map/ppermute | solution.py:300
  34.9 0.7 %collective-permute-start.12 = (f32[32,8,128]{2,1,0:T(8,128)S(1)}, f32[32,8,128]{2,1,0:T(8,128)S(1)}, u32[]{:S(2)}, u32[]{:S(2)}) collective-permute-start(f32[32,8,128]{2,1,0:T(8,128)S(1)} %get-tuple-element.105.refs_1_), channel_id=1, source_target_pairs={{0,2},{1,5},{2,0},{3,7},{4,6},{5,1},{6,4},{7,3},{8,10},{9,13},{10,... | collective-permute-start | bytes 393224 | tf_op jit(solution)/shard_map/ppermute | solution.py:300
  35.6 2.3 %collective-permute-done.13.refs_2_ = f32[33,8,128]{2,1,0:T(8,128)S(1)} collective-permute-done((f32[33,8,128]{2,1,0:T(8,128)S(1)}, f32[33,8,128]{2,1,0:T(8,128)S(1)}, u32[]{:S(2)}, u32[]{:S(2)}) %collective-permute-start.13) | collective-permute-done | bytes 135200 | tf_op jit(solution)/shard_map/ppermute | solution.py:300
  38.0 0.7 %store_kernel.3 = (f32[256,8,128]{2,1,0:T(8,128)}, f32[8,128]{1,0:T(8,128)S(1)}) custom-call(s32[1]{0:T(128)} %bitcast.refs_0_, f32[65,8,128]{2,1,0:T(8,128)S(1)} %get-tuple-element.108.refs_1_, f32[8,128]{1,0:T(8,128)S(1)} %get-tuple-element.109.refs_2_), custom_call_target="tpu_custom_call", output_to_operand_aliasing={{1}: (2, {})} | custom-call | tf_op jit(solution)/shard_map/store_kernel/pallas_call | solution.py:65
  38.7 1.2 %collective-permute-done.12.refs_2_ = f32[32,8,128]{2,1,0:T(8,128)S(1)} collective-permute-done((f32[32,8,128]{2,1,0:T(8,128)S(1)}, f32[32,8,128]{2,1,0:T(8,128)S(1)}, u32[]{:S(2)}, u32[]{:S(2)}) %collective-permute-start.12) | collective-permute-done | bytes 131104 | tf_op jit(solution)/shard_map/ppermute | solution.py:300
  40.1 0.8 %store_kernel.4 = (f32[256,8,128]{2,1,0:T(8,128)}, f32[8,512]{1,0:T(8,128)}, f32[8,128]{1,0:T(8,128)S(1)}) custom-call(s32[1]{0:T(128)} %bitcast.refs_0_, f32[65,8,128]{2,1,0:T(8,128)S(1)} %collective-permute-done.15.refs_1_, f32[64,8,128]{2,1,0:T(8,128)S(1)} %get-tuple-element.111.refs_2_, ...), custom_call_target="tpu_custom_call", output_to_operand_aliasing={{0}: (5, {}), {2}: (6, {})} | custom-call | tf_op jit(solution)/shard_map/store_kernel/pallas_call | solution.py:65
  40.9 0.7 %collective-permute-done.14.refs_1_ = f32[64,8,128]{2,1,0:T(8,128)S(1)} collective-permute-done((f32[64,8,128]{2,1,0:T(8,128)S(1)}, f32[64,8,128]{2,1,0:T(8,128)S(1)}, u32[]{:S(2)}, u32[]{:S(2)}) %collective-permute-start.14) | collective-permute-done | bytes 262176 | tf_op jit(solution)/shard_map/ppermute | solution.py:300
  41.6 0.7 %store_kernel.5 = (f32[256,8,128]{2,1,0:T(8,128)}, f32[8,128]{1,0:T(8,128)S(1)}) custom-call(s32[1]{0:T(128)} %bitcast.refs_0_, f32[64,8,128]{2,1,0:T(8,128)S(1)} %collective-permute-done.14.refs_1_, f32[256,8,128]{2,1,0:T(8,128)} %get-tuple-element.116.refs_2_, f32[8,128]{1,0:T(8,128)S(1)} %get-tuple-element.117.refs_3_), custom_call_target="tpu_custom_call", output_to_operand_aliasing={{0}: (2, {}), {1}: (3, {})} | custom-call | tf_op jit(solution)/shard_map/store_kernel/pallas_call | solution.py:65
  (23 shorter events, 0.5 us)
Async XLA Ops:
  0.6 7.1 %collective-permute-start = (f32[8,512]{1,0:T(8,128)}, f32[8,512]{1,0:T(8,128)S(1)}, u32[]{:S(2)}, u32[]{:S(2)}) collective-permute-start(f32[8,512]{1,0:T(8,128)} %refs_3_.1), channel_id=1, source_target_pairs={{0,1},{1,2},{2,3},{3,4},{4,5},{5,6},{6,7},{7,8},{8,9},{9,10},{10,1... | collective-permute-start | bytes 49160 | tf_op jit(solution)/shard_map/ppermute | solution.py:303
  9.1 2.6 %collective-permute-start.2 = (f32[65,8,128]{2,1,0:T(8,128)S(1)}, f32[65,8,128]{2,1,0:T(8,128)S(1)}, u32[]{:S(2)}, u32[]{:S(2)}) collective-permute-start(f32[65,8,128]{2,1,0:T(8,128)S(1)} %bitcast.9), channel_id=1, source_target_pairs={{0,1},{1,0},{2,3},{3,2},{4,5},{5,4},{6,7},{7,6},{8,9},{9,8},{10,11... | collective-permute-start | bytes 798728 | tf_op jit(solution)/shard_map/ppermute | solution.py:300
  9.2 3.3 %collective-permute-start.1 = (f32[64,8,128]{2,1,0:T(8,128)S(1)}, f32[64,8,128]{2,1,0:T(8,128)S(1)}, u32[]{:S(2)}, u32[]{:S(2)}) collective-permute-start(f32[64,8,128]{2,1,0:T(8,128)S(1)} %bitcast.10), channel_id=1, source_target_pairs={{0,1},{1,0},{2,3},{3,2},{4,5},{5,4},{6,7},{7,6},{8,9},{9,8},{10,11... | collective-permute-start | bytes 786440 | tf_op jit(solution)/shard_map/ppermute | solution.py:300
  11.6 16.4 %copy-start = (f32[256,8,128]{2,1,0:T(8,128)S(1)}, f32[256,8,128]{2,1,0:T(8,128)}, u32[]{:S(2)}) copy-start(f32[256,8,128]{2,1,0:T(8,128)} %refs_4_.3) | copy-start | bytes 3145732
  11.7 5.1 %collective-permute-start.5 = (f32[33,8,128]{2,1,0:T(8,128)S(1)}, f32[33,8,128]{2,1,0:T(8,128)S(1)}, u32[]{:S(2)}, u32[]{:S(2)}) collective-permute-start(f32[33,8,128]{2,1,0:T(8,128)S(1)} %get-tuple-element.85), channel_id=1, source_target_pairs={{0,2},{1,5},{2,0},{3,7},{4,6},{5,1},{6,4},{7,3},{8,10},{9,13},{10,... | collective-permute-start | bytes 405512 | tf_op jit(solution)/shard_map/ppermute | solution.py:300
  12.5 5.7 %collective-permute-start.3 = (f32[32,8,128]{2,1,0:T(8,128)S(1)}, f32[32,8,128]{2,1,0:T(8,128)S(1)}, u32[]{:S(2)}, u32[]{:S(2)}) collective-permute-start(f32[32,8,128]{2,1,0:T(8,128)S(1)} %get-tuple-element.82), channel_id=1, source_target_pairs={{0,2},{1,5},{2,0},{3,7},{4,6},{5,1},{6,4},{7,3},{8,10},{9,13},{10,... | collective-permute-start | bytes 393224 | tf_op jit(solution)/shard_map/ppermute | solution.py:300
  13.9 3.8 %collective-permute-start.4 = (f32[8,768]{1,0:T(8,128)S(1)}, f32[8,768]{1,0:T(8,128)S(1)}, u32[]{:S(2)}, u32[]{:S(2)}) collective-permute-start(f32[8,768]{1,0:T(8,128)S(1)} %get-tuple-element.83.refs_1_), channel_id=1, source_target_pairs={{0,16},{16,0},{1,17},{17,1},{2,18},{18,2},{3,19},{19,3},{4,20},{20... | collective-permute-start | bytes 73736 | tf_op jit(solution)/shard_map/ppermute | solution.py:350
  16.8 4.4 %collective-permute-start.7 = (f32[17,8,128]{2,1,0:T(8,128)S(1)}, f32[17,8,128]{2,1,0:T(8,128)S(1)}, u32[]{:S(2)}, u32[]{:S(2)}) collective-permute-start(f32[17,8,128]{2,1,0:T(8,128)S(1)} %get-tuple-element.92), channel_id=1, source_target_pairs={{0,4},{1,3},{2,6},{3,1},{4,0},{5,7},{6,2},{7,5},{8,12},{9,11},{10,... | collective-permute-start | bytes 208904 | tf_op jit(solution)/shard_map/ppermute | solution.py:300
  18.2 4.8 %collective-permute-start.6 = (f32[16,8,128]{2,1,0:T(8,128)S(1)}, f32[16,8,128]{2,1,0:T(8,128)S(1)}, u32[]{:S(2)}, u32[]{:S(2)}) collective-permute-start(f32[16,8,128]{2,1,0:T(8,128)S(1)} %get-tuple-element.90), channel_id=1, source_target_pairs={{0,4},{1,3},{2,6},{3,1},{4,0},{5,7},{6,2},{7,5},{8,12},{9,11},{10,... | collective-permute-start | bytes 196616 | tf_op jit(solution)/shard_map/ppermute | solution.py:300
  21.2 6.8 %collective-permute-start.9 = (f32[18,8,128]{2,1,0:T(8,128)S(1)}, f32[18,8,128]{2,1,0:T(8,128)S(1)}, u32[]{:S(2)}, u32[]{:S(2)}) collective-permute-start(f32[18,8,128]{2,1,0:T(8,128)S(1)} %get-tuple-element.97.refs_1_), channel_id=1, source_target_pairs={{0,8},{1,9},{2,10},{3,11},{4,12},{5,13},{6,14},{7,15},{8,0},{9,1},... | collective-permute-start | bytes 221192 | tf_op jit(solution)/shard_map/ppermute | solution.py:300
  23.0 6.4 %collective-permute-start.8 = (f32[16,8,128]{2,1,0:T(8,128)S(1)}, f32[16,8,128]{2,1,0:T(8,128)S(1)}, u32[]{:S(2)}, u32[]{:S(2)}) collective-permute-start(f32[16,8,128]{2,1,0:T(8,128)S(1)} %get-tuple-element.96.refs_1_), channel_id=1, source_target_pairs={{0,8},{1,9},{2,10},{3,11},{4,12},{5,13},{6,14},{7,15},{8,0},{9,1},... | collective-permute-start | bytes 196616 | tf_op jit(solution)/shard_map/ppermute | solution.py:300
  28.0 4.5 %collective-permute-start.11 = (f32[17,8,128]{2,1,0:T(8,128)S(1)}, f32[17,8,128]{2,1,0:T(8,128)S(1)}, u32[]{:S(2)}, u32[]{:S(2)}) collective-permute-start(f32[17,8,128]{2,1,0:T(8,128)S(1)} %get-tuple-element.102.refs_1_), channel_id=1, source_target_pairs={{0,4},{1,3},{2,6},{3,1},{4,0},{5,7},{6,2},{7,5},{8,12},{9,11},{10,... | collective-permute-start | bytes 208904 | tf_op jit(solution)/shard_map/ppermute | solution.py:300
  29.4 5.5 %collective-permute-start.10 = (f32[16,8,128]{2,1,0:T(8,128)S(1)}, f32[16,8,128]{2,1,0:T(8,128)S(1)}, u32[]{:S(2)}, u32[]{:S(2)}) collective-permute-start(f32[16,8,128]{2,1,0:T(8,128)S(1)} %get-tuple-element.101.refs_1_), channel_id=1, source_target_pairs={{0,4},{1,3},{2,6},{3,1},{4,0},{5,7},{6,2},{7,5},{8,12},{9,11},{10,... | collective-permute-start | bytes 196616 | tf_op jit(solution)/shard_map/ppermute | solution.py:300
  32.5 5.3 %collective-permute-start.13 = (f32[33,8,128]{2,1,0:T(8,128)S(1)}, f32[33,8,128]{2,1,0:T(8,128)S(1)}, u32[]{:S(2)}, u32[]{:S(2)}) collective-permute-start(f32[33,8,128]{2,1,0:T(8,128)S(1)} %get-tuple-element.106.refs_1_), channel_id=1, source_target_pairs={{0,2},{1,5},{2,0},{3,7},{4,6},{5,1},{6,4},{7,3},{8,10},{9,13},{10,... | collective-permute-start | bytes 405512 | tf_op jit(solution)/shard_map/ppermute | solution.py:300
  34.9 5.0 %collective-permute-start.12 = (f32[32,8,128]{2,1,0:T(8,128)S(1)}, f32[32,8,128]{2,1,0:T(8,128)S(1)}, u32[]{:S(2)}, u32[]{:S(2)}) collective-permute-start(f32[32,8,128]{2,1,0:T(8,128)S(1)} %get-tuple-element.105.refs_1_), channel_id=1, source_target_pairs={{0,2},{1,5},{2,0},{3,7},{4,6},{5,1},{6,4},{7,3},{8,10},{9,13},{10,... | collective-permute-start | bytes 393224 | tf_op jit(solution)/shard_map/ppermute | solution.py:300
  37.9 2.1 %collective-permute-start.15 = (f32[65,8,128]{2,1,0:T(8,128)S(1)}, f32[65,8,128]{2,1,0:T(8,128)S(1)}, u32[]{:S(2)}, u32[]{:S(2)}) collective-permute-start(f32[65,8,128]{2,1,0:T(8,128)S(1)} %get-tuple-element.108.refs_1_), channel_id=1, source_target_pairs={{0,1},{1,0},{2,3},{3,2},{4,5},{5,4},{6,7},{7,6},{8,9},{9,8},{10,11... | collective-permute-start | bytes 798728 | tf_op jit(solution)/shard_map/ppermute | solution.py:300
  40.0 1.6 %collective-permute-start.14 = (f32[64,8,128]{2,1,0:T(8,128)S(1)}, f32[64,8,128]{2,1,0:T(8,128)S(1)}, u32[]{:S(2)}, u32[]{:S(2)}) collective-permute-start(f32[64,8,128]{2,1,0:T(8,128)S(1)} %get-tuple-element.111.refs_2_), channel_id=1, source_target_pairs={{0,1},{1,0},{2,3},{3,2},{4,5},{5,4},{6,7},{7,6},{8,9},{9,8},{10,11... | collective-permute-start | bytes 786440 | tf_op jit(solution)/shard_map/ppermute | solution.py:300

commit v5 on v4

--- a/solution.py
+++ b/solution.py
@@ -15,7 +15,6 @@
 MIB = 1024 * 1024
 BODY_LIMIT = 20
 ONES = 16
-LOADS_AFTER = 0
 PARTS = (1, 1)
 
 
@@ -78,30 +77,19 @@
         return made[:results]
 
 
-def body_kernel(me_ref, counts_hbm, motifs_hbm, loads_hbm, mh_ref, ml_ref, rh_ref, rl_ref, numer_ref, counts_ref,
-                loads_ref, total_ref, motifs_ref, rest_ref, th, tl, sems):
-    rows, frames = counts_hbm.shape
-    motif_count = loads_ref.shape[0]
-    lags = counts_ref.shape[1]
-    copies = [
-        pltpu.make_async_copy(loads_hbm, loads_ref, sems.at[0]),
-        pltpu.make_async_copy(motifs_hbm, motifs_ref, sems.at[1]),
-        pltpu.make_async_copy(counts_hbm.at[:, pl.ds(lags, frames - lags)], rest_ref, sems.at[2]),
-        pltpu.make_async_copy(counts_hbm.at[:, pl.ds(0, lags)], counts_ref, sems.at[3]),
-    ]
-    for copy in copies:
-        copy.start()
-    copies[0].wait()
+def open_kernel(me_ref, out_ref):
+    out_ref[...] = jnp.zeros_like(out_ref)
+
+
+def body_kernel(me_ref, counts_ref, motifs_ref, loads_ref, mh_ref, ml_ref, rh_ref, rl_ref, numer_ref, total_ref, th, tl):
+    rows, frames = counts_ref.shape
+    motif_count, lags = total_ref.shape
     for k in range(motif_count):
         at = pl.ds(k * lags, lags)
         th[at, :], tl[at, :] = split(toeplitz(loads_ref[pl.ds(k, 1), :], lags)[:, lags:])
-    copies[1].wait()
-    for k in range(motif_count):
-        at = pl.ds(k * lags, lags)
         mh_ref[:, at], ml_ref[:, at] = split(motifs_ref[pl.ds(k, rows, stride=motif_count), :])
     estimate = dot3(mh_ref[...], ml_ref[...], th[...], tl[...], NN)
-    copies[2].wait()
-    rh_ref[...], rl_ref[...] = split(rest_ref[...] / estimate)
+    rh_ref[...], rl_ref[...] = split(counts_ref[:, lags:] / estimate)
     ones = jnp.ones((ONES, frames - lags), BF16)
     xh = jnp.concatenate([rh_ref[...], ones], axis=0)
     xl = jnp.concatenate([rl_ref[...], jnp.zeros_like(ones)], axis=0)
@@ -109,13 +97,6 @@
         at = pl.ds(k * lags, 2 * lags)
         numer_ref[:, at] = dot3(xh, xl, th[at, :], tl[at, :], NT)
     total_ref[...] = jnp.sum(motifs_ref[...].reshape(rows, motif_count, lags), axis=0)
-    copies[3].wait()
-
-
-def numer_rows(numer, motif_count, out_ref, count):
-    lags = out_ref.shape[-1]
-    for k in range(motif_count):
-        out_ref[pl.ds(k, count, stride=motif_count), :] = numer[:count, k * lags:(k + 1) * lags]
 
 
 def blocks(sizes, core):
@@ -130,15 +111,15 @@
 
 def head_kernel(sizes, me_ref, tail_ref, counts_ref, loads_ref, mh_ref, ml_ref, numer_ref, *refs):
     *send_refs, fh_ref, fl_ref, hh_ref, hl_ref, denom_ref = refs
-    rows, lags = counts_ref.shape
-    motif_count, frames = loads_ref.shape
+    rows, frames = counts_ref.shape
+    motif_count, lags = denom_ref.shape
     for k in range(motif_count):
         at = pl.ds(k * lags, lags)
         tail = jnp.where(me_ref[0] == 0, 0.0, tail_ref[pl.ds(k, 1), frames - lags:])
         row = jnp.concatenate([tail, loads_ref[pl.ds(k, 1), :lags]], axis=1)
         hh_ref[at, :], hl_ref[at, :] = split(toeplitz(row, lags)[:, lags:])
     estimate = dot3(mh_ref[...], ml_ref[...], hh_ref[...], hl_ref[...], NN)
-    fh_ref[...], fl_ref[...] = split(counts_ref[...] / estimate)
+    fh_ref[...], fl_ref[...] = split(counts_ref[:, :lags] / estimate)
     away = blocks(sizes, 1 - (me_ref[0] & 1))
     ones = jnp.ones((ONES, lags), BF16)
     xh = jnp.concatenate([*(fh_ref[at, :] for at in away), ones], axis=0)
@@ -208,9 +189,12 @@
     if denom_out:
         denom = mine_ref[rows] + got_ref[rows]
         denom_out[0][...] = denom
-        out_ref[rows] = carry(me, steps - 1, mine_ref[rows + 1], got_ref[rows + 1])
     else:
         denom = denom_ref[...]
+    at_row = mine_ref.shape[0] - 1
+    row = carry(me, steps - 1, mine_ref[at_row], got_ref[at_row])
+    for i in range(rows, out_ref.shape[0]):
+        out_ref[i] = row
     out_ref[:rows] = motifs_ref[pl.ds(at, rows)] * numer / denom[None]
 
 
@@ -219,8 +203,9 @@
     bit = place(me, step, steps)
     out_ref[pl.ds(bit * half, half)] = mine_ref[:half]
     out_ref[pl.ds((1 - bit) * half, half)] = got_ref[:half]
-    if mine_ref.shape[0] > half:
-        out_ref[2 * half] = carry(me, carry_bit(me, step, steps), mine_ref[half], got_ref[half])
+    row = carry(me, carry_bit(me, step, steps), mine_ref[half], got_ref[half])
+    for i in range(2 * half, out_ref.shape[0]):
+        out_ref[i] = row
 
 
 def store_kernel(parts, row_at, ranks, me_ref, *refs):
@@ -300,20 +285,19 @@
         return lax.ppermute(x, "tm", [(i, i ^ (1 << order(i & 1, steps)[step])) for i in range(ranks)])
 
     call = Chain(lax.axis_index("tm").astype(jnp.int32).reshape(1))
-    tail = lax.ppermute(loadings, "tm", [(i, (i + 1) % ranks) for i in range(ranks)])
     flat = motifs.reshape(rows * motif_count, lags)
     depth, rest = motif_count * lags, frames - lags
     macs = rows * depth * frames * 3
-    mh, ml, rh, rl, numer, head_counts, own_loads, total = call(
+    (call.token,) = call(open_kernel, [shape(motif_count, lags)], flops=10 ** 10)
+    call.token, sent = lax.optimization_barrier((call.token, loadings))
+    tail = lax.ppermute(sent, "tm", [(i, (i + 1) % ranks) for i in range(ranks)])
+    mh, ml, rh, rl, numer, total = call(
         body_kernel,
         [shape(rows, depth, dtype=BF16)] * 2 + [shape(rows, rest, dtype=BF16)] * 2
-        + [shape(rows + ONES, depth), shape(rows, lags), shape(motif_count, frames), shape(motif_count, lags)],
-        *(pltpu.with_memory_space_constraint(x, pltpu.HBM) for x in (counts, flat, loadings)),
-        spaces=[pltpu.HBM] * 3,
-        scratch=[pltpu.VMEM((rows * motif_count, lags), F32), pltpu.VMEM((rows, rest), F32)]
-        + [pltpu.VMEM((depth, rest), BF16)] * 2 + [pltpu.SemaphoreType.DMA((4,))],
-        limit=BODY_LIMIT, flops=4 * macs,
+        + [shape(rows + ONES, depth), shape(motif_count, lags)],
+        counts, flat, loadings, scratch=[pltpu.VMEM((depth, rest), BF16)] * 2, limit=BODY_LIMIT, flops=4 * macs,
     )
+    head_counts, own_loads = counts, loadings
     sizes = [rows * share // sum(PARTS) for share in PARTS]
     assert sum(sizes) == rows and all(size % (ranks // 2) == 0 for size in sizes)
     chunks = range(len(sizes))
@@ -326,7 +310,6 @@
         tail, head_counts, own_loads, mh, ml, numer, limit=6,
     )
 
-    call.token = denom
 
     def cube(x):
         return x.reshape(-1, motif_count, lags)
@@ -339,15 +322,6 @@
         functools.partial(home_kernel, sizes), parts, fh, fl, hh, hl, denom, numer, limit=6, flops=macs // 4
     )
     keep = [cube(x) for x in keep]
-    (part,) = call(
-        lagged_kernel, [shape(motif_count, frames + 2 * lags)], mh, ml, fh, fl, rh, rl, total,
-        scratch=[pltpu.VMEM((rows, depth), BF16)] * 2, limit=8, flops=2 * macs,
-    )
-    other = jnp.zeros_like(part)
-    for flip in range(flips):
-        if flip:
-            (part,) = call(pair_kernel, [part], part, other, order=False)
-        other = lax.ppermute(part, "neur", [(i, i ^ (1 << flip)) for i in range(groups)])
     for step in range(1, steps - 1):
         for c in chunks:
             half[c] //= 2
@@ -355,22 +329,33 @@
                 functools.partial(fold_kernel, step, steps, half[c]), [cubes(half[c] + extra[c])] * 2, keep[c], got[c]
             )
             got[c] = swap(send[c], step)
-            if step == 2 and c == LOADS_AFTER:
-                ahead, numer, scale = call(
-                    functools.partial(loads_kernel, ranks), [shape(motif_count, lags)] + [shape(motif_count, frames)] * 2,
-                    part, other, own_loads,
-                )
+        if step == 1:
+            (part,) = call(
+                lagged_kernel, [shape(motif_count, frames + 2 * lags)], mh, ml, fh, fl, rh, rl, total,
+                scratch=[pltpu.VMEM((rows, depth), BF16)] * 2, limit=8, flops=2 * macs,
+            )
+            other = jnp.zeros_like(part)
+            for flip in range(flips):
+                if flip:
+                    (part,) = call(pair_kernel, [part], part, other, order=False)
+                other = lax.ppermute(part, "neur", [(i, i ^ (1 << flip)) for i in range(groups)])
+    last = chunks[-1]
     for c in chunks:
-        if c == 0:
-            (keep[c],) = call(pair_row_kernel, [cubes(half[c] + 2)], keep[c], got[c], ahead)
+        if c == last:
+            ahead, numer, scale = call(
+                functools.partial(loads_kernel, ranks), [shape(motif_count, lags)] + [shape(motif_count, frames)] * 2,
+                part, other, own_loads,
+            )
+            (keep[c],) = call(pair_row_kernel, [cubes(half[c] + extra[c] + 1)], keep[c], got[c], ahead)
         else:
-            (keep[c],) = call(pair_kernel, [cubes(half[c])], keep[c], got[c])
+            (keep[c],) = call(pair_row_kernel, [cubes(half[c] + extra[c] + 1)], keep[c], got[c], denom)
         got[c] = swap(keep[c], steps - 1)
+    carried = [1 + (c != last) for c in chunks]
     mine = [None for c in chunks]
     for c in chunks:
         mine[c], *more = call(
             functools.partial(update_kernel, sum(sizes[:c]), sizes[c], steps),
-            [cubes(half[c] + extra[c])] + [shape(motif_count, lags)] * extra[c], keep[c], got[c], denom, motifs,
+            [cubes(half[c] + carried[c])] + [shape(motif_count, lags)] * extra[c], keep[c], got[c], denom, motifs,
         )
         if more:
             denom = more[0]
@@ -379,7 +364,7 @@
     for step in range(steps - 2, 0, -1):
         for c in chunks:
             (mine[c],) = call(
-                functools.partial(join_kernel, step, steps, half[c]), [cubes(2 * half[c] + extra[c])], mine[c], got[c]
+                functools.partial(join_kernel, step, steps, half[c]), [cubes(2 * half[c] + carried[c])], mine[c], got[c]
             )
             half[c] *= 2
             got[c] = swap(mine[c], step - 1)
@@ -394,7 +379,7 @@
 def store(call, out, new_loadings, rows, waiting, numer, scale, ranks):
     waiting = sorted(waiting, key=lambda block: block[2])
     first, half, own, block = waiting[0]
-    brings = first == 0 and not own
+    brings = len(waiting) == 1 and not own
     given = [block for *_, block in waiting] + [numer, scale] * brings
     spaces = [pltpu.VMEM] * len(given)
     results = [jax.ShapeDtypeStruct((rows, *block.shape[1:]), F32)] + [jax.ShapeDtypeStruct(numer.shape, F32)] * brings

time: 42.5 us -> 41.6 us (0.979)
  starting transfers between devices: 15.3 us -> 13.2 us
  waiting for transfers between devices: 16.5 us -> 18 us
  Pallas kernels: 9.63 us -> 8.55 us
  local copies, waits for them, and re-layouts: 0.01 us -> 0.89 us
    ppermute x14, starting transfers between devices: 12.9 us -> 10.8 us  [swap(): lax.ppermute(x, 'tm', [(i, i ^ 1 << order(i & 1, steps)[step]) for i in r...]
    pallas_call x20 -> x21, Pallas kernels: 9.63 us -> 8.55 us  [__call__(): pl.pallas_call(run, out_shape=[*out_shapes, *(jax.ShapeDtypeStruct(t.shap...]
    unnamed x3 -> x6, local copies, waits for them, and re-layouts: 0.01 us -> 0.89 us
    ppermute x14, waiting for transfers between devices: 13.4 us -> 14.2 us  [swap(): lax.ppermute(x, 'tm', [(i, i ^ 1 << order(i & 1, steps)[step]) for i in r...]
    ppermute x1, waiting for transfers between devices: 3.05 us -> 3.7 us  [body(): lax.ppermute(sent, 'tm', [(i, (i + 1) % ranks) for i in range(ranks)])]
  transfers between devices with their start and end apart: 16 -> 16, of which waited for: 11 -> 14; matrix products, arithmetic and copies ran while one was open for 0% -> 0% of each run, Pallas kernels for 18% -> 16%
where the time goes in v5:
time: 41.6 us; the launch traced here: 41.4 us
  waiting for transfers between devices  18 us (43%)
  starting transfers between devices  13.2 us (32%)
  Pallas kernels  8.55 us (21%)
  local copies, waits for them, and re-layouts  0.89 us (2%)
  between operations  0.82 us (2%)
    ppermute x14, waiting for transfers between devices, swap(): lax.ppermute(x, 'tm', [(i, i ^ 1 << order(i & 1, steps)[step]) for i in r...  14.2 us
    ppermute x14, starting transfers between devices, swap(): lax.ppermute(x, 'tm', [(i, i ^ 1 << order(i & 1, steps)[step]) for i in r...  10.8 us
    pallas_call x21, Pallas kernels, __call__(): pl.pallas_call(run, out_shape=[*out_shapes, *(jax.ShapeDtypeStruct(t.shap...  8.55 us
    ppermute x1, waiting for transfers between devices, body(): lax.ppermute(sent, 'tm', [(i, (i + 1) % ranks) for i in range(ranks)])  3.7 us
    ppermute x1, starting transfers between devices, body(): lax.ppermute(part, 'neur', [(i, i ^ 1 << flip) for i in range(groups)])  1.94 us
    unnamed x6, local copies, waits for them, and re-layouts  0.89 us
  transfers between devices with their start and end apart: 16, of which 14 were waited for; matrix products, arithmetic and copies ran while one was open for 0% of the time, Pallas kernels for 16%

profile of v5, /device:TPU:0, one launch (start us, length us, event | category | flops | bytes accessed | tf_op | source)
XLA Modules:
  0.0 41.4 jit_solution(9662005707328207127)
XLA Ops:
  0.7 0.7 %copy-done.2 = f32[8,512]{1,0:T(8,128)S(1)} copy-done((f32[8,512]{1,0:T(8,128)S(1)}, f32[8,512]{1,0:T(8,128)}, u32[]{:S(2)}) %copy-start.2) | copy-done | bytes 16408
  1.4 0.5 %collective-permute-start = (f32[8,512]{1,0:T(8,128)S(1)}, f32[8,512]{1,0:T(8,128)S(1)}, u32[]{:S(2)}, u32[]{:S(2)}) collective-permute-start(f32[8,512]{1,0:T(8,128)S(1)} %copy-done.2), channel_id=1, source_target_pairs={{0,1},{1,2},{2,3},{3,4},{4,5},{5,6},{6,7},{7,8},{8,9},{9,10},{10,1... | collective-permute-start | bytes 49160 | tf_op jit(solution)/shard_map/ppermute | solution.py:293
  2.0 2.5 %body_kernel.1 = (bf16[256,1024]{1,0:T(8,128)(2,1)S(1)}, bf16[256,1024]{1,0:T(8,128)(2,1)S(1)}, bf16[256,384]{1,0:T(8,128)(2,1)S(1)}, bf16[256,384]{1,0:T(8,128)...) custom-call(s32[1]{0:T(128)} %bitcast.refs_0_, ...), custom_call_target="tpu_custom_call", output_to_operand_aliasing={{6}: (4, {})} | custom-call | flops 1610612736 | tf_op jit(solution)/shard_map/body_kernel/pallas_call | solution.py:64
  4.5 3.7 %collective-permute-done.refs_1_ = f32[8,512]{1,0:T(8,128)S(1)} collective-permute-done((f32[8,512]{1,0:T(8,128)S(1)}, f32[8,512]{1,0:T(8,128)S(1)}, u32[]{:S(2)}, u32[]{:S(2)}) %collective-permute-start) | collective-permute-done | bytes 16416 | tf_op jit(solution)/shard_map/ppermute | solution.py:293
  8.2 1.3 %head_kernel.1 = (f32[520,128]{1,0:T(8,128)S(1)}, f32[512,128]{1,0:T(8,128)S(1)}, bf16[256,128]{1,0:T(8,128)(2,1)S(1)}, bf16[256,128]{1,0:T(8,128)(2,1)S(1)}, bf...) custom-call(s32[1]{0:T(128)} %bitcast.refs_0_, ...), custom_call_target="tpu_custom_call", output_to_operand_aliasing={{7}: (7, {})} | custom-call | tf_op jit(solution)/shard_map/head_kernel/pallas_call | solution.py:64
  9.6 0.5 %collective-permute-start.1 = (f32[64,8,128]{2,1,0:T(8,128)S(1)}, f32[64,8,128]{2,1,0:T(8,128)S(1)}, u32[]{:S(2)}, u32[]{:S(2)}) collective-permute-start(f32[64,8,128]{2,1,0:T(8,128)S(1)} %bitcast.10), channel_id=1, source_target_pairs={{0,1},{1,0},{2,3},{3,2},{4,5},{5,4},{6,7},{7,6},{8,9},{9,8},{10,11... | collective-permute-start | bytes 786440 | tf_op jit(solution)/shard_map/ppermute | solution.py:285
  10.1 0.4 home_kernel.1
  10.5 0.6 %collective-permute-done.2.refs_2_ = f32[65,8,128]{2,1,0:T(8,128)S(1)} collective-permute-done((f32[65,8,128]{2,1,0:T(8,128)S(1)}, f32[65,8,128]{2,1,0:T(8,128)S(1)}, u32[]{:S(2)}, u32[]{:S(2)}) %collective-permute-start.2) | collective-permute-done | bytes 266272 | tf_op jit(solution)/shard_map/ppermute | solution.py:285
  11.2 0.3 collective-permute-done.1.refs_2_
  11.5 1.8 %collective-permute-start.3 = (f32[32,8,128]{2,1,0:T(8,128)S(1)}, f32[32,8,128]{2,1,0:T(8,128)S(1)}, u32[]{:S(2)}, u32[]{:S(2)}) collective-permute-start(f32[32,8,128]{2,1,0:T(8,128)S(1)} %get-tuple-element.82), channel_id=1, source_target_pairs={{0,2},{1,5},{2,0},{3,7},{4,6},{5,1},{6,4},{7,3},{8,10},{9,13},{10,... | collective-permute-start | bytes 393224 | tf_op jit(solution)/shard_map/ppermute | solution.py:285
  13.4 1.6 %lagged_kernel.1 = (f32[8,768]{1,0:T(8,128)S(1)}, f32[8,128]{1,0:T(8,128)S(1)}) custom-call(s32[1]{0:T(128)} %bitcast.refs_0_, bf16[256,1024]{1,0:T(8,128)(2,1)S(1)} %get-tuple-element.65.refs_4_.refs_1_, bf16[256,1024]{1,0:T(8,128)(2,1)S(1)} %get-tuple-element.66.refs_5_.refs_2_, ...), custom_call_target="tpu_custom_call", output_to_operand_aliasing={{1}: (8, {})} | custom-call | flops 805306368 | tf_op jit(solution)/shard_map/lagged_kernel/pallas_call | solution.py:64
  15.0 1.3 %collective-permute-done.4.refs_2_ = f32[33,8,128]{2,1,0:T(8,128)S(1)} collective-permute-done((f32[33,8,128]{2,1,0:T(8,128)S(1)}, f32[33,8,128]{2,1,0:T(8,128)S(1)}, u32[]{:S(2)}, u32[]{:S(2)}) %collective-permute-start.4) | collective-permute-done | bytes 135200 | tf_op jit(solution)/shard_map/ppermute | solution.py:285
  16.3 0.3 collective-permute-start.7
  16.5 1.1 %collective-permute-done.3.refs_2_ = f32[32,8,128]{2,1,0:T(8,128)S(1)} collective-permute-done((f32[32,8,128]{2,1,0:T(8,128)S(1)}, f32[32,8,128]{2,1,0:T(8,128)S(1)}, u32[]{:S(2)}, u32[]{:S(2)}) %collective-permute-start.3) | collective-permute-done | bytes 131104 | tf_op jit(solution)/shard_map/ppermute | solution.py:285
  17.7 0.8 %collective-permute-start.5 = (f32[16,8,128]{2,1,0:T(8,128)S(1)}, f32[16,8,128]{2,1,0:T(8,128)S(1)}, u32[]{:S(2)}, u32[]{:S(2)}) collective-permute-start(f32[16,8,128]{2,1,0:T(8,128)S(1)} %get-tuple-element.92), channel_id=1, source_target_pairs={{0,4},{1,3},{2,6},{3,1},{4,0},{5,7},{6,2},{7,5},{8,12},{9,11},{10,... | collective-permute-start | bytes 196616 | tf_op jit(solution)/shard_map/ppermute | solution.py:285
  18.4 1.9 %collective-permute-start.6 = (f32[8,768]{1,0:T(8,128)S(1)}, f32[8,768]{1,0:T(8,128)S(1)}, u32[]{:S(2)}, u32[]{:S(2)}) collective-permute-start(f32[8,768]{1,0:T(8,128)S(1)} %get-tuple-element.93.refs_1_), channel_id=1, source_target_pairs={{0,16},{16,0},{1,17},{17,1},{2,18},{18,2},{3,19},{19,3},{4,20},{20... | collective-permute-start | bytes 73736 | tf_op jit(solution)/shard_map/ppermute | solution.py:341
  20.6 1.5 %collective-permute-start.9 = (f32[18,8,128]{2,1,0:T(8,128)S(1)}, f32[18,8,128]{2,1,0:T(8,128)S(1)}, u32[]{:S(2)}, u32[]{:S(2)}) collective-permute-start(f32[18,8,128]{2,1,0:T(8,128)S(1)} %get-tuple-element.101.refs_1_), channel_id=1, source_target_pairs={{0,8},{1,9},{2,10},{3,11},{4,12},{5,13},{6,14},{7,15},{8,0},{9,1},... | collective-permute-start | bytes 221192 | tf_op jit(solution)/shard_map/ppermute | solution.py:285
  22.3 0.3 loads_kernel.1
  22.6 2.2 %collective-permute-start.8 = (f32[17,8,128]{2,1,0:T(8,128)S(1)}, f32[17,8,128]{2,1,0:T(8,128)S(1)}, u32[]{:S(2)}, u32[]{:S(2)}) collective-permute-start(f32[17,8,128]{2,1,0:T(8,128)S(1)} %get-tuple-element.100.refs_1_), channel_id=1, source_target_pairs={{0,8},{1,9},{2,10},{3,11},{4,12},{5,13},{6,14},{7,15},{8,0},{9,1},... | collective-permute-start | bytes 208904 | tf_op jit(solution)/shard_map/ppermute | solution.py:285
  24.7 2.7 %collective-permute-done.9.refs_2_ = f32[18,8,128]{2,1,0:T(8,128)S(1)} collective-permute-done((f32[18,8,128]{2,1,0:T(8,128)S(1)}, f32[18,8,128]{2,1,0:T(8,128)S(1)}, u32[]{:S(2)}, u32[]{:S(2)}) %collective-permute-start.9) | collective-permute-done | bytes 73760 | tf_op jit(solution)/shard_map/ppermute | solution.py:285
  27.5 1.4 %collective-permute-done.8.refs_2_ = f32[17,8,128]{2,1,0:T(8,128)S(1)} collective-permute-done((f32[17,8,128]{2,1,0:T(8,128)S(1)}, f32[17,8,128]{2,1,0:T(8,128)S(1)}, u32[]{:S(2)}, u32[]{:S(2)}) %collective-permute-start.8) | collective-permute-done | bytes 69664 | tf_op jit(solution)/shard_map/ppermute | solution.py:285
  28.9 0.7 %collective-permute-start.10 = (f32[17,8,128]{2,1,0:T(8,128)S(1)}, f32[17,8,128]{2,1,0:T(8,128)S(1)}, u32[]{:S(2)}, u32[]{:S(2)}) collective-permute-start(f32[17,8,128]{2,1,0:T(8,128)S(1)} %get-tuple-element.105.refs_1_), channel_id=1, source_target_pairs={{0,4},{1,3},{2,6},{3,1},{4,0},{5,7},{6,2},{7,5},{8,12},{9,11},{10,... | collective-permute-start | bytes 208904 | tf_op jit(solution)/shard_map/ppermute | solution.py:285
  29.6 2.2 %collective-permute-done.11.refs_2_ = f32[18,8,128]{2,1,0:T(8,128)S(1)} collective-permute-done((f32[18,8,128]{2,1,0:T(8,128)S(1)}, f32[18,8,128]{2,1,0:T(8,128)S(1)}, u32[]{:S(2)}, u32[]{:S(2)}) %collective-permute-start.11) | collective-permute-done | bytes 73760 | tf_op jit(solution)/shard_map/ppermute | solution.py:285
  31.8 1.5 %collective-permute-start.13 = (f32[34,8,128]{2,1,0:T(8,128)S(1)}, f32[34,8,128]{2,1,0:T(8,128)S(1)}, u32[]{:S(2)}, u32[]{:S(2)}) collective-permute-start(f32[34,8,128]{2,1,0:T(8,128)S(1)} %get-tuple-element.110.refs_1_), channel_id=1, source_target_pairs={{0,2},{1,5},{2,0},{3,7},{4,6},{5,1},{6,4},{7,3},{8,10},{9,13},{10,... | collective-permute-start | bytes 417800 | tf_op jit(solution)/shard_map/ppermute | solution.py:285
  33.4 0.6 %collective-permute-done.10.refs_2_ = f32[17,8,128]{2,1,0:T(8,128)S(1)} collective-permute-done((f32[17,8,128]{2,1,0:T(8,128)S(1)}, f32[17,8,128]{2,1,0:T(8,128)S(1)}, u32[]{:S(2)}, u32[]{:S(2)}) %collective-permute-start.10) | collective-permute-done | bytes 69664 | tf_op jit(solution)/shard_map/ppermute | solution.py:285
  34.0 1.2 %collective-permute-start.12 = (f32[33,8,128]{2,1,0:T(8,128)S(1)}, f32[33,8,128]{2,1,0:T(8,128)S(1)}, u32[]{:S(2)}, u32[]{:S(2)}) collective-permute-start(f32[33,8,128]{2,1,0:T(8,128)S(1)} %get-tuple-element.109.refs_1_), channel_id=1, source_target_pairs={{0,2},{1,5},{2,0},{3,7},{4,6},{5,1},{6,4},{7,3},{8,10},{9,13},{10,... | collective-permute-start | bytes 405512 | tf_op jit(solution)/shard_map/ppermute | solution.py:285
  35.1 1.8 %collective-permute-done.13.refs_2_ = f32[34,8,128]{2,1,0:T(8,128)S(1)} collective-permute-done((f32[34,8,128]{2,1,0:T(8,128)S(1)}, f32[34,8,128]{2,1,0:T(8,128)S(1)}, u32[]{:S(2)}, u32[]{:S(2)}) %collective-permute-start.13) | collective-permute-done | bytes 139296 | tf_op jit(solution)/shard_map/ppermute | solution.py:285
  37.1 0.7 %store_kernel.3 = (f32[256,8,128]{2,1,0:T(8,128)}, f32[8,128]{1,0:T(8,128)S(1)}) custom-call(s32[1]{0:T(128)} %bitcast.refs_0_, f32[66,8,128]{2,1,0:T(8,128)S(1)} %get-tuple-element.112.refs_1_, f32[8,128]{1,0:T(8,128)S(1)} %get-tuple-element.113.refs_2_), custom_call_target="tpu_custom_call", output_to_operand_aliasing={{1}: (2, {})} | custom-call | tf_op jit(solution)/shard_map/store_kernel/pallas_call | solution.py:64
  37.8 1.2 %collective-permute-done.12.refs_2_ = f32[33,8,128]{2,1,0:T(8,128)S(1)} collective-permute-done((f32[33,8,128]{2,1,0:T(8,128)S(1)}, f32[33,8,128]{2,1,0:T(8,128)S(1)}, u32[]{:S(2)}, u32[]{:S(2)}) %collective-permute-start.12) | collective-permute-done | bytes 135200 | tf_op jit(solution)/shard_map/ppermute | solution.py:285
  39.2 0.8 %store_kernel.4 = (f32[256,8,128]{2,1,0:T(8,128)}, f32[8,128]{1,0:T(8,128)S(1)}) custom-call(s32[1]{0:T(128)} %bitcast.refs_0_, f32[66,8,128]{2,1,0:T(8,128)S(1)} %collective-permute-done.15.refs_1_, f32[65,8,128]{2,1,0:T(8,128)S(1)} %get-tuple-element.115.refs_2_, ...), custom_call_target="tpu_custom_call", output_to_operand_aliasing={{0}: (3, {}), {1}: (4, {})} | custom-call | tf_op jit(solution)/shard_map/store_kernel/pallas_call | solution.py:64
  40.0 0.7 %collective-permute-done.14.refs_1_ = f32[65,8,128]{2,1,0:T(8,128)S(1)} collective-permute-done((f32[65,8,128]{2,1,0:T(8,128)S(1)}, f32[65,8,128]{2,1,0:T(8,128)S(1)}, u32[]{:S(2)}, u32[]{:S(2)}) %collective-permute-start.14) | collective-permute-done | bytes 266272 | tf_op jit(solution)/shard_map/ppermute | solution.py:285
  40.7 0.7 %store_kernel.5 = (f32[256,8,128]{2,1,0:T(8,128)}, f32[8,512]{1,0:T(8,128)}, f32[8,128]{1,0:T(8,128)S(1)}) custom-call(s32[1]{0:T(128)} %bitcast.refs_0_, f32[65,8,128]{2,1,0:T(8,128)S(1)} %collective-permute-done.14.refs_1_, f32[8,512]{1,0:T(8,128)S(1)} %get-tuple-element.116.refs_2_, ...), custom_call_target="tpu_custom_call", output_to_operand_aliasing={{0}: (4, {}), {2}: (5, {})} | custom-call | tf_op jit(solution)/shard_map/store_kernel/pallas_call | solution.py:64
  (27 shorter events, 1.2 us)
Async XLA Ops:
  0.6 0.7 %copy-start.2 = (f32[8,512]{1,0:T(8,128)S(1)}, f32[8,512]{1,0:T(8,128)}, u32[]{:S(2)}) copy-start(f32[8,512]{1,0:T(8,128)} %refs_3_.5) | copy-start | bytes 49156
  0.6 1.2 %copy-start = (f32[256,8,128]{2,1,0:T(8,128)S(1)}, f32[256,8,128]{2,1,0:T(8,128)}, u32[]{:S(2)}) copy-start(f32[256,8,128]{2,1,0:T(8,128)} %refs_4_.3) | copy-start | bytes 3145732
  0.7 1.4 %copy-start.1 = (f32[256,512]{1,0:T(8,128)S(1)}, f32[256,512]{1,0:T(8,128)}, u32[]{:S(2)}) copy-start(f32[256,512]{1,0:T(8,128)} %refs_2_.1) | copy-start | bytes 1572868
  1.4 6.9 %collective-permute-start = (f32[8,512]{1,0:T(8,128)S(1)}, f32[8,512]{1,0:T(8,128)S(1)}, u32[]{:S(2)}, u32[]{:S(2)}) collective-permute-start(f32[8,512]{1,0:T(8,128)S(1)} %copy-done.2), channel_id=1, source_target_pairs={{0,1},{1,2},{2,3},{3,4},{4,5},{5,6},{6,7},{7,8},{8,9},{9,10},{10,1... | collective-permute-start | bytes 49160 | tf_op jit(solution)/shard_map/ppermute | solution.py:293
  9.5 1.6 %collective-permute-start.2 = (f32[65,8,128]{2,1,0:T(8,128)S(1)}, f32[65,8,128]{2,1,0:T(8,128)S(1)}, u32[]{:S(2)}, u32[]{:S(2)}) collective-permute-start(f32[65,8,128]{2,1,0:T(8,128)S(1)} %bitcast.9), channel_id=1, source_target_pairs={{0,1},{1,0},{2,3},{3,2},{4,5},{5,4},{6,7},{7,6},{8,9},{9,8},{10,11... | collective-permute-start | bytes 798728 | tf_op jit(solution)/shard_map/ppermute | solution.py:285
  9.6 1.9 %collective-permute-start.1 = (f32[64,8,128]{2,1,0:T(8,128)S(1)}, f32[64,8,128]{2,1,0:T(8,128)S(1)}, u32[]{:S(2)}, u32[]{:S(2)}) collective-permute-start(f32[64,8,128]{2,1,0:T(8,128)S(1)} %bitcast.10), channel_id=1, source_target_pairs={{0,1},{1,0},{2,3},{3,2},{4,5},{5,4},{6,7},{7,6},{8,9},{9,8},{10,11... | collective-permute-start | bytes 786440 | tf_op jit(solution)/shard_map/ppermute | solution.py:285
  11.2 5.1 %collective-permute-start.4 = (f32[33,8,128]{2,1,0:T(8,128)S(1)}, f32[33,8,128]{2,1,0:T(8,128)S(1)}, u32[]{:S(2)}, u32[]{:S(2)}) collective-permute-start(f32[33,8,128]{2,1,0:T(8,128)S(1)} %get-tuple-element.84), channel_id=1, source_target_pairs={{0,2},{1,5},{2,0},{3,7},{4,6},{5,1},{6,4},{7,3},{8,10},{9,13},{10,... | collective-permute-start | bytes 405512 | tf_op jit(solution)/shard_map/ppermute | solution.py:285
  11.5 6.1 %collective-permute-start.3 = (f32[32,8,128]{2,1,0:T(8,128)S(1)}, f32[32,8,128]{2,1,0:T(8,128)S(1)}, u32[]{:S(2)}, u32[]{:S(2)}) collective-permute-start(f32[32,8,128]{2,1,0:T(8,128)S(1)} %get-tuple-element.82), channel_id=1, source_target_pairs={{0,2},{1,5},{2,0},{3,7},{4,6},{5,1},{6,4},{7,3},{8,10},{9,13},{10,... | collective-permute-start | bytes 393224 | tf_op jit(solution)/shard_map/ppermute | solution.py:285
  16.3 4.4 %collective-permute-start.7 = (f32[17,8,128]{2,1,0:T(8,128)S(1)}, f32[17,8,128]{2,1,0:T(8,128)S(1)}, u32[]{:S(2)}, u32[]{:S(2)}) collective-permute-start(f32[17,8,128]{2,1,0:T(8,128)S(1)} %get-tuple-element.95), channel_id=1, source_target_pairs={{0,4},{1,3},{2,6},{3,1},{4,0},{5,7},{6,2},{7,5},{8,12},{9,11},{10,... | collective-permute-start | bytes 208904 | tf_op jit(solution)/shard_map/ppermute | solution.py:285
  17.7 4.9 %collective-permute-start.5 = (f32[16,8,128]{2,1,0:T(8,128)S(1)}, f32[16,8,128]{2,1,0:T(8,128)S(1)}, u32[]{:S(2)}, u32[]{:S(2)}) collective-permute-start(f32[16,8,128]{2,1,0:T(8,128)S(1)} %get-tuple-element.92), channel_id=1, source_target_pairs={{0,4},{1,3},{2,6},{3,1},{4,0},{5,7},{6,2},{7,5},{8,12},{9,11},{10,... | collective-permute-start | bytes 196616 | tf_op jit(solution)/shard_map/ppermute | solution.py:285
  18.4 3.8 %collective-permute-start.6 = (f32[8,768]{1,0:T(8,128)S(1)}, f32[8,768]{1,0:T(8,128)S(1)}, u32[]{:S(2)}, u32[]{:S(2)}) collective-permute-start(f32[8,768]{1,0:T(8,128)S(1)} %get-tuple-element.93.refs_1_), channel_id=1, source_target_pairs={{0,16},{16,0},{1,17},{17,1},{2,18},{18,2},{3,19},{19,3},{4,20},{20... | collective-permute-start | bytes 73736 | tf_op jit(solution)/shard_map/ppermute | solution.py:341
  20.6 6.7 %collective-permute-start.9 = (f32[18,8,128]{2,1,0:T(8,128)S(1)}, f32[18,8,128]{2,1,0:T(8,128)S(1)}, u32[]{:S(2)}, u32[]{:S(2)}) collective-permute-start(f32[18,8,128]{2,1,0:T(8,128)S(1)} %get-tuple-element.101.refs_1_), channel_id=1, source_target_pairs={{0,8},{1,9},{2,10},{3,11},{4,12},{5,13},{6,14},{7,15},{8,0},{9,1},... | collective-permute-start | bytes 221192 | tf_op jit(solution)/shard_map/ppermute | solution.py:285
  22.6 6.3 %collective-permute-start.8 = (f32[17,8,128]{2,1,0:T(8,128)S(1)}, f32[17,8,128]{2,1,0:T(8,128)S(1)}, u32[]{:S(2)}, u32[]{:S(2)}) collective-permute-start(f32[17,8,128]{2,1,0:T(8,128)S(1)} %get-tuple-element.100.refs_1_), channel_id=1, source_target_pairs={{0,8},{1,9},{2,10},{3,11},{4,12},{5,13},{6,14},{7,15},{8,0},{9,1},... | collective-permute-start | bytes 208904 | tf_op jit(solution)/shard_map/ppermute | solution.py:285
  27.4 4.4 %collective-permute-start.11 = (f32[18,8,128]{2,1,0:T(8,128)S(1)}, f32[18,8,128]{2,1,0:T(8,128)S(1)}, u32[]{:S(2)}, u32[]{:S(2)}) collective-permute-start(f32[18,8,128]{2,1,0:T(8,128)S(1)} %get-tuple-element.106.refs_1_), channel_id=1, source_target_pairs={{0,4},{1,3},{2,6},{3,1},{4,0},{5,7},{6,2},{7,5},{8,12},{9,11},{10,... | collective-permute-start | bytes 221192 | tf_op jit(solution)/shard_map/ppermute | solution.py:285
  28.9 5.0 %collective-permute-start.10 = (f32[17,8,128]{2,1,0:T(8,128)S(1)}, f32[17,8,128]{2,1,0:T(8,128)S(1)}, u32[]{:S(2)}, u32[]{:S(2)}) collective-permute-start(f32[17,8,128]{2,1,0:T(8,128)S(1)} %get-tuple-element.105.refs_1_), channel_id=1, source_target_pairs={{0,4},{1,3},{2,6},{3,1},{4,0},{5,7},{6,2},{7,5},{8,12},{9,11},{10,... | collective-permute-start | bytes 208904 | tf_op jit(solution)/shard_map/ppermute | solution.py:285
  31.8 5.1 %collective-permute-start.13 = (f32[34,8,128]{2,1,0:T(8,128)S(1)}, f32[34,8,128]{2,1,0:T(8,128)S(1)}, u32[]{:S(2)}, u32[]{:S(2)}) collective-permute-start(f32[34,8,128]{2,1,0:T(8,128)S(1)} %get-tuple-element.110.refs_1_), channel_id=1, source_target_pairs={{0,2},{1,5},{2,0},{3,7},{4,6},{5,1},{6,4},{7,3},{8,10},{9,13},{10,... | collective-permute-start | bytes 417800 | tf_op jit(solution)/shard_map/ppermute | solution.py:285
  34.0 5.1 %collective-permute-start.12 = (f32[33,8,128]{2,1,0:T(8,128)S(1)}, f32[33,8,128]{2,1,0:T(8,128)S(1)}, u32[]{:S(2)}, u32[]{:S(2)}) collective-permute-start(f32[33,8,128]{2,1,0:T(8,128)S(1)} %get-tuple-element.109.refs_1_), channel_id=1, source_target_pairs={{0,2},{1,5},{2,0},{3,7},{4,6},{5,1},{6,4},{7,3},{8,10},{9,13},{10,... | collective-permute-start | bytes 405512 | tf_op jit(solution)/shard_map/ppermute | solution.py:285
  37.0 2.2 %collective-permute-start.15 = (f32[66,8,128]{2,1,0:T(8,128)S(1)}, f32[66,8,128]{2,1,0:T(8,128)S(1)}, u32[]{:S(2)}, u32[]{:S(2)}) collective-permute-start(f32[66,8,128]{2,1,0:T(8,128)S(1)} %get-tuple-element.112.refs_1_), channel_id=1, source_target_pairs={{0,1},{1,0},{2,3},{3,2},{4,5},{5,4},{6,7},{7,6},{8,9},{9,8},{10,11... | collective-permute-start | bytes 811016 | tf_op jit(solution)/shard_map/ppermute | solution.py:285
  39.1 1.6 %collective-permute-start.14 = (f32[65,8,128]{2,1,0:T(8,128)S(1)}, f32[65,8,128]{2,1,0:T(8,128)S(1)}, u32[]{:S(2)}, u32[]{:S(2)}) collective-permute-start(f32[65,8,128]{2,1,0:T(8,128)S(1)} %get-tuple-element.115.refs_2_), channel_id=1, source_target_pairs={{0,1},{1,0},{2,3},{3,2},{4,5},{5,4},{6,7},{7,6},{8,9},{9,8},{10,11... | collective-permute-start | bytes 798728 | tf_op jit(solution)/shard_map/ppermute | solution.py:285

commit v6 on v5

--- a/solution.py
+++ b/solution.py
@@ -40,7 +40,7 @@
 
 
 def order(core, steps):
-    return [0, 2, 1, *range(3, steps)] if core else list(range(steps))
+    return [0, *range(3, steps), 1, 2] if core else list(range(steps))
 
 
 class Chain:

time: 41.6 us -> 40.7 us (0.978)
  waiting for transfers between devices: 18 us -> 15.5 us
  starting transfers between devices: 13.2 us -> 14.8 us
    ppermute x14, waiting for transfers between devices: 14.2 us -> 11.6 us  [swap(): lax.ppermute(x, 'tm', [(i, i ^ 1 << order(i & 1, steps)[step]) for i in r...]
    ppermute x14, starting transfers between devices: 10.8 us -> 12.4 us  [swap(): lax.ppermute(x, 'tm', [(i, i ^ 1 << order(i & 1, steps)[step]) for i in r...]
where the time goes in v6:
time: 40.7 us; the launch traced here: 40.5 us
  waiting for transfers between devices  15.5 us (38%)
  starting transfers between devices  14.8 us (36%)
  Pallas kernels  8.54 us (21%)
  local copies, waits for them, and re-layouts  0.89 us (2%)
  between operations  0.79 us (2%)
    ppermute x14, starting transfers between devices, swap(): lax.ppermute(x, 'tm', [(i, i ^ 1 << order(i & 1, steps)[step]) for i in r...  12.4 us
    ppermute x14, waiting for transfers between devices, swap(): lax.ppermute(x, 'tm', [(i, i ^ 1 << order(i & 1, steps)[step]) for i in r...  11.6 us
    pallas_call x21, Pallas kernels, __call__(): pl.pallas_call(run, out_shape=[*out_shapes, *(jax.ShapeDtypeStruct(t.shap...  8.54 us
    ppermute x1, waiting for transfers between devices, body(): lax.ppermute(sent, 'tm', [(i, (i + 1) % ranks) for i in range(ranks)])  3.7 us
    ppermute x1, starting transfers between devices, body(): lax.ppermute(part, 'neur', [(i, i ^ 1 << flip) for i in range(groups)])  1.94 us
    unnamed x6, local copies, waits for them, and re-layouts  0.89 us
  transfers between devices with their start and end apart: 16, of which 14 were waited for; matrix products, arithmetic and copies ran while one was open for 0% of the time, Pallas kernels for 16%

profile of v6, /device:TPU:0, one launch (start us, length us, event | category | flops | bytes accessed | tf_op | source)
XLA Modules:
  0.0 40.5 jit_solution(12385885184458708640)
XLA Ops:
  0.7 0.7 %copy-done.2 = f32[8,512]{1,0:T(8,128)S(1)} copy-done((f32[8,512]{1,0:T(8,128)S(1)}, f32[8,512]{1,0:T(8,128)}, u32[]{:S(2)}) %copy-start.2) | copy-done | bytes 16408
  1.4 0.5 %collective-permute-start = (f32[8,512]{1,0:T(8,128)S(1)}, f32[8,512]{1,0:T(8,128)S(1)}, u32[]{:S(2)}, u32[]{:S(2)}) collective-permute-start(f32[8,512]{1,0:T(8,128)S(1)} %copy-done.2), channel_id=1, source_target_pairs={{0,1},{1,2},{2,3},{3,4},{4,5},{5,6},{6,7},{7,8},{8,9},{9,10},{10,1... | collective-permute-start | bytes 49160 | tf_op jit(solution)/shard_map/ppermute | solution.py:293
  2.0 2.5 %body_kernel.1 = (bf16[256,1024]{1,0:T(8,128)(2,1)S(1)}, bf16[256,1024]{1,0:T(8,128)(2,1)S(1)}, bf16[256,384]{1,0:T(8,128)(2,1)S(1)}, bf16[256,384]{1,0:T(8,128)...) custom-call(s32[1]{0:T(128)} %bitcast.refs_0_, ...), custom_call_target="tpu_custom_call", output_to_operand_aliasing={{6}: (4, {})} | custom-call | flops 1610612736 | tf_op jit(solution)/shard_map/body_kernel/pallas_call | solution.py:64
  4.5 3.7 %collective-permute-done.refs_1_ = f32[8,512]{1,0:T(8,128)S(1)} collective-permute-done((f32[8,512]{1,0:T(8,128)S(1)}, f32[8,512]{1,0:T(8,128)S(1)}, u32[]{:S(2)}, u32[]{:S(2)}) %collective-permute-start) | collective-permute-done | bytes 16416 | tf_op jit(solution)/shard_map/ppermute | solution.py:293
  8.2 1.3 %head_kernel.1 = (f32[520,128]{1,0:T(8,128)S(1)}, f32[512,128]{1,0:T(8,128)S(1)}, bf16[256,128]{1,0:T(8,128)(2,1)S(1)}, bf16[256,128]{1,0:T(8,128)(2,1)S(1)}, bf...) custom-call(s32[1]{0:T(128)} %bitcast.refs_0_, ...), custom_call_target="tpu_custom_call", output_to_operand_aliasing={{7}: (7, {})} | custom-call | tf_op jit(solution)/shard_map/head_kernel/pallas_call | solution.py:64
  9.6 0.5 %collective-permute-start.1 = (f32[64,8,128]{2,1,0:T(8,128)S(1)}, f32[64,8,128]{2,1,0:T(8,128)S(1)}, u32[]{:S(2)}, u32[]{:S(2)}) collective-permute-start(f32[64,8,128]{2,1,0:T(8,128)S(1)} %bitcast.10), channel_id=1, source_target_pairs={{0,1},{1,0},{2,3},{3,2},{4,5},{5,4},{6,7},{7,6},{8,9},{9,8},{10,11... | collective-permute-start | bytes 786440 | tf_op jit(solution)/shard_map/ppermute | solution.py:285
  10.1 0.4 home_kernel.1
  10.5 0.6 %collective-permute-done.2.refs_2_ = f32[65,8,128]{2,1,0:T(8,128)S(1)} collective-permute-done((f32[65,8,128]{2,1,0:T(8,128)S(1)}, f32[65,8,128]{2,1,0:T(8,128)S(1)}, u32[]{:S(2)}, u32[]{:S(2)}) %collective-permute-start.2) | collective-permute-done | bytes 266272 | tf_op jit(solution)/shard_map/ppermute | solution.py:285
  11.5 1.8 %collective-permute-start.3 = (f32[32,8,128]{2,1,0:T(8,128)S(1)}, f32[32,8,128]{2,1,0:T(8,128)S(1)}, u32[]{:S(2)}, u32[]{:S(2)}) collective-permute-start(f32[32,8,128]{2,1,0:T(8,128)S(1)} %get-tuple-element.82), channel_id=1, source_target_pairs={{0,2},{1,9},{2,0},{3,11},{4,6},{5,13},{6,4},{7,15},{8,10},{9,1},{1... | collective-permute-start | bytes 393224 | tf_op jit(solution)/shard_map/ppermute | solution.py:285
  13.4 1.6 %lagged_kernel.1 = (f32[8,768]{1,0:T(8,128)S(1)}, f32[8,128]{1,0:T(8,128)S(1)}) custom-call(s32[1]{0:T(128)} %bitcast.refs_0_, bf16[256,1024]{1,0:T(8,128)(2,1)S(1)} %get-tuple-element.65.refs_4_.refs_1_, bf16[256,1024]{1,0:T(8,128)(2,1)S(1)} %get-tuple-element.66.refs_5_.refs_2_, ...), custom_call_target="tpu_custom_call", output_to_operand_aliasing={{1}: (8, {})} | custom-call | flops 805306368 | tf_op jit(solution)/shard_map/lagged_kernel/pallas_call | solution.py:64
  15.0 1.3 %collective-permute-done.4.refs_2_ = f32[33,8,128]{2,1,0:T(8,128)S(1)} collective-permute-done((f32[33,8,128]{2,1,0:T(8,128)S(1)}, f32[33,8,128]{2,1,0:T(8,128)S(1)}, u32[]{:S(2)}, u32[]{:S(2)}) %collective-permute-start.4) | collective-permute-done | bytes 135200 | tf_op jit(solution)/shard_map/ppermute | solution.py:285
  16.3 0.3 collective-permute-start.7
  16.5 1.1 %collective-permute-done.3.refs_2_ = f32[32,8,128]{2,1,0:T(8,128)S(1)} collective-permute-done((f32[32,8,128]{2,1,0:T(8,128)S(1)}, f32[32,8,128]{2,1,0:T(8,128)S(1)}, u32[]{:S(2)}, u32[]{:S(2)}) %collective-permute-start.3) | collective-permute-done | bytes 131104 | tf_op jit(solution)/shard_map/ppermute | solution.py:285
  17.7 0.8 %collective-permute-start.5 = (f32[16,8,128]{2,1,0:T(8,128)S(1)}, f32[16,8,128]{2,1,0:T(8,128)S(1)}, u32[]{:S(2)}, u32[]{:S(2)}) collective-permute-start(f32[16,8,128]{2,1,0:T(8,128)S(1)} %get-tuple-element.92), channel_id=1, source_target_pairs={{0,4},{1,3},{2,6},{3,1},{4,0},{5,7},{6,2},{7,5},{8,12},{9,11},{10,... | collective-permute-start | bytes 196616 | tf_op jit(solution)/shard_map/ppermute | solution.py:285
  18.4 1.9 %collective-permute-start.6 = (f32[8,768]{1,0:T(8,128)S(1)}, f32[8,768]{1,0:T(8,128)S(1)}, u32[]{:S(2)}, u32[]{:S(2)}) collective-permute-start(f32[8,768]{1,0:T(8,128)S(1)} %get-tuple-element.93.refs_1_), channel_id=1, source_target_pairs={{0,16},{16,0},{1,17},{17,1},{2,18},{18,2},{3,19},{19,3},{4,20},{20... | collective-permute-start | bytes 73736 | tf_op jit(solution)/shard_map/ppermute | solution.py:341
  20.4 0.6 %collective-permute-done.7.refs_2_ = f32[17,8,128]{2,1,0:T(8,128)S(1)} collective-permute-done((f32[17,8,128]{2,1,0:T(8,128)S(1)}, f32[17,8,128]{2,1,0:T(8,128)S(1)}, u32[]{:S(2)}, u32[]{:S(2)}) %collective-permute-start.7) | collective-permute-done | bytes 69664 | tf_op jit(solution)/shard_map/ppermute | solution.py:285
  21.0 1.1 %collective-permute-start.9 = (f32[18,8,128]{2,1,0:T(8,128)S(1)}, f32[18,8,128]{2,1,0:T(8,128)S(1)}, u32[]{:S(2)}, u32[]{:S(2)}) collective-permute-start(f32[18,8,128]{2,1,0:T(8,128)S(1)} %get-tuple-element.101.refs_1_), channel_id=1, source_target_pairs={{0,8},{1,5},{2,10},{3,7},{4,12},{5,1},{6,14},{7,3},{8,0},{9,13},{1... | collective-permute-start | bytes 221192 | tf_op jit(solution)/shard_map/ppermute | solution.py:285
  22.6 2.2 %collective-permute-start.8 = (f32[17,8,128]{2,1,0:T(8,128)S(1)}, f32[17,8,128]{2,1,0:T(8,128)S(1)}, u32[]{:S(2)}, u32[]{:S(2)}) collective-permute-start(f32[17,8,128]{2,1,0:T(8,128)S(1)} %get-tuple-element.100.refs_1_), channel_id=1, source_target_pairs={{0,8},{1,5},{2,10},{3,7},{4,12},{5,1},{6,14},{7,3},{8,0},{9,13},{1... | collective-permute-start | bytes 208904 | tf_op jit(solution)/shard_map/ppermute | solution.py:285
  24.7 2.2 %collective-permute-done.9.refs_2_ = f32[18,8,128]{2,1,0:T(8,128)S(1)} collective-permute-done((f32[18,8,128]{2,1,0:T(8,128)S(1)}, f32[18,8,128]{2,1,0:T(8,128)S(1)}, u32[]{:S(2)}, u32[]{:S(2)}) %collective-permute-start.9) | collective-permute-done | bytes 73760 | tf_op jit(solution)/shard_map/ppermute | solution.py:285
  26.9 0.9 %collective-permute-start.11 = (f32[18,8,128]{2,1,0:T(8,128)S(1)}, f32[18,8,128]{2,1,0:T(8,128)S(1)}, u32[]{:S(2)}, u32[]{:S(2)}) collective-permute-start(f32[18,8,128]{2,1,0:T(8,128)S(1)} %get-tuple-element.106.refs_1_), channel_id=1, source_target_pairs={{0,4},{1,3},{2,6},{3,1},{4,0},{5,7},{6,2},{7,5},{8,12},{9,11},{10,... | collective-permute-start | bytes 221192 | tf_op jit(solution)/shard_map/ppermute | solution.py:285
  28.0 1.8 %collective-permute-start.10 = (f32[17,8,128]{2,1,0:T(8,128)S(1)}, f32[17,8,128]{2,1,0:T(8,128)S(1)}, u32[]{:S(2)}, u32[]{:S(2)}) collective-permute-start(f32[17,8,128]{2,1,0:T(8,128)S(1)} %get-tuple-element.105.refs_1_), channel_id=1, source_target_pairs={{0,4},{1,3},{2,6},{3,1},{4,0},{5,7},{6,2},{7,5},{8,12},{9,11},{10,... | collective-permute-start | bytes 208904 | tf_op jit(solution)/shard_map/ppermute | solution.py:285
  29.7 1.6 %collective-permute-done.11.refs_2_ = f32[18,8,128]{2,1,0:T(8,128)S(1)} collective-permute-done((f32[18,8,128]{2,1,0:T(8,128)S(1)}, f32[18,8,128]{2,1,0:T(8,128)S(1)}, u32[]{:S(2)}, u32[]{:S(2)}) %collective-permute-start.11) | collective-permute-done | bytes 73760 | tf_op jit(solution)/shard_map/ppermute | solution.py:285
  31.4 0.5 %collective-permute-start.13 = (f32[34,8,128]{2,1,0:T(8,128)S(1)}, f32[34,8,128]{2,1,0:T(8,128)S(1)}, u32[]{:S(2)}, u32[]{:S(2)}) collective-permute-start(f32[34,8,128]{2,1,0:T(8,128)S(1)} %get-tuple-element.110.refs_1_), channel_id=1, source_target_pairs={{0,2},{1,9},{2,0},{3,11},{4,6},{5,13},{6,4},{7,15},{8,10},{9,1},{1... | collective-permute-start | bytes 417800 | tf_op jit(solution)/shard_map/ppermute | solution.py:285
  31.9 0.5 %collective-permute-done.10.refs_2_ = f32[17,8,128]{2,1,0:T(8,128)S(1)} collective-permute-done((f32[17,8,128]{2,1,0:T(8,128)S(1)}, f32[17,8,128]{2,1,0:T(8,128)S(1)}, u32[]{:S(2)}, u32[]{:S(2)}) %collective-permute-start.10) | collective-permute-done | bytes 69664 | tf_op jit(solution)/shard_map/ppermute | solution.py:285
  32.4 1.2 %collective-permute-start.12 = (f32[33,8,128]{2,1,0:T(8,128)S(1)}, f32[33,8,128]{2,1,0:T(8,128)S(1)}, u32[]{:S(2)}, u32[]{:S(2)}) collective-permute-start(f32[33,8,128]{2,1,0:T(8,128)S(1)} %get-tuple-element.109.refs_1_), channel_id=1, source_target_pairs={{0,2},{1,9},{2,0},{3,11},{4,6},{5,13},{6,4},{7,15},{8,10},{9,1},{1... | collective-permute-start | bytes 405512 | tf_op jit(solution)/shard_map/ppermute | solution.py:285
  33.5 2.9 %collective-permute-done.13.refs_2_ = f32[34,8,128]{2,1,0:T(8,128)S(1)} collective-permute-done((f32[34,8,128]{2,1,0:T(8,128)S(1)}, f32[34,8,128]{2,1,0:T(8,128)S(1)}, u32[]{:S(2)}, u32[]{:S(2)}) %collective-permute-start.13) | collective-permute-done | bytes 139296 | tf_op jit(solution)/shard_map/ppermute | solution.py:285
  36.5 0.6 %collective-permute-start.15 = (f32[66,8,128]{2,1,0:T(8,128)S(1)}, f32[66,8,128]{2,1,0:T(8,128)S(1)}, u32[]{:S(2)}, u32[]{:S(2)}) collective-permute-start(f32[66,8,128]{2,1,0:T(8,128)S(1)} %get-tuple-element.112.refs_1_), channel_id=1, source_target_pairs={{0,1},{1,0},{2,3},{3,2},{4,5},{5,4},{6,7},{7,6},{8,9},{9,8},{10,11... | collective-permute-start | bytes 811016 | tf_op jit(solution)/shard_map/ppermute | solution.py:285
  37.1 0.7 %store_kernel.3 = (f32[256,8,128]{2,1,0:T(8,128)}, f32[8,128]{1,0:T(8,128)S(1)}) custom-call(s32[1]{0:T(128)} %bitcast.refs_0_, f32[66,8,128]{2,1,0:T(8,128)S(1)} %get-tuple-element.112.refs_1_, f32[8,128]{1,0:T(8,128)S(1)} %get-tuple-element.113.refs_2_), custom_call_target="tpu_custom_call", output_to_operand_aliasing={{1}: (2, {})} | custom-call | tf_op jit(solution)/shard_map/store_kernel/pallas_call | solution.py:64
  38.0 0.6 %collective-permute-start.14 = (f32[65,8,128]{2,1,0:T(8,128)S(1)}, f32[65,8,128]{2,1,0:T(8,128)S(1)}, u32[]{:S(2)}, u32[]{:S(2)}) collective-permute-start(f32[65,8,128]{2,1,0:T(8,128)S(1)} %get-tuple-element.115.refs_2_), channel_id=1, source_target_pairs={{0,1},{1,0},{2,3},{3,2},{4,5},{5,4},{6,7},{7,6},{8,9},{9,8},{10,11... | collective-permute-start | bytes 798728 | tf_op jit(solution)/shard_map/ppermute | solution.py:285
  38.6 0.8 %store_kernel.4 = (f32[256,8,128]{2,1,0:T(8,128)}, f32[8,128]{1,0:T(8,128)S(1)}) custom-call(s32[1]{0:T(128)} %bitcast.refs_0_, f32[66,8,128]{2,1,0:T(8,128)S(1)} %collective-permute-done.15.refs_1_, f32[65,8,128]{2,1,0:T(8,128)S(1)} %get-tuple-element.115.refs_2_, ...), custom_call_target="tpu_custom_call", output_to_operand_aliasing={{0}: (3, {}), {1}: (4, {})} | custom-call | tf_op jit(solution)/shard_map/store_kernel/pallas_call | solution.py:64
  39.4 0.3 collective-permute-done.14.refs_1_
  39.7 0.7 %store_kernel.5 = (f32[256,8,128]{2,1,0:T(8,128)}, f32[8,512]{1,0:T(8,128)}, f32[8,128]{1,0:T(8,128)S(1)}) custom-call(s32[1]{0:T(128)} %bitcast.refs_0_, f32[65,8,128]{2,1,0:T(8,128)S(1)} %collective-permute-done.14.refs_1_, f32[8,512]{1,0:T(8,128)S(1)} %get-tuple-element.116.refs_2_, ...), custom_call_target="tpu_custom_call", output_to_operand_aliasing={{0}: (4, {}), {2}: (5, {})} | custom-call | tf_op jit(solution)/shard_map/store_kernel/pallas_call | solution.py:64
  (27 shorter events, 1.5 us)
Async XLA Ops:
  0.6 0.7 %copy-start.2 = (f32[8,512]{1,0:T(8,128)S(1)}, f32[8,512]{1,0:T(8,128)}, u32[]{:S(2)}) copy-start(f32[8,512]{1,0:T(8,128)} %refs_3_.5) | copy-start | bytes 49156
  0.6 1.2 %copy-start = (f32[256,8,128]{2,1,0:T(8,128)S(1)}, f32[256,8,128]{2,1,0:T(8,128)}, u32[]{:S(2)}) copy-start(f32[256,8,128]{2,1,0:T(8,128)} %refs_4_.3) | copy-start | bytes 3145732
  0.7 1.4 %copy-start.1 = (f32[256,512]{1,0:T(8,128)S(1)}, f32[256,512]{1,0:T(8,128)}, u32[]{:S(2)}) copy-start(f32[256,512]{1,0:T(8,128)} %refs_2_.1) | copy-start | bytes 1572868
  1.4 6.9 %collective-permute-start = (f32[8,512]{1,0:T(8,128)S(1)}, f32[8,512]{1,0:T(8,128)S(1)}, u32[]{:S(2)}, u32[]{:S(2)}) collective-permute-start(f32[8,512]{1,0:T(8,128)S(1)} %copy-done.2), channel_id=1, source_target_pairs={{0,1},{1,2},{2,3},{3,4},{4,5},{5,6},{6,7},{7,8},{8,9},{9,10},{10,1... | collective-permute-start | bytes 49160 | tf_op jit(solution)/shard_map/ppermute | solution.py:293
  9.5 1.6 %collective-permute-start.2 = (f32[65,8,128]{2,1,0:T(8,128)S(1)}, f32[65,8,128]{2,1,0:T(8,128)S(1)}, u32[]{:S(2)}, u32[]{:S(2)}) collective-permute-start(f32[65,8,128]{2,1,0:T(8,128)S(1)} %bitcast.9), channel_id=1, source_target_pairs={{0,1},{1,0},{2,3},{3,2},{4,5},{5,4},{6,7},{7,6},{8,9},{9,8},{10,11... | collective-permute-start | bytes 798728 | tf_op jit(solution)/shard_map/ppermute | solution.py:285
  9.6 1.9 %collective-permute-start.1 = (f32[64,8,128]{2,1,0:T(8,128)S(1)}, f32[64,8,128]{2,1,0:T(8,128)S(1)}, u32[]{:S(2)}, u32[]{:S(2)}) collective-permute-start(f32[64,8,128]{2,1,0:T(8,128)S(1)} %bitcast.10), channel_id=1, source_target_pairs={{0,1},{1,0},{2,3},{3,2},{4,5},{5,4},{6,7},{7,6},{8,9},{9,8},{10,11... | collective-permute-start | bytes 786440 | tf_op jit(solution)/shard_map/ppermute | solution.py:285
  11.2 5.1 %collective-permute-start.4 = (f32[33,8,128]{2,1,0:T(8,128)S(1)}, f32[33,8,128]{2,1,0:T(8,128)S(1)}, u32[]{:S(2)}, u32[]{:S(2)}) collective-permute-start(f32[33,8,128]{2,1,0:T(8,128)S(1)} %get-tuple-element.84), channel_id=1, source_target_pairs={{0,2},{1,9},{2,0},{3,11},{4,6},{5,13},{6,4},{7,15},{8,10},{9,1},{1... | collective-permute-start | bytes 405512 | tf_op jit(solution)/shard_map/ppermute | solution.py:285
  11.5 6.1 %collective-permute-start.3 = (f32[32,8,128]{2,1,0:T(8,128)S(1)}, f32[32,8,128]{2,1,0:T(8,128)S(1)}, u32[]{:S(2)}, u32[]{:S(2)}) collective-permute-start(f32[32,8,128]{2,1,0:T(8,128)S(1)} %get-tuple-element.82), channel_id=1, source_target_pairs={{0,2},{1,9},{2,0},{3,11},{4,6},{5,13},{6,4},{7,15},{8,10},{9,1},{1... | collective-permute-start | bytes 393224 | tf_op jit(solution)/shard_map/ppermute | solution.py:285
  16.3 4.7 %collective-permute-start.7 = (f32[17,8,128]{2,1,0:T(8,128)S(1)}, f32[17,8,128]{2,1,0:T(8,128)S(1)}, u32[]{:S(2)}, u32[]{:S(2)}) collective-permute-start(f32[17,8,128]{2,1,0:T(8,128)S(1)} %get-tuple-element.95), channel_id=1, source_target_pairs={{0,4},{1,3},{2,6},{3,1},{4,0},{5,7},{6,2},{7,5},{8,12},{9,11},{10,... | collective-permute-start | bytes 208904 | tf_op jit(solution)/shard_map/ppermute | solution.py:285
  17.7 4.9 %collective-permute-start.5 = (f32[16,8,128]{2,1,0:T(8,128)S(1)}, f32[16,8,128]{2,1,0:T(8,128)S(1)}, u32[]{:S(2)}, u32[]{:S(2)}) collective-permute-start(f32[16,8,128]{2,1,0:T(8,128)S(1)} %get-tuple-element.92), channel_id=1, source_target_pairs={{0,4},{1,3},{2,6},{3,1},{4,0},{5,7},{6,2},{7,5},{8,12},{9,11},{10,... | collective-permute-start | bytes 196616 | tf_op jit(solution)/shard_map/ppermute | solution.py:285
  18.4 3.8 %collective-permute-start.6 = (f32[8,768]{1,0:T(8,128)S(1)}, f32[8,768]{1,0:T(8,128)S(1)}, u32[]{:S(2)}, u32[]{:S(2)}) collective-permute-start(f32[8,768]{1,0:T(8,128)S(1)} %get-tuple-element.93.refs_1_), channel_id=1, source_target_pairs={{0,16},{16,0},{1,17},{17,1},{2,18},{18,2},{3,19},{19,3},{4,20},{20... | collective-permute-start | bytes 73736 | tf_op jit(solution)/shard_map/ppermute | solution.py:341
  21.0 5.9 %collective-permute-start.9 = (f32[18,8,128]{2,1,0:T(8,128)S(1)}, f32[18,8,128]{2,1,0:T(8,128)S(1)}, u32[]{:S(2)}, u32[]{:S(2)}) collective-permute-start(f32[18,8,128]{2,1,0:T(8,128)S(1)} %get-tuple-element.101.refs_1_), channel_id=1, source_target_pairs={{0,8},{1,5},{2,10},{3,7},{4,12},{5,1},{6,14},{7,3},{8,0},{9,13},{1... | collective-permute-start | bytes 221192 | tf_op jit(solution)/shard_map/ppermute | solution.py:285
  22.6 5.4 %collective-permute-start.8 = (f32[17,8,128]{2,1,0:T(8,128)S(1)}, f32[17,8,128]{2,1,0:T(8,128)S(1)}, u32[]{:S(2)}, u32[]{:S(2)}) collective-permute-start(f32[17,8,128]{2,1,0:T(8,128)S(1)} %get-tuple-element.100.refs_1_), channel_id=1, source_target_pairs={{0,8},{1,5},{2,10},{3,7},{4,12},{5,1},{6,14},{7,3},{8,0},{9,13},{1... | collective-permute-start | bytes 208904 | tf_op jit(solution)/shard_map/ppermute | solution.py:285
  26.9 4.4 %collective-permute-start.11 = (f32[18,8,128]{2,1,0:T(8,128)S(1)}, f32[18,8,128]{2,1,0:T(8,128)S(1)}, u32[]{:S(2)}, u32[]{:S(2)}) collective-permute-start(f32[18,8,128]{2,1,0:T(8,128)S(1)} %get-tuple-element.106.refs_1_), channel_id=1, source_target_pairs={{0,4},{1,3},{2,6},{3,1},{4,0},{5,7},{6,2},{7,5},{8,12},{9,11},{10,... | collective-permute-start | bytes 221192 | tf_op jit(solution)/shard_map/ppermute | solution.py:285
  28.0 4.4 %collective-permute-start.10 = (f32[17,8,128]{2,1,0:T(8,128)S(1)}, f32[17,8,128]{2,1,0:T(8,128)S(1)}, u32[]{:S(2)}, u32[]{:S(2)}) collective-permute-start(f32[17,8,128]{2,1,0:T(8,128)S(1)} %get-tuple-element.105.refs_1_), channel_id=1, source_target_pairs={{0,4},{1,3},{2,6},{3,1},{4,0},{5,7},{6,2},{7,5},{8,12},{9,11},{10,... | collective-permute-start | bytes 208904 | tf_op jit(solution)/shard_map/ppermute | solution.py:285
  31.4 5.1 %collective-permute-start.13 = (f32[34,8,128]{2,1,0:T(8,128)S(1)}, f32[34,8,128]{2,1,0:T(8,128)S(1)}, u32[]{:S(2)}, u32[]{:S(2)}) collective-permute-start(f32[34,8,128]{2,1,0:T(8,128)S(1)} %get-tuple-element.110.refs_1_), channel_id=1, source_target_pairs={{0,2},{1,9},{2,0},{3,11},{4,6},{5,13},{6,4},{7,15},{8,10},{9,1},{1... | collective-permute-start | bytes 417800 | tf_op jit(solution)/shard_map/ppermute | solution.py:285
  32.4 5.6 %collective-permute-start.12 = (f32[33,8,128]{2,1,0:T(8,128)S(1)}, f32[33,8,128]{2,1,0:T(8,128)S(1)}, u32[]{:S(2)}, u32[]{:S(2)}) collective-permute-start(f32[33,8,128]{2,1,0:T(8,128)S(1)} %get-tuple-element.109.refs_1_), channel_id=1, source_target_pairs={{0,2},{1,9},{2,0},{3,11},{4,6},{5,13},{6,4},{7,15},{8,10},{9,1},{1... | collective-permute-start | bytes 405512 | tf_op jit(solution)/shard_map/ppermute | solution.py:285
  36.5 2.1 %collective-permute-start.15 = (f32[66,8,128]{2,1,0:T(8,128)S(1)}, f32[66,8,128]{2,1,0:T(8,128)S(1)}, u32[]{:S(2)}, u32[]{:S(2)}) collective-permute-start(f32[66,8,128]{2,1,0:T(8,128)S(1)} %get-tuple-element.112.refs_1_), channel_id=1, source_target_pairs={{0,1},{1,0},{2,3},{3,2},{4,5},{5,4},{6,7},{7,6},{8,9},{9,8},{10,11... | collective-permute-start | bytes 811016 | tf_op jit(solution)/shard_map/ppermute | solution.py:285
  38.0 1.8 %collective-permute-start.14 = (f32[65,8,128]{2,1,0:T(8,128)S(1)}, f32[65,8,128]{2,1,0:T(8,128)S(1)}, u32[]{:S(2)}, u32[]{:S(2)}) collective-permute-start(f32[65,8,128]{2,1,0:T(8,128)S(1)} %get-tuple-element.115.refs_2_), channel_id=1, source_target_pairs={{0,1},{1,0},{2,3},{3,2},{4,5},{5,4},{6,7},{7,6},{8,9},{9,8},{10,11... | collective-permute-start | bytes 798728 | tf_op jit(solution)/shard_map/ppermute | solution.py:285

commit v7 on v6

--- a/solution.py
+++ b/solution.py
@@ -198,12 +198,15 @@
     out_ref[:rows] = motifs_ref[pl.ds(at, rows)] * numer / denom[None]
 
 
-def join_kernel(step, steps, half, me_ref, mine_ref, got_ref, out_ref):
+def join_kernel(step, steps, size, half, me_ref, mine_ref, got_ref, out_ref):
     me = me_ref[0]
     bit = place(me, step, steps)
-    out_ref[pl.ds(bit * half, half)] = mine_ref[:half]
-    out_ref[pl.ds((1 - bit) * half, half)] = got_ref[:half]
-    row = carry(me, carry_bit(me, step, steps), mine_ref[half], got_ref[half])
+    for i in range(half // size):
+        here = pl.ds(i * size, size)
+        out_ref[pl.ds(2 * i * size + bit * size, size)] = mine_ref[here]
+        out_ref[pl.ds(2 * i * size + (1 - bit) * size, size)] = got_ref[here]
+    span = 1 << carry_bit(me, step, steps)
+    row = jnp.where((me & (span - 1)) == span - 2, got_ref[half], mine_ref[half])
     for i in range(2 * half, out_ref.shape[0]):
         out_ref[i] = row
 
@@ -359,16 +362,17 @@
         )
         if more:
             denom = more[0]
-        got[c] = swap(mine[c], steps - 2)
+        got[c] = swap(mine[c], 1)
     out, new_loadings, waiting = None, None, []
-    for step in range(steps - 2, 0, -1):
+    size = list(half)
+    for step in range(1, steps - 1):
         for c in chunks:
             (mine[c],) = call(
-                functools.partial(join_kernel, step, steps, half[c]), [cubes(2 * half[c] + carried[c])], mine[c], got[c]
+                functools.partial(join_kernel, step, steps, size[c], half[c]), [cubes(2 * half[c] + carried[c])], mine[c], got[c]
             )
             half[c] *= 2
-            got[c] = swap(mine[c], step - 1)
-            if step == 1:
+            got[c] = swap(mine[c], (step + 1) % (steps - 1))
+            if step == steps - 2:
                 waiting.append((sum(sizes[:c]), half[c], True, mine[c]))
                 out, new_loadings = store(call, out, new_loadings, rows, waiting, numer, scale, ranks)
                 waiting = [(sum(sizes[:c]), half[c], False, got[c])]

time: 40.7 us -> 40.5 us (level)
  starting transfers between devices: 14.8 us -> 14.1 us
  waiting for transfers between devices: 15.5 us -> 16 us
    ppermute x14, starting transfers between devices: 12.4 us -> 11.7 us  [swap(): lax.ppermute(x, 'tm', [(i, i ^ 1 << order(i & 1, steps)[step]) for i in r...]
    ppermute x14, waiting for transfers between devices: 11.6 us -> 12.1 us  [swap(): lax.ppermute(x, 'tm', [(i, i ^ 1 << order(i & 1, steps)[step]) for i in r...]
  transfers between devices with their start and end apart: 16 -> 16, of which waited for: 14 -> 15; matrix products, arithmetic and copies ran while one was open for 0% -> 0% of each run, Pallas kernels for 16% -> 16%
where the time goes in v7:
time: 40.5 us; the launch traced here: 40.3 us
  waiting for transfers between devices  16 us (40%)
  starting transfers between devices  14.1 us (35%)
  Pallas kernels  8.54 us (21%)
  local copies, waits for them, and re-layouts  0.89 us (2%)
  between operations  0.81 us (2%)
    ppermute x14, waiting for transfers between devices, swap(): lax.ppermute(x, 'tm', [(i, i ^ 1 << order(i & 1, steps)[step]) for i in r...  12.1 us
    ppermute x14, starting transfers between devices, swap(): lax.ppermute(x, 'tm', [(i, i ^ 1 << order(i & 1, steps)[step]) for i in r...  11.7 us
    pallas_call x21, Pallas kernels, __call__(): pl.pallas_call(run, out_shape=[*out_shapes, *(jax.ShapeDtypeStruct(t.shap...  8.54 us
    ppermute x1, waiting for transfers between devices, body(): lax.ppermute(sent, 'tm', [(i, (i + 1) % ranks) for i in range(ranks)])  3.7 us
    ppermute x1, starting transfers between devices, body(): lax.ppermute(part, 'neur', [(i, i ^ 1 << flip) for i in range(groups)])  1.94 us
    unnamed x6, local copies, waits for them, and re-layouts  0.89 us
  transfers between devices with their start and end apart: 16, of which 15 were waited for; matrix products, arithmetic and copies ran while one was open for 0% of the time, Pallas kernels for 16%

profile of v7, /device:TPU:0, one launch (start us, length us, event | category | flops | bytes accessed | tf_op | source)
XLA Modules:
  0.0 40.3 jit_solution(13227011596899628036)
XLA Ops:
  0.7 0.7 %copy-done.2 = f32[8,512]{1,0:T(8,128)S(1)} copy-done((f32[8,512]{1,0:T(8,128)S(1)}, f32[8,512]{1,0:T(8,128)}, u32[]{:S(2)}) %copy-start.2) | copy-done | bytes 16408
  1.4 0.5 %collective-permute-start = (f32[8,512]{1,0:T(8,128)S(1)}, f32[8,512]{1,0:T(8,128)S(1)}, u32[]{:S(2)}, u32[]{:S(2)}) collective-permute-start(f32[8,512]{1,0:T(8,128)S(1)} %copy-done.2), channel_id=1, source_target_pairs={{0,1},{1,2},{2,3},{3,4},{4,5},{5,6},{6,7},{7,8},{8,9},{9,10},{10,1... | collective-permute-start | bytes 49160 | tf_op jit(solution)/shard_map/ppermute | solution.py:296
  2.0 2.5 %body_kernel.1 = (bf16[256,1024]{1,0:T(8,128)(2,1)S(1)}, bf16[256,1024]{1,0:T(8,128)(2,1)S(1)}, bf16[256,384]{1,0:T(8,128)(2,1)S(1)}, bf16[256,384]{1,0:T(8,128)...) custom-call(s32[1]{0:T(128)} %bitcast.refs_0_, ...), custom_call_target="tpu_custom_call", output_to_operand_aliasing={{6}: (4, {})} | custom-call | flops 1610612736 | tf_op jit(solution)/shard_map/body_kernel/pallas_call | solution.py:64
  4.5 3.7 %collective-permute-done.refs_1_ = f32[8,512]{1,0:T(8,128)S(1)} collective-permute-done((f32[8,512]{1,0:T(8,128)S(1)}, f32[8,512]{1,0:T(8,128)S(1)}, u32[]{:S(2)}, u32[]{:S(2)}) %collective-permute-start) | collective-permute-done | bytes 16416 | tf_op jit(solution)/shard_map/ppermute | solution.py:296
  8.2 1.3 %head_kernel.1 = (f32[520,128]{1,0:T(8,128)S(1)}, f32[512,128]{1,0:T(8,128)S(1)}, bf16[256,128]{1,0:T(8,128)(2,1)S(1)}, bf16[256,128]{1,0:T(8,128)(2,1)S(1)}, bf...) custom-call(s32[1]{0:T(128)} %bitcast.refs_0_, ...), custom_call_target="tpu_custom_call", output_to_operand_aliasing={{7}: (7, {})} | custom-call | tf_op jit(solution)/shard_map/head_kernel/pallas_call | solution.py:64
  9.6 0.5 %collective-permute-start.1 = (f32[64,8,128]{2,1,0:T(8,128)S(1)}, f32[64,8,128]{2,1,0:T(8,128)S(1)}, u32[]{:S(2)}, u32[]{:S(2)}) collective-permute-start(f32[64,8,128]{2,1,0:T(8,128)S(1)} %bitcast.10), channel_id=1, source_target_pairs={{0,1},{1,0},{2,3},{3,2},{4,5},{5,4},{6,7},{7,6},{8,9},{9,8},{10,11... | collective-permute-start | bytes 786440 | tf_op jit(solution)/shard_map/ppermute | solution.py:288
  10.1 0.4 home_kernel.1
  10.5 0.6 %collective-permute-done.2.refs_2_ = f32[65,8,128]{2,1,0:T(8,128)S(1)} collective-permute-done((f32[65,8,128]{2,1,0:T(8,128)S(1)}, f32[65,8,128]{2,1,0:T(8,128)S(1)}, u32[]{:S(2)}, u32[]{:S(2)}) %collective-permute-start.2) | collective-permute-done | bytes 266272 | tf_op jit(solution)/shard_map/ppermute | solution.py:288
  11.5 1.8 %collective-permute-start.3 = (f32[32,8,128]{2,1,0:T(8,128)S(1)}, f32[32,8,128]{2,1,0:T(8,128)S(1)}, u32[]{:S(2)}, u32[]{:S(2)}) collective-permute-start(f32[32,8,128]{2,1,0:T(8,128)S(1)} %get-tuple-element.82), channel_id=1, source_target_pairs={{0,2},{1,9},{2,0},{3,11},{4,6},{5,13},{6,4},{7,15},{8,10},{9,1},{1... | collective-permute-start | bytes 393224 | tf_op jit(solution)/shard_map/ppermute | solution.py:288
  13.4 1.6 %lagged_kernel.1 = (f32[8,768]{1,0:T(8,128)S(1)}, f32[8,128]{1,0:T(8,128)S(1)}) custom-call(s32[1]{0:T(128)} %bitcast.refs_0_, bf16[256,1024]{1,0:T(8,128)(2,1)S(1)} %get-tuple-element.65.refs_4_.refs_1_, bf16[256,1024]{1,0:T(8,128)(2,1)S(1)} %get-tuple-element.66.refs_5_.refs_2_, ...), custom_call_target="tpu_custom_call", output_to_operand_aliasing={{1}: (8, {})} | custom-call | flops 805306368 | tf_op jit(solution)/shard_map/lagged_kernel/pallas_call | solution.py:64
  15.0 1.3 %collective-permute-done.4.refs_2_ = f32[33,8,128]{2,1,0:T(8,128)S(1)} collective-permute-done((f32[33,8,128]{2,1,0:T(8,128)S(1)}, f32[33,8,128]{2,1,0:T(8,128)S(1)}, u32[]{:S(2)}, u32[]{:S(2)}) %collective-permute-start.4) | collective-permute-done | bytes 135200 | tf_op jit(solution)/shard_map/ppermute | solution.py:288
  16.3 0.3 collective-permute-start.7
  16.5 1.1 %collective-permute-done.3.refs_2_ = f32[32,8,128]{2,1,0:T(8,128)S(1)} collective-permute-done((f32[32,8,128]{2,1,0:T(8,128)S(1)}, f32[32,8,128]{2,1,0:T(8,128)S(1)}, u32[]{:S(2)}, u32[]{:S(2)}) %collective-permute-start.3) | collective-permute-done | bytes 131104 | tf_op jit(solution)/shard_map/ppermute | solution.py:288
  17.7 0.8 %collective-permute-start.5 = (f32[16,8,128]{2,1,0:T(8,128)S(1)}, f32[16,8,128]{2,1,0:T(8,128)S(1)}, u32[]{:S(2)}, u32[]{:S(2)}) collective-permute-start(f32[16,8,128]{2,1,0:T(8,128)S(1)} %get-tuple-element.92), channel_id=1, source_target_pairs={{0,4},{1,3},{2,6},{3,1},{4,0},{5,7},{6,2},{7,5},{8,12},{9,11},{10,... | collective-permute-start | bytes 196616 | tf_op jit(solution)/shard_map/ppermute | solution.py:288
  18.4 1.9 %collective-permute-start.6 = (f32[8,768]{1,0:T(8,128)S(1)}, f32[8,768]{1,0:T(8,128)S(1)}, u32[]{:S(2)}, u32[]{:S(2)}) collective-permute-start(f32[8,768]{1,0:T(8,128)S(1)} %get-tuple-element.93.refs_1_), channel_id=1, source_target_pairs={{0,16},{16,0},{1,17},{17,1},{2,18},{18,2},{3,19},{19,3},{4,20},{20... | collective-permute-start | bytes 73736 | tf_op jit(solution)/shard_map/ppermute | solution.py:344
  20.4 0.6 %collective-permute-done.7.refs_2_ = f32[17,8,128]{2,1,0:T(8,128)S(1)} collective-permute-done((f32[17,8,128]{2,1,0:T(8,128)S(1)}, f32[17,8,128]{2,1,0:T(8,128)S(1)}, u32[]{:S(2)}, u32[]{:S(2)}) %collective-permute-start.7) | collective-permute-done | bytes 69664 | tf_op jit(solution)/shard_map/ppermute | solution.py:288
  21.0 1.1 %collective-permute-start.9 = (f32[18,8,128]{2,1,0:T(8,128)S(1)}, f32[18,8,128]{2,1,0:T(8,128)S(1)}, u32[]{:S(2)}, u32[]{:S(2)}) collective-permute-start(f32[18,8,128]{2,1,0:T(8,128)S(1)} %get-tuple-element.101.refs_1_), channel_id=1, source_target_pairs={{0,8},{1,5},{2,10},{3,7},{4,12},{5,1},{6,14},{7,3},{8,0},{9,13},{1... | collective-permute-start | bytes 221192 | tf_op jit(solution)/shard_map/ppermute | solution.py:288
  22.3 0.3 loads_kernel.1
  22.6 2.2 %collective-permute-start.8 = (f32[17,8,128]{2,1,0:T(8,128)S(1)}, f32[17,8,128]{2,1,0:T(8,128)S(1)}, u32[]{:S(2)}, u32[]{:S(2)}) collective-permute-start(f32[17,8,128]{2,1,0:T(8,128)S(1)} %get-tuple-element.100.refs_1_), channel_id=1, source_target_pairs={{0,8},{1,5},{2,10},{3,7},{4,12},{5,1},{6,14},{7,3},{8,0},{9,13},{1... | collective-permute-start | bytes 208904 | tf_op jit(solution)/shard_map/ppermute | solution.py:288
  24.7 2.2 %collective-permute-done.9.refs_2_ = f32[18,8,128]{2,1,0:T(8,128)S(1)} collective-permute-done((f32[18,8,128]{2,1,0:T(8,128)S(1)}, f32[18,8,128]{2,1,0:T(8,128)S(1)}, u32[]{:S(2)}, u32[]{:S(2)}) %collective-permute-start.9) | collective-permute-done | bytes 73760 | tf_op jit(solution)/shard_map/ppermute | solution.py:288
  26.9 0.5 %collective-permute-start.11 = (f32[18,8,128]{2,1,0:T(8,128)S(1)}, f32[18,8,128]{2,1,0:T(8,128)S(1)}, u32[]{:S(2)}, u32[]{:S(2)}) collective-permute-start(f32[18,8,128]{2,1,0:T(8,128)S(1)} %get-tuple-element.106.refs_1_), channel_id=1, source_target_pairs={{0,2},{1,9},{2,0},{3,11},{4,6},{5,13},{6,4},{7,15},{8,10},{9,1},{1... | collective-permute-start | bytes 221192 | tf_op jit(solution)/shard_map/ppermute | solution.py:288
  27.5 0.5 %collective-permute-done.8.refs_2_ = f32[17,8,128]{2,1,0:T(8,128)S(1)} collective-permute-done((f32[17,8,128]{2,1,0:T(8,128)S(1)}, f32[17,8,128]{2,1,0:T(8,128)S(1)}, u32[]{:S(2)}, u32[]{:S(2)}) %collective-permute-start.8) | collective-permute-done | bytes 69664 | tf_op jit(solution)/shard_map/ppermute | solution.py:288
  28.0 1.1 %collective-permute-start.10 = (f32[17,8,128]{2,1,0:T(8,128)S(1)}, f32[17,8,128]{2,1,0:T(8,128)S(1)}, u32[]{:S(2)}, u32[]{:S(2)}) collective-permute-start(f32[17,8,128]{2,1,0:T(8,128)S(1)} %get-tuple-element.105.refs_1_), channel_id=1, source_target_pairs={{0,2},{1,9},{2,0},{3,11},{4,6},{5,13},{6,4},{7,15},{8,10},{9,1},{1... | collective-permute-start | bytes 208904 | tf_op jit(solution)/shard_map/ppermute | solution.py:288
  29.1 2.2 %collective-permute-done.11.refs_2_ = f32[18,8,128]{2,1,0:T(8,128)S(1)} collective-permute-done((f32[18,8,128]{2,1,0:T(8,128)S(1)}, f32[18,8,128]{2,1,0:T(8,128)S(1)}, u32[]{:S(2)}, u32[]{:S(2)}) %collective-permute-start.11) | collective-permute-done | bytes 73760 | tf_op jit(solution)/shard_map/ppermute | solution.py:288
  31.4 0.9 %collective-permute-start.13 = (f32[34,8,128]{2,1,0:T(8,128)S(1)}, f32[34,8,128]{2,1,0:T(8,128)S(1)}, u32[]{:S(2)}, u32[]{:S(2)}) collective-permute-start(f32[34,8,128]{2,1,0:T(8,128)S(1)} %get-tuple-element.110.refs_1_), channel_id=1, source_target_pairs={{0,4},{1,3},{2,6},{3,1},{4,0},{5,7},{6,2},{7,5},{8,12},{9,11},{10,... | collective-permute-start | bytes 417800 | tf_op jit(solution)/shard_map/ppermute | solution.py:288
  32.4 2.2 %collective-permute-start.12 = (f32[33,8,128]{2,1,0:T(8,128)S(1)}, f32[33,8,128]{2,1,0:T(8,128)S(1)}, u32[]{:S(2)}, u32[]{:S(2)}) collective-permute-start(f32[33,8,128]{2,1,0:T(8,128)S(1)} %get-tuple-element.109.refs_1_), channel_id=1, source_target_pairs={{0,4},{1,3},{2,6},{3,1},{4,0},{5,7},{6,2},{7,5},{8,12},{9,11},{10,... | collective-permute-start | bytes 405512 | tf_op jit(solution)/shard_map/ppermute | solution.py:288
  34.6 1.9 %collective-permute-done.13.refs_2_ = f32[34,8,128]{2,1,0:T(8,128)S(1)} collective-permute-done((f32[34,8,128]{2,1,0:T(8,128)S(1)}, f32[34,8,128]{2,1,0:T(8,128)S(1)}, u32[]{:S(2)}, u32[]{:S(2)}) %collective-permute-start.13) | collective-permute-done | bytes 139296 | tf_op jit(solution)/shard_map/ppermute | solution.py:288
  36.6 0.7 %store_kernel.3 = (f32[256,8,128]{2,1,0:T(8,128)}, f32[8,128]{1,0:T(8,128)S(1)}) custom-call(s32[1]{0:T(128)} %bitcast.refs_0_, f32[66,8,128]{2,1,0:T(8,128)S(1)} %get-tuple-element.112.refs_1_, f32[8,128]{1,0:T(8,128)S(1)} %get-tuple-element.113.refs_2_), custom_call_target="tpu_custom_call", output_to_operand_aliasing={{1}: (2, {})} | custom-call | tf_op jit(solution)/shard_map/store_kernel/pallas_call | solution.py:64
  37.3 0.6 %collective-permute-done.12.refs_2_ = f32[33,8,128]{2,1,0:T(8,128)S(1)} collective-permute-done((f32[33,8,128]{2,1,0:T(8,128)S(1)}, f32[33,8,128]{2,1,0:T(8,128)S(1)}, u32[]{:S(2)}, u32[]{:S(2)}) %collective-permute-start.12) | collective-permute-done | bytes 135200 | tf_op jit(solution)/shard_map/ppermute | solution.py:288
  38.1 0.8 %store_kernel.4 = (f32[256,8,128]{2,1,0:T(8,128)}, f32[8,128]{1,0:T(8,128)S(1)}) custom-call(s32[1]{0:T(128)} %bitcast.refs_0_, f32[66,8,128]{2,1,0:T(8,128)S(1)} %collective-permute-done.15.refs_1_, f32[65,8,128]{2,1,0:T(8,128)S(1)} %get-tuple-element.115.refs_2_, ...), custom_call_target="tpu_custom_call", output_to_operand_aliasing={{0}: (3, {}), {1}: (4, {})} | custom-call | tf_op jit(solution)/shard_map/store_kernel/pallas_call | solution.py:64
  39.0 0.6 %collective-permute-done.14.refs_1_ = f32[65,8,128]{2,1,0:T(8,128)S(1)} collective-permute-done((f32[65,8,128]{2,1,0:T(8,128)S(1)}, f32[65,8,128]{2,1,0:T(8,128)S(1)}, u32[]{:S(2)}, u32[]{:S(2)}) %collective-permute-start.14) | collective-permute-done | bytes 266272 | tf_op jit(solution)/shard_map/ppermute | solution.py:288
  39.6 0.7 %store_kernel.5 = (f32[256,8,128]{2,1,0:T(8,128)}, f32[8,512]{1,0:T(8,128)}, f32[8,128]{1,0:T(8,128)S(1)}) custom-call(s32[1]{0:T(128)} %bitcast.refs_0_, f32[65,8,128]{2,1,0:T(8,128)S(1)} %collective-permute-done.14.refs_1_, f32[8,512]{1,0:T(8,128)S(1)} %get-tuple-element.116.refs_2_, ...), custom_call_target="tpu_custom_call", output_to_operand_aliasing={{0}: (4, {}), {2}: (5, {})} | custom-call | tf_op jit(solution)/shard_map/store_kernel/pallas_call | solution.py:64
  (27 shorter events, 1.3 us)
Async XLA Ops:
  0.6 0.7 %copy-start.2 = (f32[8,512]{1,0:T(8,128)S(1)}, f32[8,512]{1,0:T(8,128)}, u32[]{:S(2)}) copy-start(f32[8,512]{1,0:T(8,128)} %refs_3_.5) | copy-start | bytes 49156
  0.6 1.2 %copy-start = (f32[256,8,128]{2,1,0:T(8,128)S(1)}, f32[256,8,128]{2,1,0:T(8,128)}, u32[]{:S(2)}) copy-start(f32[256,8,128]{2,1,0:T(8,128)} %refs_4_.3) | copy-start | bytes 3145732
  0.7 1.4 %copy-start.1 = (f32[256,512]{1,0:T(8,128)S(1)}, f32[256,512]{1,0:T(8,128)}, u32[]{:S(2)}) copy-start(f32[256,512]{1,0:T(8,128)} %refs_2_.1) | copy-start | bytes 1572868
  1.4 6.9 %collective-permute-start = (f32[8,512]{1,0:T(8,128)S(1)}, f32[8,512]{1,0:T(8,128)S(1)}, u32[]{:S(2)}, u32[]{:S(2)}) collective-permute-start(f32[8,512]{1,0:T(8,128)S(1)} %copy-done.2), channel_id=1, source_target_pairs={{0,1},{1,2},{2,3},{3,4},{4,5},{5,6},{6,7},{7,8},{8,9},{9,10},{10,1... | collective-permute-start | bytes 49160 | tf_op jit(solution)/shard_map/ppermute | solution.py:296
  9.5 1.6 %collective-permute-start.2 = (f32[65,8,128]{2,1,0:T(8,128)S(1)}, f32[65,8,128]{2,1,0:T(8,128)S(1)}, u32[]{:S(2)}, u32[]{:S(2)}) collective-permute-start(f32[65,8,128]{2,1,0:T(8,128)S(1)} %bitcast.9), channel_id=1, source_target_pairs={{0,1},{1,0},{2,3},{3,2},{4,5},{5,4},{6,7},{7,6},{8,9},{9,8},{10,11... | collective-permute-start | bytes 798728 | tf_op jit(solution)/shard_map/ppermute | solution.py:288
  9.6 1.9 %collective-permute-start.1 = (f32[64,8,128]{2,1,0:T(8,128)S(1)}, f32[64,8,128]{2,1,0:T(8,128)S(1)}, u32[]{:S(2)}, u32[]{:S(2)}) collective-permute-start(f32[64,8,128]{2,1,0:T(8,128)S(1)} %bitcast.10), channel_id=1, source_target_pairs={{0,1},{1,0},{2,3},{3,2},{4,5},{5,4},{6,7},{7,6},{8,9},{9,8},{10,11... | collective-permute-start | bytes 786440 | tf_op jit(solution)/shard_map/ppermute | solution.py:288
  11.2 5.1 %collective-permute-start.4 = (f32[33,8,128]{2,1,0:T(8,128)S(1)}, f32[33,8,128]{2,1,0:T(8,128)S(1)}, u32[]{:S(2)}, u32[]{:S(2)}) collective-permute-start(f32[33,8,128]{2,1,0:T(8,128)S(1)} %get-tuple-element.84), channel_id=1, source_target_pairs={{0,2},{1,9},{2,0},{3,11},{4,6},{5,13},{6,4},{7,15},{8,10},{9,1},{1... | collective-permute-start | bytes 405512 | tf_op jit(solution)/shard_map/ppermute | solution.py:288
  11.5 6.1 %collective-permute-start.3 = (f32[32,8,128]{2,1,0:T(8,128)S(1)}, f32[32,8,128]{2,1,0:T(8,128)S(1)}, u32[]{:S(2)}, u32[]{:S(2)}) collective-permute-start(f32[32,8,128]{2,1,0:T(8,128)S(1)} %get-tuple-element.82), channel_id=1, source_target_pairs={{0,2},{1,9},{2,0},{3,11},{4,6},{5,13},{6,4},{7,15},{8,10},{9,1},{1... | collective-permute-start | bytes 393224 | tf_op jit(solution)/shard_map/ppermute | solution.py:288
  16.3 4.7 %collective-permute-start.7 = (f32[17,8,128]{2,1,0:T(8,128)S(1)}, f32[17,8,128]{2,1,0:T(8,128)S(1)}, u32[]{:S(2)}, u32[]{:S(2)}) collective-permute-start(f32[17,8,128]{2,1,0:T(8,128)S(1)} %get-tuple-element.95), channel_id=1, source_target_pairs={{0,4},{1,3},{2,6},{3,1},{4,0},{5,7},{6,2},{7,5},{8,12},{9,11},{10,... | collective-permute-start | bytes 208904 | tf_op jit(solution)/shard_map/ppermute | solution.py:288
  17.7 4.9 %collective-permute-start.5 = (f32[16,8,128]{2,1,0:T(8,128)S(1)}, f32[16,8,128]{2,1,0:T(8,128)S(1)}, u32[]{:S(2)}, u32[]{:S(2)}) collective-permute-start(f32[16,8,128]{2,1,0:T(8,128)S(1)} %get-tuple-element.92), channel_id=1, source_target_pairs={{0,4},{1,3},{2,6},{3,1},{4,0},{5,7},{6,2},{7,5},{8,12},{9,11},{10,... | collective-permute-start | bytes 196616 | tf_op jit(solution)/shard_map/ppermute | solution.py:288
  18.4 3.8 %collective-permute-start.6 = (f32[8,768]{1,0:T(8,128)S(1)}, f32[8,768]{1,0:T(8,128)S(1)}, u32[]{:S(2)}, u32[]{:S(2)}) collective-permute-start(f32[8,768]{1,0:T(8,128)S(1)} %get-tuple-element.93.refs_1_), channel_id=1, source_target_pairs={{0,16},{16,0},{1,17},{17,1},{2,18},{18,2},{3,19},{19,3},{4,20},{20... | collective-permute-start | bytes 73736 | tf_op jit(solution)/shard_map/ppermute | solution.py:344
  21.0 5.9 %collective-permute-start.9 = (f32[18,8,128]{2,1,0:T(8,128)S(1)}, f32[18,8,128]{2,1,0:T(8,128)S(1)}, u32[]{:S(2)}, u32[]{:S(2)}) collective-permute-start(f32[18,8,128]{2,1,0:T(8,128)S(1)} %get-tuple-element.101.refs_1_), channel_id=1, source_target_pairs={{0,8},{1,5},{2,10},{3,7},{4,12},{5,1},{6,14},{7,3},{8,0},{9,13},{1... | collective-permute-start | bytes 221192 | tf_op jit(solution)/shard_map/ppermute | solution.py:288
  22.6 5.4 %collective-permute-start.8 = (f32[17,8,128]{2,1,0:T(8,128)S(1)}, f32[17,8,128]{2,1,0:T(8,128)S(1)}, u32[]{:S(2)}, u32[]{:S(2)}) collective-permute-start(f32[17,8,128]{2,1,0:T(8,128)S(1)} %get-tuple-element.100.refs_1_), channel_id=1, source_target_pairs={{0,8},{1,5},{2,10},{3,7},{4,12},{5,1},{6,14},{7,3},{8,0},{9,13},{1... | collective-permute-start | bytes 208904 | tf_op jit(solution)/shard_map/ppermute | solution.py:288
  26.9 4.4 %collective-permute-start.11 = (f32[18,8,128]{2,1,0:T(8,128)S(1)}, f32[18,8,128]{2,1,0:T(8,128)S(1)}, u32[]{:S(2)}, u32[]{:S(2)}) collective-permute-start(f32[18,8,128]{2,1,0:T(8,128)S(1)} %get-tuple-element.106.refs_1_), channel_id=1, source_target_pairs={{0,2},{1,9},{2,0},{3,11},{4,6},{5,13},{6,4},{7,15},{8,10},{9,1},{1... | collective-permute-start | bytes 221192 | tf_op jit(solution)/shard_map/ppermute | solution.py:288
  28.0 4.4 %collective-permute-start.10 = (f32[17,8,128]{2,1,0:T(8,128)S(1)}, f32[17,8,128]{2,1,0:T(8,128)S(1)}, u32[]{:S(2)}, u32[]{:S(2)}) collective-permute-start(f32[17,8,128]{2,1,0:T(8,128)S(1)} %get-tuple-element.105.refs_1_), channel_id=1, source_target_pairs={{0,2},{1,9},{2,0},{3,11},{4,6},{5,13},{6,4},{7,15},{8,10},{9,1},{1... | collective-permute-start | bytes 208904 | tf_op jit(solution)/shard_map/ppermute | solution.py:288
  31.4 5.1 %collective-permute-start.13 = (f32[34,8,128]{2,1,0:T(8,128)S(1)}, f32[34,8,128]{2,1,0:T(8,128)S(1)}, u32[]{:S(2)}, u32[]{:S(2)}) collective-permute-start(f32[34,8,128]{2,1,0:T(8,128)S(1)} %get-tuple-element.110.refs_1_), channel_id=1, source_target_pairs={{0,4},{1,3},{2,6},{3,1},{4,0},{5,7},{6,2},{7,5},{8,12},{9,11},{10,... | collective-permute-start | bytes 417800 | tf_op jit(solution)/shard_map/ppermute | solution.py:288
  32.4 5.6 %collective-permute-start.12 = (f32[33,8,128]{2,1,0:T(8,128)S(1)}, f32[33,8,128]{2,1,0:T(8,128)S(1)}, u32[]{:S(2)}, u32[]{:S(2)}) collective-permute-start(f32[33,8,128]{2,1,0:T(8,128)S(1)} %get-tuple-element.109.refs_1_), channel_id=1, source_target_pairs={{0,4},{1,3},{2,6},{3,1},{4,0},{5,7},{6,2},{7,5},{8,12},{9,11},{10,... | collective-permute-start | bytes 405512 | tf_op jit(solution)/shard_map/ppermute | solution.py:288
  36.5 1.6 %collective-permute-start.15 = (f32[66,8,128]{2,1,0:T(8,128)S(1)}, f32[66,8,128]{2,1,0:T(8,128)S(1)}, u32[]{:S(2)}, u32[]{:S(2)}) collective-permute-start(f32[66,8,128]{2,1,0:T(8,128)S(1)} %get-tuple-element.112.refs_1_), channel_id=1, source_target_pairs={{0,1},{1,0},{2,3},{3,2},{4,5},{5,4},{6,7},{7,6},{8,9},{9,8},{10,11... | collective-permute-start | bytes 811016 | tf_op jit(solution)/shard_map/ppermute | solution.py:288
  38.0 1.6 %collective-permute-start.14 = (f32[65,8,128]{2,1,0:T(8,128)S(1)}, f32[65,8,128]{2,1,0:T(8,128)S(1)}, u32[]{:S(2)}, u32[]{:S(2)}) collective-permute-start(f32[65,8,128]{2,1,0:T(8,128)S(1)} %get-tuple-element.115.refs_2_), channel_id=1, source_target_pairs={{0,1},{1,0},{2,3},{3,2},{4,5},{5,4},{6,7},{7,6},{8,9},{9,8},{10,11... | collective-permute-start | bytes 798728 | tf_op jit(solution)/shard_map/ppermute | solution.py:288

commit v8 on v7

--- a/solution.py
+++ b/solution.py
@@ -110,7 +110,7 @@
 
 
 def head_kernel(sizes, me_ref, tail_ref, counts_ref, loads_ref, mh_ref, ml_ref, numer_ref, *refs):
-    *send_refs, fh_ref, fl_ref, hh_ref, hl_ref, denom_ref = refs
+    send_ref, fh_ref, fl_ref, hh_ref, hl_ref, denom_ref = refs
     rows, frames = counts_ref.shape
     motif_count, lags = denom_ref.shape
     for k in range(motif_count):
@@ -120,20 +120,31 @@
         hh_ref[at, :], hl_ref[at, :] = split(toeplitz(row, lags)[:, lags:])
     estimate = dot3(mh_ref[...], ml_ref[...], hh_ref[...], hl_ref[...], NN)
     fh_ref[...], fl_ref[...] = split(counts_ref[:, :lags] / estimate)
-    away = blocks(sizes, 1 - (me_ref[0] & 1))
+    away = blocks(sizes, 1 - (me_ref[0] & 1))[0]
+    count = away.size
     ones = jnp.ones((ONES, lags), BF16)
-    xh = jnp.concatenate([*(fh_ref[at, :] for at in away), ones], axis=0)
-    xl = jnp.concatenate([*(fl_ref[at, :] for at in away), jnp.zeros_like(ones)], axis=0)
+    xh = jnp.concatenate([fh_ref[away, :], ones], axis=0)
+    xl = jnp.concatenate([fl_ref[away, :], jnp.zeros_like(ones)], axis=0)
     for k in range(0, motif_count, 2):
         at = pl.ds(k * lags, 2 * lags)
         numer = dot3(xh, xl, hh_ref[at, :], hl_ref[at, :], NT)
         for j in range(2):
             there, here = pl.ds((k + j) * lags, lags), slice(j * lags, (j + 1) * lags)
-            for ref, at, slab in zip(send_refs, away, slabs(numer, sizes)):
-                ref[pl.ds(k + j, at.size, stride=motif_count), :] = slab[:, here] + numer_ref[at, there]
-            denom = numer[rows // 2:rows // 2 + 1, here] + numer_ref[pl.ds(rows, 1), there]
-            send_refs[0][pl.ds(away[0].size * motif_count + k + j, 1), :] = denom
+            send_ref[pl.ds(k + j, count, stride=motif_count), :] = numer[:count, here] + numer_ref[away, there]
+            denom = numer[count:count + 1, here] + numer_ref[pl.ds(rows, 1), there]
+            send_ref[pl.ds(count * motif_count + k + j, 1), :] = denom
             denom_ref[pl.ds(k + j, 1), :] = denom
+
+
+def away_kernel(sizes, me_ref, fh_ref, fl_ref, hh_ref, hl_ref, numer_ref, *send_refs):
+    lags = send_refs[0].shape[1]
+    motif_count = hh_ref.shape[0] // lags
+    for ref, at in zip(send_refs, blocks(sizes, 1 - (me_ref[0] & 1))[1:]):
+        for k in range(0, motif_count, 2):
+            both = pl.ds(k * lags, 2 * lags)
+            numer = dot3(fh_ref[at, :], fl_ref[at, :], hh_ref[both, :], hl_ref[both, :], NT) + numer_ref[at, both]
+            for j in range(2):
+                ref[pl.ds(k + j, at.size, stride=motif_count), :] = numer[:, j * lags:(j + 1) * lags]
 
 
 def home_kernel(sizes, me_ref, fh_ref, fl_ref, hh_ref, hl_ref, denom_ref, numer_ref, *keep_refs):
@@ -307,9 +318,9 @@
     half = [size // 2 for size in sizes]
     extra = [int(c == 0) for c in chunks]
     parts = [shape((half[c] + extra[c]) * motif_count, lags) for c in chunks]
-    *send, fh, fl, hh, hl, denom = call(
+    send, fh, fl, hh, hl, denom = call(
         functools.partial(head_kernel, sizes),
-        parts + [shape(rows, lags, dtype=BF16)] * 2 + [shape(depth, lags, dtype=BF16)] * 2 + [shape(motif_count, lags)],
+        parts[:1] + [shape(rows, lags, dtype=BF16)] * 2 + [shape(depth, lags, dtype=BF16)] * 2 + [shape(motif_count, lags)],
         tail, head_counts, own_loads, mh, ml, numer, limit=6,
     )
 
@@ -320,6 +331,8 @@
     def cubes(count):
         return shape(count, motif_count, lags)
 
+    later = call(functools.partial(away_kernel, sizes), parts[1:], fh, fl, hh, hl, numer, limit=6)
+    send = [send, *later]
     got = [swap(cube(x), 0) for x in send]
     keep = call(
         functools.partial(home_kernel, sizes), parts, fh, fl, hh, hl, denom, numer, limit=6, flops=macs // 4

time: 40.5 us -> 40.5 us (level)
    pallas_call x21 -> x22, Pallas kernels: 8.54 us -> 8.93 us  [__call__(): pl.pallas_call(run, out_shape=[*out_shapes, *(jax.ShapeDtypeStruct(t.shap...]
  transfers between devices with their start and end apart: 16 -> 16, of which waited for: 15 -> 15; matrix products, arithmetic and copies ran while one was open for 0% -> 0% of each run, Pallas kernels for 16% -> 17%
where the time goes in v8:
time: 40.5 us; the launch traced here: 40.3 us
  waiting for transfers between devices  15.7 us (39%)
  starting transfers between devices  14 us (35%)
  Pallas kernels  8.93 us (22%)
  local copies, waits for them, and re-layouts  0.89 us (2%)
  between operations  0.8 us (2%)
    ppermute x14, waiting for transfers between devices, swap(): lax.ppermute(x, 'tm', [(i, i ^ 1 << order(i & 1, steps)[step]) for i in r...  11.8 us
    ppermute x14, starting transfers between devices, swap(): lax.ppermute(x, 'tm', [(i, i ^ 1 << order(i & 1, steps)[step]) for i in r...  11.6 us
    pallas_call x22, Pallas kernels, __call__(): pl.pallas_call(run, out_shape=[*out_shapes, *(jax.ShapeDtypeStruct(t.shap...  8.93 us
    ppermute x1, waiting for transfers between devices, body(): lax.ppermute(sent, 'tm', [(i, (i + 1) % ranks) for i in range(ranks)])  3.7 us
    ppermute x1, starting transfers between devices, body(): lax.ppermute(part, 'neur', [(i, i ^ 1 << flip) for i in range(groups)])  1.94 us
    unnamed x6, local copies, waits for them, and re-layouts  0.89 us
  transfers between devices with their start and end apart: 16, of which 15 were waited for; matrix products, arithmetic and copies ran while one was open for 0% of the time, Pallas kernels for 17%

profile of v8, /device:TPU:0, one launch (start us, length us, event | category | flops | bytes accessed | tf_op | source)
XLA Modules:
  0.0 40.3 jit_solution(3042546222593295495)
XLA Ops:
  0.7 0.7 %copy-done.2 = f32[8,512]{1,0:T(8,128)S(1)} copy-done((f32[8,512]{1,0:T(8,128)S(1)}, f32[8,512]{1,0:T(8,128)}, u32[]{:S(2)}) %copy-start.2) | copy-done | bytes 16408
  1.4 0.5 %collective-permute-start = (f32[8,512]{1,0:T(8,128)S(1)}, f32[8,512]{1,0:T(8,128)S(1)}, u32[]{:S(2)}, u32[]{:S(2)}) collective-permute-start(f32[8,512]{1,0:T(8,128)S(1)} %copy-done.2), channel_id=1, source_target_pairs={{0,1},{1,2},{2,3},{3,4},{4,5},{5,6},{6,7},{7,8},{8,9},{9,10},{10,1... | collective-permute-start | bytes 49160 | tf_op jit(solution)/shard_map/ppermute | solution.py:307
  2.0 2.5 %body_kernel.1 = (bf16[256,1024]{1,0:T(8,128)(2,1)S(1)}, bf16[256,1024]{1,0:T(8,128)(2,1)S(1)}, bf16[256,384]{1,0:T(8,128)(2,1)S(1)}, bf16[256,384]{1,0:T(8,128)...) custom-call(s32[1]{0:T(128)} %bitcast.refs_0_, ...), custom_call_target="tpu_custom_call", output_to_operand_aliasing={{6}: (4, {})} | custom-call | flops 1610612736 | tf_op jit(solution)/shard_map/body_kernel/pallas_call | solution.py:64
  4.5 3.7 %collective-permute-done.refs_1_ = f32[8,512]{1,0:T(8,128)S(1)} collective-permute-done((f32[8,512]{1,0:T(8,128)S(1)}, f32[8,512]{1,0:T(8,128)S(1)}, u32[]{:S(2)}, u32[]{:S(2)}) %collective-permute-start) | collective-permute-done | bytes 16416 | tf_op jit(solution)/shard_map/ppermute | solution.py:307
  8.2 1.3 %head_kernel.1 = (f32[520,128]{1,0:T(8,128)S(1)}, bf16[256,128]{1,0:T(8,128)(2,1)S(1)}, bf16[256,128]{1,0:T(8,128)(2,1)S(1)}, bf16[1024,128]{1,0:T(8,128)(2,1)S(...) custom-call(s32[1]{0:T(128)} %bitcast.refs_0_, ...), custom_call_target="tpu_custom_call", output_to_operand_aliasing={{6}: (7, {})} | custom-call | tf_op jit(solution)/shard_map/head_kernel/pallas_call | solution.py:64
  9.6 0.4 away_kernel.1
  10.0 0.6 %collective-permute-start.1 = (f32[64,8,128]{2,1,0:T(8,128)S(1)}, f32[64,8,128]{2,1,0:T(8,128)S(1)}, u32[]{:S(2)}, u32[]{:S(2)}) collective-permute-start(f32[64,8,128]{2,1,0:T(8,128)S(1)} %bitcast.10), channel_id=1, source_target_pairs={{0,1},{1,0},{2,3},{3,2},{4,5},{5,4},{6,7},{7,6},{8,9},{9,8},{10,11... | collective-permute-start | bytes 786440 | tf_op jit(solution)/shard_map/ppermute | solution.py:299
  10.5 0.4 home_kernel.1
  11.2 0.5 %collective-permute-done.1.refs_2_ = f32[64,8,128]{2,1,0:T(8,128)S(1)} collective-permute-done((f32[64,8,128]{2,1,0:T(8,128)S(1)}, f32[64,8,128]{2,1,0:T(8,128)S(1)}, u32[]{:S(2)}, u32[]{:S(2)}) %collective-permute-start.1) | collective-permute-done | bytes 262176 | tf_op jit(solution)/shard_map/ppermute | solution.py:299
  11.7 1.6 %collective-permute-start.3 = (f32[32,8,128]{2,1,0:T(8,128)S(1)}, f32[32,8,128]{2,1,0:T(8,128)S(1)}, u32[]{:S(2)}, u32[]{:S(2)}) collective-permute-start(f32[32,8,128]{2,1,0:T(8,128)S(1)} %get-tuple-element.84), channel_id=1, source_target_pairs={{0,2},{1,9},{2,0},{3,11},{4,6},{5,13},{6,4},{7,15},{8,10},{9,1},{1... | collective-permute-start | bytes 393224 | tf_op jit(solution)/shard_map/ppermute | solution.py:299
  13.3 1.6 %lagged_kernel.1 = (f32[8,768]{1,0:T(8,128)S(1)}, f32[8,128]{1,0:T(8,128)S(1)}) custom-call(s32[1]{0:T(128)} %bitcast.refs_0_, bf16[256,1024]{1,0:T(8,128)(2,1)S(1)} %get-tuple-element.66.refs_4_.refs_1_, bf16[256,1024]{1,0:T(8,128)(2,1)S(1)} %get-tuple-element.67.refs_5_.refs_2_, ...), custom_call_target="tpu_custom_call", output_to_operand_aliasing={{1}: (8, {})} | custom-call | flops 805306368 | tf_op jit(solution)/shard_map/lagged_kernel/pallas_call | solution.py:64
  14.9 1.3 %collective-permute-done.4.refs_2_ = f32[33,8,128]{2,1,0:T(8,128)S(1)} collective-permute-done((f32[33,8,128]{2,1,0:T(8,128)S(1)}, f32[33,8,128]{2,1,0:T(8,128)S(1)}, u32[]{:S(2)}, u32[]{:S(2)}) %collective-permute-start.4) | collective-permute-done | bytes 135200 | tf_op jit(solution)/shard_map/ppermute | solution.py:299
  16.2 0.3 collective-permute-start.7
  16.5 1.1 %collective-permute-done.3.refs_2_ = f32[32,8,128]{2,1,0:T(8,128)S(1)} collective-permute-done((f32[32,8,128]{2,1,0:T(8,128)S(1)}, f32[32,8,128]{2,1,0:T(8,128)S(1)}, u32[]{:S(2)}, u32[]{:S(2)}) %collective-permute-start.3) | collective-permute-done | bytes 131104 | tf_op jit(solution)/shard_map/ppermute | solution.py:299
  17.6 0.8 %collective-permute-start.5 = (f32[16,8,128]{2,1,0:T(8,128)S(1)}, f32[16,8,128]{2,1,0:T(8,128)S(1)}, u32[]{:S(2)}, u32[]{:S(2)}) collective-permute-start(f32[16,8,128]{2,1,0:T(8,128)S(1)} %get-tuple-element.94), channel_id=1, source_target_pairs={{0,4},{1,3},{2,6},{3,1},{4,0},{5,7},{6,2},{7,5},{8,12},{9,11},{10,... | collective-permute-start | bytes 196616 | tf_op jit(solution)/shard_map/ppermute | solution.py:299
  18.4 1.9 %collective-permute-start.6 = (f32[8,768]{1,0:T(8,128)S(1)}, f32[8,768]{1,0:T(8,128)S(1)}, u32[]{:S(2)}, u32[]{:S(2)}) collective-permute-start(f32[8,768]{1,0:T(8,128)S(1)} %get-tuple-element.95.refs_1_), channel_id=1, source_target_pairs={{0,16},{16,0},{1,17},{17,1},{2,18},{18,2},{3,19},{19,3},{4,20},{20... | collective-permute-start | bytes 73736 | tf_op jit(solution)/shard_map/ppermute | solution.py:357
  20.4 0.6 %collective-permute-done.7.refs_2_ = f32[17,8,128]{2,1,0:T(8,128)S(1)} collective-permute-done((f32[17,8,128]{2,1,0:T(8,128)S(1)}, f32[17,8,128]{2,1,0:T(8,128)S(1)}, u32[]{:S(2)}, u32[]{:S(2)}) %collective-permute-start.7) | collective-permute-done | bytes 69664 | tf_op jit(solution)/shard_map/ppermute | solution.py:299
  20.9 1.1 %collective-permute-start.9 = (f32[18,8,128]{2,1,0:T(8,128)S(1)}, f32[18,8,128]{2,1,0:T(8,128)S(1)}, u32[]{:S(2)}, u32[]{:S(2)}) collective-permute-start(f32[18,8,128]{2,1,0:T(8,128)S(1)} %get-tuple-element.103.refs_1_), channel_id=1, source_target_pairs={{0,8},{1,5},{2,10},{3,7},{4,12},{5,1},{6,14},{7,3},{8,0},{9,13},{1... | collective-permute-start | bytes 221192 | tf_op jit(solution)/shard_map/ppermute | solution.py:299
  22.5 2.2 %collective-permute-start.8 = (f32[17,8,128]{2,1,0:T(8,128)S(1)}, f32[17,8,128]{2,1,0:T(8,128)S(1)}, u32[]{:S(2)}, u32[]{:S(2)}) collective-permute-start(f32[17,8,128]{2,1,0:T(8,128)S(1)} %get-tuple-element.102.refs_1_), channel_id=1, source_target_pairs={{0,8},{1,5},{2,10},{3,7},{4,12},{5,1},{6,14},{7,3},{8,0},{9,13},{1... | collective-permute-start | bytes 208904 | tf_op jit(solution)/shard_map/ppermute | solution.py:299
  24.7 2.2 %collective-permute-done.9.refs_2_ = f32[18,8,128]{2,1,0:T(8,128)S(1)} collective-permute-done((f32[18,8,128]{2,1,0:T(8,128)S(1)}, f32[18,8,128]{2,1,0:T(8,128)S(1)}, u32[]{:S(2)}, u32[]{:S(2)}) %collective-permute-start.9) | collective-permute-done | bytes 73760 | tf_op jit(solution)/shard_map/ppermute | solution.py:299
  26.9 0.5 %collective-permute-start.11 = (f32[18,8,128]{2,1,0:T(8,128)S(1)}, f32[18,8,128]{2,1,0:T(8,128)S(1)}, u32[]{:S(2)}, u32[]{:S(2)}) collective-permute-start(f32[18,8,128]{2,1,0:T(8,128)S(1)} %get-tuple-element.108.refs_1_), channel_id=1, source_target_pairs={{0,2},{1,9},{2,0},{3,11},{4,6},{5,13},{6,4},{7,15},{8,10},{9,1},{1... | collective-permute-start | bytes 221192 | tf_op jit(solution)/shard_map/ppermute | solution.py:299
  27.4 0.5 %collective-permute-done.8.refs_2_ = f32[17,8,128]{2,1,0:T(8,128)S(1)} collective-permute-done((f32[17,8,128]{2,1,0:T(8,128)S(1)}, f32[17,8,128]{2,1,0:T(8,128)S(1)}, u32[]{:S(2)}, u32[]{:S(2)}) %collective-permute-start.8) | collective-permute-done | bytes 69664 | tf_op jit(solution)/shard_map/ppermute | solution.py:299
  27.9 1.1 %collective-permute-start.10 = (f32[17,8,128]{2,1,0:T(8,128)S(1)}, f32[17,8,128]{2,1,0:T(8,128)S(1)}, u32[]{:S(2)}, u32[]{:S(2)}) collective-permute-start(f32[17,8,128]{2,1,0:T(8,128)S(1)} %get-tuple-element.107.refs_1_), channel_id=1, source_target_pairs={{0,2},{1,9},{2,0},{3,11},{4,6},{5,13},{6,4},{7,15},{8,10},{9,1},{1... | collective-permute-start | bytes 208904 | tf_op jit(solution)/shard_map/ppermute | solution.py:299
  29.1 2.2 %collective-permute-done.11.refs_2_ = f32[18,8,128]{2,1,0:T(8,128)S(1)} collective-permute-done((f32[18,8,128]{2,1,0:T(8,128)S(1)}, f32[18,8,128]{2,1,0:T(8,128)S(1)}, u32[]{:S(2)}, u32[]{:S(2)}) %collective-permute-start.11) | collective-permute-done | bytes 73760 | tf_op jit(solution)/shard_map/ppermute | solution.py:299
  31.3 0.9 %collective-permute-start.13 = (f32[34,8,128]{2,1,0:T(8,128)S(1)}, f32[34,8,128]{2,1,0:T(8,128)S(1)}, u32[]{:S(2)}, u32[]{:S(2)}) collective-permute-start(f32[34,8,128]{2,1,0:T(8,128)S(1)} %get-tuple-element.112.refs_1_), channel_id=1, source_target_pairs={{0,4},{1,3},{2,6},{3,1},{4,0},{5,7},{6,2},{7,5},{8,12},{9,11},{10,... | collective-permute-start | bytes 417800 | tf_op jit(solution)/shard_map/ppermute | solution.py:299
  32.3 2.2 %collective-permute-start.12 = (f32[33,8,128]{2,1,0:T(8,128)S(1)}, f32[33,8,128]{2,1,0:T(8,128)S(1)}, u32[]{:S(2)}, u32[]{:S(2)}) collective-permute-start(f32[33,8,128]{2,1,0:T(8,128)S(1)} %get-tuple-element.111.refs_1_), channel_id=1, source_target_pairs={{0,4},{1,3},{2,6},{3,1},{4,0},{5,7},{6,2},{7,5},{8,12},{9,11},{10,... | collective-permute-start | bytes 405512 | tf_op jit(solution)/shard_map/ppermute | solution.py:299
  34.5 1.9 %collective-permute-done.13.refs_2_ = f32[34,8,128]{2,1,0:T(8,128)S(1)} collective-permute-done((f32[34,8,128]{2,1,0:T(8,128)S(1)}, f32[34,8,128]{2,1,0:T(8,128)S(1)}, u32[]{:S(2)}, u32[]{:S(2)}) %collective-permute-start.13) | collective-permute-done | bytes 139296 | tf_op jit(solution)/shard_map/ppermute | solution.py:299
  36.6 0.7 %store_kernel.3 = (f32[256,8,128]{2,1,0:T(8,128)}, f32[8,128]{1,0:T(8,128)S(1)}) custom-call(s32[1]{0:T(128)} %bitcast.refs_0_, f32[66,8,128]{2,1,0:T(8,128)S(1)} %get-tuple-element.114.refs_1_, f32[8,128]{1,0:T(8,128)S(1)} %get-tuple-element.115.refs_2_), custom_call_target="tpu_custom_call", output_to_operand_aliasing={{1}: (2, {})} | custom-call | tf_op jit(solution)/shard_map/store_kernel/pallas_call | solution.py:64
  37.3 0.6 %collective-permute-done.12.refs_2_ = f32[33,8,128]{2,1,0:T(8,128)S(1)} collective-permute-done((f32[33,8,128]{2,1,0:T(8,128)S(1)}, f32[33,8,128]{2,1,0:T(8,128)S(1)}, u32[]{:S(2)}, u32[]{:S(2)}) %collective-permute-start.12) | collective-permute-done | bytes 135200 | tf_op jit(solution)/shard_map/ppermute | solution.py:299
  38.1 0.8 %store_kernel.4 = (f32[256,8,128]{2,1,0:T(8,128)}, f32[8,128]{1,0:T(8,128)S(1)}) custom-call(s32[1]{0:T(128)} %bitcast.refs_0_, f32[66,8,128]{2,1,0:T(8,128)S(1)} %collective-permute-done.15.refs_1_, f32[65,8,128]{2,1,0:T(8,128)S(1)} %get-tuple-element.117.refs_2_, ...), custom_call_target="tpu_custom_call", output_to_operand_aliasing={{0}: (3, {}), {1}: (4, {})} | custom-call | tf_op jit(solution)/shard_map/store_kernel/pallas_call | solution.py:64
  38.9 0.6 %collective-permute-done.14.refs_1_ = f32[65,8,128]{2,1,0:T(8,128)S(1)} collective-permute-done((f32[65,8,128]{2,1,0:T(8,128)S(1)}, f32[65,8,128]{2,1,0:T(8,128)S(1)}, u32[]{:S(2)}, u32[]{:S(2)}) %collective-permute-start.14) | collective-permute-done | bytes 266272 | tf_op jit(solution)/shard_map/ppermute | solution.py:299
  39.5 0.7 %store_kernel.5 = (f32[256,8,128]{2,1,0:T(8,128)}, f32[8,512]{1,0:T(8,128)}, f32[8,128]{1,0:T(8,128)S(1)}) custom-call(s32[1]{0:T(128)} %bitcast.refs_0_, f32[65,8,128]{2,1,0:T(8,128)S(1)} %collective-permute-done.14.refs_1_, f32[8,512]{1,0:T(8,128)S(1)} %get-tuple-element.118.refs_2_, ...), custom_call_target="tpu_custom_call", output_to_operand_aliasing={{0}: (4, {}), {2}: (5, {})} | custom-call | tf_op jit(solution)/shard_map/store_kernel/pallas_call | solution.py:64
  (28 shorter events, 1.5 us)
Async XLA Ops:
  0.6 0.7 %copy-start.2 = (f32[8,512]{1,0:T(8,128)S(1)}, f32[8,512]{1,0:T(8,128)}, u32[]{:S(2)}) copy-start(f32[8,512]{1,0:T(8,128)} %refs_3_.5) | copy-start | bytes 49156
  0.6 1.2 %copy-start = (f32[256,8,128]{2,1,0:T(8,128)S(1)}, f32[256,8,128]{2,1,0:T(8,128)}, u32[]{:S(2)}) copy-start(f32[256,8,128]{2,1,0:T(8,128)} %refs_4_.3) | copy-start | bytes 3145732
  0.7 1.4 %copy-start.1 = (f32[256,512]{1,0:T(8,128)S(1)}, f32[256,512]{1,0:T(8,128)}, u32[]{:S(2)}) copy-start(f32[256,512]{1,0:T(8,128)} %refs_2_.1) | copy-start | bytes 1572868
  1.4 6.9 %collective-permute-start = (f32[8,512]{1,0:T(8,128)S(1)}, f32[8,512]{1,0:T(8,128)S(1)}, u32[]{:S(2)}, u32[]{:S(2)}) collective-permute-start(f32[8,512]{1,0:T(8,128)S(1)} %copy-done.2), channel_id=1, source_target_pairs={{0,1},{1,2},{2,3},{3,4},{4,5},{5,6},{6,7},{7,8},{8,9},{9,10},{10,1... | collective-permute-start | bytes 49160 | tf_op jit(solution)/shard_map/ppermute | solution.py:307
  9.5 1.6 %collective-permute-start.2 = (f32[65,8,128]{2,1,0:T(8,128)S(1)}, f32[65,8,128]{2,1,0:T(8,128)S(1)}, u32[]{:S(2)}, u32[]{:S(2)}) collective-permute-start(f32[65,8,128]{2,1,0:T(8,128)S(1)} %bitcast.9), channel_id=1, source_target_pairs={{0,1},{1,0},{2,3},{3,2},{4,5},{5,4},{6,7},{7,6},{8,9},{9,8},{10,11... | collective-permute-start | bytes 798728 | tf_op jit(solution)/shard_map/ppermute | solution.py:299
  10.0 1.7 %collective-permute-start.1 = (f32[64,8,128]{2,1,0:T(8,128)S(1)}, f32[64,8,128]{2,1,0:T(8,128)S(1)}, u32[]{:S(2)}, u32[]{:S(2)}) collective-permute-start(f32[64,8,128]{2,1,0:T(8,128)S(1)} %bitcast.10), channel_id=1, source_target_pairs={{0,1},{1,0},{2,3},{3,2},{4,5},{5,4},{6,7},{7,6},{8,9},{9,8},{10,11... | collective-permute-start | bytes 786440 | tf_op jit(solution)/shard_map/ppermute | solution.py:299
  11.1 5.1 %collective-permute-start.4 = (f32[33,8,128]{2,1,0:T(8,128)S(1)}, f32[33,8,128]{2,1,0:T(8,128)S(1)}, u32[]{:S(2)}, u32[]{:S(2)}) collective-permute-start(f32[33,8,128]{2,1,0:T(8,128)S(1)} %get-tuple-element.86), channel_id=1, source_target_pairs={{0,2},{1,9},{2,0},{3,11},{4,6},{5,13},{6,4},{7,15},{8,10},{9,1},{1... | collective-permute-start | bytes 405512 | tf_op jit(solution)/shard_map/ppermute | solution.py:299
  11.7 5.9 %collective-permute-start.3 = (f32[32,8,128]{2,1,0:T(8,128)S(1)}, f32[32,8,128]{2,1,0:T(8,128)S(1)}, u32[]{:S(2)}, u32[]{:S(2)}) collective-permute-start(f32[32,8,128]{2,1,0:T(8,128)S(1)} %get-tuple-element.84), channel_id=1, source_target_pairs={{0,2},{1,9},{2,0},{3,11},{4,6},{5,13},{6,4},{7,15},{8,10},{9,1},{1... | collective-permute-start | bytes 393224 | tf_op jit(solution)/shard_map/ppermute | solution.py:299
  16.2 4.7 %collective-permute-start.7 = (f32[17,8,128]{2,1,0:T(8,128)S(1)}, f32[17,8,128]{2,1,0:T(8,128)S(1)}, u32[]{:S(2)}, u32[]{:S(2)}) collective-permute-start(f32[17,8,128]{2,1,0:T(8,128)S(1)} %get-tuple-element.97), channel_id=1, source_target_pairs={{0,4},{1,3},{2,6},{3,1},{4,0},{5,7},{6,2},{7,5},{8,12},{9,11},{10,... | collective-permute-start | bytes 208904 | tf_op jit(solution)/shard_map/ppermute | solution.py:299
  17.6 4.9 %collective-permute-start.5 = (f32[16,8,128]{2,1,0:T(8,128)S(1)}, f32[16,8,128]{2,1,0:T(8,128)S(1)}, u32[]{:S(2)}, u32[]{:S(2)}) collective-permute-start(f32[16,8,128]{2,1,0:T(8,128)S(1)} %get-tuple-element.94), channel_id=1, source_target_pairs={{0,4},{1,3},{2,6},{3,1},{4,0},{5,7},{6,2},{7,5},{8,12},{9,11},{10,... | collective-permute-start | bytes 196616 | tf_op jit(solution)/shard_map/ppermute | solution.py:299
  18.4 3.8 %collective-permute-start.6 = (f32[8,768]{1,0:T(8,128)S(1)}, f32[8,768]{1,0:T(8,128)S(1)}, u32[]{:S(2)}, u32[]{:S(2)}) collective-permute-start(f32[8,768]{1,0:T(8,128)S(1)} %get-tuple-element.95.refs_1_), channel_id=1, source_target_pairs={{0,16},{16,0},{1,17},{17,1},{2,18},{18,2},{3,19},{19,3},{4,20},{20... | collective-permute-start | bytes 73736 | tf_op jit(solution)/shard_map/ppermute | solution.py:357
  20.9 5.9 %collective-permute-start.9 = (f32[18,8,128]{2,1,0:T(8,128)S(1)}, f32[18,8,128]{2,1,0:T(8,128)S(1)}, u32[]{:S(2)}, u32[]{:S(2)}) collective-permute-start(f32[18,8,128]{2,1,0:T(8,128)S(1)} %get-tuple-element.103.refs_1_), channel_id=1, source_target_pairs={{0,8},{1,5},{2,10},{3,7},{4,12},{5,1},{6,14},{7,3},{8,0},{9,13},{1... | collective-permute-start | bytes 221192 | tf_op jit(solution)/shard_map/ppermute | solution.py:299
  22.5 5.4 %collective-permute-start.8 = (f32[17,8,128]{2,1,0:T(8,128)S(1)}, f32[17,8,128]{2,1,0:T(8,128)S(1)}, u32[]{:S(2)}, u32[]{:S(2)}) collective-permute-start(f32[17,8,128]{2,1,0:T(8,128)S(1)} %get-tuple-element.102.refs_1_), channel_id=1, source_target_pairs={{0,8},{1,5},{2,10},{3,7},{4,12},{5,1},{6,14},{7,3},{8,0},{9,13},{1... | collective-permute-start | bytes 208904 | tf_op jit(solution)/shard_map/ppermute | solution.py:299
  26.9 4.4 %collective-permute-start.11 = (f32[18,8,128]{2,1,0:T(8,128)S(1)}, f32[18,8,128]{2,1,0:T(8,128)S(1)}, u32[]{:S(2)}, u32[]{:S(2)}) collective-permute-start(f32[18,8,128]{2,1,0:T(8,128)S(1)} %get-tuple-element.108.refs_1_), channel_id=1, source_target_pairs={{0,2},{1,9},{2,0},{3,11},{4,6},{5,13},{6,4},{7,15},{8,10},{9,1},{1... | collective-permute-start | bytes 221192 | tf_op jit(solution)/shard_map/ppermute | solution.py:299
  27.9 4.4 %collective-permute-start.10 = (f32[17,8,128]{2,1,0:T(8,128)S(1)}, f32[17,8,128]{2,1,0:T(8,128)S(1)}, u32[]{:S(2)}, u32[]{:S(2)}) collective-permute-start(f32[17,8,128]{2,1,0:T(8,128)S(1)} %get-tuple-element.107.refs_1_), channel_id=1, source_target_pairs={{0,2},{1,9},{2,0},{3,11},{4,6},{5,13},{6,4},{7,15},{8,10},{9,1},{1... | collective-permute-start | bytes 208904 | tf_op jit(solution)/shard_map/ppermute | solution.py:299
  31.3 5.1 %collective-permute-start.13 = (f32[34,8,128]{2,1,0:T(8,128)S(1)}, f32[34,8,128]{2,1,0:T(8,128)S(1)}, u32[]{:S(2)}, u32[]{:S(2)}) collective-permute-start(f32[34,8,128]{2,1,0:T(8,128)S(1)} %get-tuple-element.112.refs_1_), channel_id=1, source_target_pairs={{0,4},{1,3},{2,6},{3,1},{4,0},{5,7},{6,2},{7,5},{8,12},{9,11},{10,... | collective-permute-start | bytes 417800 | tf_op jit(solution)/shard_map/ppermute | solution.py:299
  32.3 5.6 %collective-permute-start.12 = (f32[33,8,128]{2,1,0:T(8,128)S(1)}, f32[33,8,128]{2,1,0:T(8,128)S(1)}, u32[]{:S(2)}, u32[]{:S(2)}) collective-permute-start(f32[33,8,128]{2,1,0:T(8,128)S(1)} %get-tuple-element.111.refs_1_), channel_id=1, source_target_pairs={{0,4},{1,3},{2,6},{3,1},{4,0},{5,7},{6,2},{7,5},{8,12},{9,11},{10,... | collective-permute-start | bytes 405512 | tf_op jit(solution)/shard_map/ppermute | solution.py:299
  36.5 1.6 %collective-permute-start.15 = (f32[66,8,128]{2,1,0:T(8,128)S(1)}, f32[66,8,128]{2,1,0:T(8,128)S(1)}, u32[]{:S(2)}, u32[]{:S(2)}) collective-permute-start(f32[66,8,128]{2,1,0:T(8,128)S(1)} %get-tuple-element.114.refs_1_), channel_id=1, source_target_pairs={{0,1},{1,0},{2,3},{3,2},{4,5},{5,4},{6,7},{7,6},{8,9},{9,8},{10,11... | collective-permute-start | bytes 811016 | tf_op jit(solution)/shard_map/ppermute | solution.py:299
  37.9 1.6 %collective-permute-start.14 = (f32[65,8,128]{2,1,0:T(8,128)S(1)}, f32[65,8,128]{2,1,0:T(8,128)S(1)}, u32[]{:S(2)}, u32[]{:S(2)}) collective-permute-start(f32[65,8,128]{2,1,0:T(8,128)S(1)} %get-tuple-element.117.refs_2_), channel_id=1, source_target_pairs={{0,1},{1,0},{2,3},{3,2},{4,5},{5,4},{6,7},{7,6},{8,9},{9,8},{10,11... | collective-permute-start | bytes 798728 | tf_op jit(solution)/shard_map/ppermute | solution.py:299

commit v9 on v8

--- a/solution.py
+++ b/solution.py
@@ -81,9 +81,9 @@
     out_ref[...] = jnp.zeros_like(out_ref)
 
 
-def body_kernel(me_ref, counts_ref, motifs_ref, loads_ref, mh_ref, ml_ref, rh_ref, rl_ref, numer_ref, total_ref, th, tl):
+def body_kernel(me_ref, counts_ref, motifs_ref, loads_ref, mh_ref, ml_ref, rh_ref, rl_ref, numer_ref, th, tl):
     rows, frames = counts_ref.shape
-    motif_count, lags = total_ref.shape
+    motif_count, lags = loads_ref.shape[0], motifs_ref.shape[1]
     for k in range(motif_count):
         at = pl.ds(k * lags, lags)
         th[at, :], tl[at, :] = split(toeplitz(loads_ref[pl.ds(k, 1), :], lags)[:, lags:])
@@ -96,7 +96,6 @@
     for k in range(0, motif_count, 2):
         at = pl.ds(k * lags, 2 * lags)
         numer_ref[:, at] = dot3(xh, xl, th[at, :], tl[at, :], NT)
-    total_ref[...] = jnp.sum(motifs_ref[...].reshape(rows, motif_count, lags), axis=0)
 
 
 def blocks(sizes, core):
@@ -246,8 +245,9 @@
         copy.wait()
 
 
-def lagged_kernel(me_ref, mh_ref, ml_ref, fh_ref, fl_ref, rh_ref, rl_ref, total_ref, out_ref, ph, pw):
-    motif_count, lags = total_ref.shape
+def lagged_kernel(me_ref, mh_ref, ml_ref, fh_ref, fl_ref, rh_ref, rl_ref, out_ref, ph, pw):
+    motif_count = out_ref.shape[0]
+    lags = mh_ref.shape[1] // motif_count
     frames = out_ref.shape[1] - 2 * lags
     width = frames + lags
     down = lax.broadcasted_iota(jnp.int32, (lags, lags), 0)
@@ -259,6 +259,8 @@
         at = pl.ds(k * lags, lags)
         for ref, out in ((mh_ref, ph), (ml_ref, pw)):
             out[:, at] = lax.dot_general(ref[:, at], flip, NN, preferred_element_type=F32).astype(BF16)
+        motifs = mh_ref[:, at].astype(F32) + ml_ref[:, at].astype(F32)
+        out_ref[pl.ds(k, 1), width:] = jnp.sum(motifs, axis=0, keepdims=True)
     for k in range(0, motif_count, 4):
         at = pl.ds(k * lags, 4 * lags)
         lagged = dot3(ph[:, at], pw[:, at], xh, xl, TN)
@@ -268,7 +270,6 @@
             numer = jnp.sum(skewed, axis=0, keepdims=True)
             out_ref[pl.ds(k + j, 1), :frames] = numer[:, lags:]
             out_ref[pl.ds(k + j, 1), frames:width] = numer[:, :lags]
-    out_ref[:, width:] = total_ref[...]
 
 
 def loads_kernel(ranks, me_ref, mine_ref, got_ref, loads_ref, ahead_ref, numer_ref, scale_ref):
@@ -305,10 +306,10 @@
     (call.token,) = call(open_kernel, [shape(motif_count, lags)], flops=10 ** 10)
     call.token, sent = lax.optimization_barrier((call.token, loadings))
     tail = lax.ppermute(sent, "tm", [(i, (i + 1) % ranks) for i in range(ranks)])
-    mh, ml, rh, rl, numer, total = call(
+    mh, ml, rh, rl, numer = call(
         body_kernel,
         [shape(rows, depth, dtype=BF16)] * 2 + [shape(rows, rest, dtype=BF16)] * 2
-        + [shape(rows + ONES, depth), shape(motif_count, lags)],
+        + [shape(rows + ONES, depth)],
         counts, flat, loadings, scratch=[pltpu.VMEM((depth, rest), BF16)] * 2, limit=BODY_LIMIT, flops=4 * macs,
     )
     head_counts, own_loads = counts, loadings
@@ -347,7 +348,7 @@
             got[c] = swap(send[c], step)
         if step == 1:
             (part,) = call(
-                lagged_kernel, [shape(motif_count, frames + 2 * lags)], mh, ml, fh, fl, rh, rl, total,
+                lagged_kernel, [shape(motif_count, frames + 2 * lags)], mh, ml, fh, fl, rh, rl,
                 scratch=[pltpu.VMEM((rows, depth), BF16)] * 2, limit=8, flops=2 * macs,
             )
             other = jnp.zeros_like(part)

time: 40.5 us -> 40.5 us (level)
  transfers between devices with their start and end apart: 16 -> 16, of which waited for: 15 -> 15; matrix products, arithmetic and copies ran while one was open for 0% -> 0% of each run, Pallas kernels for 17% -> 18%
where the time goes in v9:
time: 40.5 us; the launch traced here: 40.3 us
  waiting for transfers between devices  15.5 us (38%)
  starting transfers between devices  14 us (35%)
  Pallas kernels  9.13 us (23%)
  local copies, waits for them, and re-layouts  0.89 us (2%)
  between operations  0.8 us (2%)
    ppermute x14, waiting for transfers between devices, swap(): lax.ppermute(x, 'tm', [(i, i ^ 1 << order(i & 1, steps)[step]) for i in r...  11.6 us
    ppermute x14, starting transfers between devices, swap(): lax.ppermute(x, 'tm', [(i, i ^ 1 << order(i & 1, steps)[step]) for i in r...  11.6 us
    pallas_call x22, Pallas kernels, __call__(): pl.pallas_call(run, out_shape=[*out_shapes, *(jax.ShapeDtypeStruct(t.shap...  9.13 us
    ppermute x1, waiting for transfers between devices, body(): lax.ppermute(sent, 'tm', [(i, (i + 1) % ranks) for i in range(ranks)])  3.7 us
    ppermute x1, starting transfers between devices, body(): lax.ppermute(part, 'neur', [(i, i ^ 1 << flip) for i in range(groups)])  1.94 us
    unnamed x6, local copies, waits for them, and re-layouts  0.89 us
  transfers between devices with their start and end apart: 16, of which 15 were waited for; matrix products, arithmetic and copies ran while one was open for 0% of the time, Pallas kernels for 18%

profile of v9, /device:TPU:0, one launch (start us, length us, event | category | flops | bytes accessed | tf_op | source)
XLA Modules:
  0.0 40.3 jit_solution(16443558480567360406)
XLA Ops:
  0.7 0.7 %copy-done.2 = f32[8,512]{1,0:T(8,128)S(1)} copy-done((f32[8,512]{1,0:T(8,128)S(1)}, f32[8,512]{1,0:T(8,128)}, u32[]{:S(2)}) %copy-start.2) | copy-done | bytes 16408
  1.4 0.5 %collective-permute-start = (f32[8,512]{1,0:T(8,128)S(1)}, f32[8,512]{1,0:T(8,128)S(1)}, u32[]{:S(2)}, u32[]{:S(2)}) collective-permute-start(f32[8,512]{1,0:T(8,128)S(1)} %copy-done.2), channel_id=1, source_target_pairs={{0,1},{1,2},{2,3},{3,4},{4,5},{5,6},{6,7},{7,8},{8,9},{9,10},{10,1... | collective-permute-start | bytes 49160 | tf_op jit(solution)/shard_map/ppermute | solution.py:308
  2.0 2.5 %body_kernel.1 = (bf16[256,1024]{1,0:T(8,128)(2,1)S(1)}, bf16[256,1024]{1,0:T(8,128)(2,1)S(1)}, bf16[256,384]{1,0:T(8,128)(2,1)S(1)}, bf16[256,384]{1,0:T(8,128)...) custom-call(s32[1]{0:T(128)} %bitcast.refs_0_, ...), custom_call_target="tpu_custom_call", output_to_operand_aliasing={{5}: (4, {})} | custom-call | flops 1610612736 | tf_op jit(solution)/shard_map/body_kernel/pallas_call | solution.py:64
  4.5 3.7 %collective-permute-done.refs_1_ = f32[8,512]{1,0:T(8,128)S(1)} collective-permute-done((f32[8,512]{1,0:T(8,128)S(1)}, f32[8,512]{1,0:T(8,128)S(1)}, u32[]{:S(2)}, u32[]{:S(2)}) %collective-permute-start) | collective-permute-done | bytes 16416 | tf_op jit(solution)/shard_map/ppermute | solution.py:308
  8.2 1.3 %head_kernel.1 = (f32[520,128]{1,0:T(8,128)S(1)}, bf16[256,128]{1,0:T(8,128)(2,1)S(1)}, bf16[256,128]{1,0:T(8,128)(2,1)S(1)}, bf16[1024,128]{1,0:T(8,128)(2,1)S(...) custom-call(s32[1]{0:T(128)} %bitcast.refs_0_, ...), custom_call_target="tpu_custom_call", output_to_operand_aliasing={{6}: (7, {})} | custom-call | tf_op jit(solution)/shard_map/head_kernel/pallas_call | solution.py:64
  9.6 0.4 away_kernel.1
  10.0 0.6 %collective-permute-start.1 = (f32[64,8,128]{2,1,0:T(8,128)S(1)}, f32[64,8,128]{2,1,0:T(8,128)S(1)}, u32[]{:S(2)}, u32[]{:S(2)}) collective-permute-start(f32[64,8,128]{2,1,0:T(8,128)S(1)} %bitcast.10), channel_id=1, source_target_pairs={{0,1},{1,0},{2,3},{3,2},{4,5},{5,4},{6,7},{7,6},{8,9},{9,8},{10,11... | collective-permute-start | bytes 786440 | tf_op jit(solution)/shard_map/ppermute | solution.py:300
  10.5 0.4 home_kernel.1
  11.2 0.5 %collective-permute-done.1.refs_2_ = f32[64,8,128]{2,1,0:T(8,128)S(1)} collective-permute-done((f32[64,8,128]{2,1,0:T(8,128)S(1)}, f32[64,8,128]{2,1,0:T(8,128)S(1)}, u32[]{:S(2)}, u32[]{:S(2)}) %collective-permute-start.1) | collective-permute-done | bytes 262176 | tf_op jit(solution)/shard_map/ppermute | solution.py:300
  11.7 1.6 %collective-permute-start.3 = (f32[32,8,128]{2,1,0:T(8,128)S(1)}, f32[32,8,128]{2,1,0:T(8,128)S(1)}, u32[]{:S(2)}, u32[]{:S(2)}) collective-permute-start(f32[32,8,128]{2,1,0:T(8,128)S(1)} %get-tuple-element.83), channel_id=1, source_target_pairs={{0,2},{1,9},{2,0},{3,11},{4,6},{5,13},{6,4},{7,15},{8,10},{9,1},{1... | collective-permute-start | bytes 393224 | tf_op jit(solution)/shard_map/ppermute | solution.py:300
  13.3 1.8 %lagged_kernel.1 = (f32[8,768]{1,0:T(8,128)S(1)}, f32[8,128]{1,0:T(8,128)S(1)}) custom-call(s32[1]{0:T(128)} %bitcast.refs_0_, bf16[256,1024]{1,0:T(8,128)(2,1)S(1)} %get-tuple-element.65.refs_4_.refs_1_, bf16[256,1024]{1,0:T(8,128)(2,1)S(1)} %get-tuple-element.66.refs_5_.refs_2_, ...), custom_call_target="tpu_custom_call", output_to_operand_aliasing={{1}: (7, {})} | custom-call | flops 805306368 | tf_op jit(solution)/shard_map/lagged_kernel/pallas_call | solution.py:64
  15.1 1.1 %collective-permute-done.4.refs_2_ = f32[33,8,128]{2,1,0:T(8,128)S(1)} collective-permute-done((f32[33,8,128]{2,1,0:T(8,128)S(1)}, f32[33,8,128]{2,1,0:T(8,128)S(1)}, u32[]{:S(2)}, u32[]{:S(2)}) %collective-permute-start.4) | collective-permute-done | bytes 135200 | tf_op jit(solution)/shard_map/ppermute | solution.py:300
  16.2 0.3 collective-permute-start.7
  16.5 1.1 %collective-permute-done.3.refs_2_ = f32[32,8,128]{2,1,0:T(8,128)S(1)} collective-permute-done((f32[32,8,128]{2,1,0:T(8,128)S(1)}, f32[32,8,128]{2,1,0:T(8,128)S(1)}, u32[]{:S(2)}, u32[]{:S(2)}) %collective-permute-start.3) | collective-permute-done | bytes 131104 | tf_op jit(solution)/shard_map/ppermute | solution.py:300
  17.6 0.8 %collective-permute-start.5 = (f32[16,8,128]{2,1,0:T(8,128)S(1)}, f32[16,8,128]{2,1,0:T(8,128)S(1)}, u32[]{:S(2)}, u32[]{:S(2)}) collective-permute-start(f32[16,8,128]{2,1,0:T(8,128)S(1)} %get-tuple-element.92), channel_id=1, source_target_pairs={{0,4},{1,3},{2,6},{3,1},{4,0},{5,7},{6,2},{7,5},{8,12},{9,11},{10,... | collective-permute-start | bytes 196616 | tf_op jit(solution)/shard_map/ppermute | solution.py:300
  18.4 1.9 %collective-permute-start.6 = (f32[8,768]{1,0:T(8,128)S(1)}, f32[8,768]{1,0:T(8,128)S(1)}, u32[]{:S(2)}, u32[]{:S(2)}) collective-permute-start(f32[8,768]{1,0:T(8,128)S(1)} %get-tuple-element.93.refs_1_), channel_id=1, source_target_pairs={{0,16},{16,0},{1,17},{17,1},{2,18},{18,2},{3,19},{19,3},{4,20},{20... | collective-permute-start | bytes 73736 | tf_op jit(solution)/shard_map/ppermute | solution.py:358
  20.4 0.6 %collective-permute-done.7.refs_2_ = f32[17,8,128]{2,1,0:T(8,128)S(1)} collective-permute-done((f32[17,8,128]{2,1,0:T(8,128)S(1)}, f32[17,8,128]{2,1,0:T(8,128)S(1)}, u32[]{:S(2)}, u32[]{:S(2)}) %collective-permute-start.7) | collective-permute-done | bytes 69664 | tf_op jit(solution)/shard_map/ppermute | solution.py:300
  20.9 1.1 %collective-permute-start.9 = (f32[18,8,128]{2,1,0:T(8,128)S(1)}, f32[18,8,128]{2,1,0:T(8,128)S(1)}, u32[]{:S(2)}, u32[]{:S(2)}) collective-permute-start(f32[18,8,128]{2,1,0:T(8,128)S(1)} %get-tuple-element.101.refs_1_), channel_id=1, source_target_pairs={{0,8},{1,5},{2,10},{3,7},{4,12},{5,1},{6,14},{7,3},{8,0},{9,13},{1... | collective-permute-start | bytes 221192 | tf_op jit(solution)/shard_map/ppermute | solution.py:300
  22.5 2.2 %collective-permute-start.8 = (f32[17,8,128]{2,1,0:T(8,128)S(1)}, f32[17,8,128]{2,1,0:T(8,128)S(1)}, u32[]{:S(2)}, u32[]{:S(2)}) collective-permute-start(f32[17,8,128]{2,1,0:T(8,128)S(1)} %get-tuple-element.100.refs_1_), channel_id=1, source_target_pairs={{0,8},{1,5},{2,10},{3,7},{4,12},{5,1},{6,14},{7,3},{8,0},{9,13},{1... | collective-permute-start | bytes 208904 | tf_op jit(solution)/shard_map/ppermute | solution.py:300
  24.7 2.2 %collective-permute-done.9.refs_2_ = f32[18,8,128]{2,1,0:T(8,128)S(1)} collective-permute-done((f32[18,8,128]{2,1,0:T(8,128)S(1)}, f32[18,8,128]{2,1,0:T(8,128)S(1)}, u32[]{:S(2)}, u32[]{:S(2)}) %collective-permute-start.9) | collective-permute-done | bytes 73760 | tf_op jit(solution)/shard_map/ppermute | solution.py:300
  26.9 0.6 %collective-permute-start.11 = (f32[18,8,128]{2,1,0:T(8,128)S(1)}, f32[18,8,128]{2,1,0:T(8,128)S(1)}, u32[]{:S(2)}, u32[]{:S(2)}) collective-permute-start(f32[18,8,128]{2,1,0:T(8,128)S(1)} %get-tuple-element.106.refs_1_), channel_id=1, source_target_pairs={{0,2},{1,9},{2,0},{3,11},{4,6},{5,13},{6,4},{7,15},{8,10},{9,1},{1... | collective-permute-start | bytes 221192 | tf_op jit(solution)/shard_map/ppermute | solution.py:300
  27.5 0.5 %collective-permute-done.8.refs_2_ = f32[17,8,128]{2,1,0:T(8,128)S(1)} collective-permute-done((f32[17,8,128]{2,1,0:T(8,128)S(1)}, f32[17,8,128]{2,1,0:T(8,128)S(1)}, u32[]{:S(2)}, u32[]{:S(2)}) %collective-permute-start.8) | collective-permute-done | bytes 69664 | tf_op jit(solution)/shard_map/ppermute | solution.py:300
  27.9 1.1 %collective-permute-start.10 = (f32[17,8,128]{2,1,0:T(8,128)S(1)}, f32[17,8,128]{2,1,0:T(8,128)S(1)}, u32[]{:S(2)}, u32[]{:S(2)}) collective-permute-start(f32[17,8,128]{2,1,0:T(8,128)S(1)} %get-tuple-element.105.refs_1_), channel_id=1, source_target_pairs={{0,2},{1,9},{2,0},{3,11},{4,6},{5,13},{6,4},{7,15},{8,10},{9,1},{1... | collective-permute-start | bytes 208904 | tf_op jit(solution)/shard_map/ppermute | solution.py:300
  29.1 2.2 %collective-permute-done.11.refs_2_ = f32[18,8,128]{2,1,0:T(8,128)S(1)} collective-permute-done((f32[18,8,128]{2,1,0:T(8,128)S(1)}, f32[18,8,128]{2,1,0:T(8,128)S(1)}, u32[]{:S(2)}, u32[]{:S(2)}) %collective-permute-start.11) | collective-permute-done | bytes 73760 | tf_op jit(solution)/shard_map/ppermute | solution.py:300
  31.3 0.9 %collective-permute-start.13 = (f32[34,8,128]{2,1,0:T(8,128)S(1)}, f32[34,8,128]{2,1,0:T(8,128)S(1)}, u32[]{:S(2)}, u32[]{:S(2)}) collective-permute-start(f32[34,8,128]{2,1,0:T(8,128)S(1)} %get-tuple-element.110.refs_1_), channel_id=1, source_target_pairs={{0,4},{1,3},{2,6},{3,1},{4,0},{5,7},{6,2},{7,5},{8,12},{9,11},{10,... | collective-permute-start | bytes 417800 | tf_op jit(solution)/shard_map/ppermute | solution.py:300
  32.3 2.2 %collective-permute-start.12 = (f32[33,8,128]{2,1,0:T(8,128)S(1)}, f32[33,8,128]{2,1,0:T(8,128)S(1)}, u32[]{:S(2)}, u32[]{:S(2)}) collective-permute-start(f32[33,8,128]{2,1,0:T(8,128)S(1)} %get-tuple-element.109.refs_1_), channel_id=1, source_target_pairs={{0,4},{1,3},{2,6},{3,1},{4,0},{5,7},{6,2},{7,5},{8,12},{9,11},{10,... | collective-permute-start | bytes 405512 | tf_op jit(solution)/shard_map/ppermute | solution.py:300
  34.5 1.9 %collective-permute-done.13.refs_2_ = f32[34,8,128]{2,1,0:T(8,128)S(1)} collective-permute-done((f32[34,8,128]{2,1,0:T(8,128)S(1)}, f32[34,8,128]{2,1,0:T(8,128)S(1)}, u32[]{:S(2)}, u32[]{:S(2)}) %collective-permute-start.13) | collective-permute-done | bytes 139296 | tf_op jit(solution)/shard_map/ppermute | solution.py:300
  36.6 0.7 %store_kernel.3 = (f32[256,8,128]{2,1,0:T(8,128)}, f32[8,128]{1,0:T(8,128)S(1)}) custom-call(s32[1]{0:T(128)} %bitcast.refs_0_, f32[66,8,128]{2,1,0:T(8,128)S(1)} %get-tuple-element.112.refs_1_, f32[8,128]{1,0:T(8,128)S(1)} %get-tuple-element.113.refs_2_), custom_call_target="tpu_custom_call", output_to_operand_aliasing={{1}: (2, {})} | custom-call | tf_op jit(solution)/shard_map/store_kernel/pallas_call | solution.py:64
  37.3 0.6 %collective-permute-done.12.refs_2_ = f32[33,8,128]{2,1,0:T(8,128)S(1)} collective-permute-done((f32[33,8,128]{2,1,0:T(8,128)S(1)}, f32[33,8,128]{2,1,0:T(8,128)S(1)}, u32[]{:S(2)}, u32[]{:S(2)}) %collective-permute-start.12) | collective-permute-done | bytes 135200 | tf_op jit(solution)/shard_map/ppermute | solution.py:300
  38.1 0.8 %store_kernel.4 = (f32[256,8,128]{2,1,0:T(8,128)}, f32[8,128]{1,0:T(8,128)S(1)}) custom-call(s32[1]{0:T(128)} %bitcast.refs_0_, f32[66,8,128]{2,1,0:T(8,128)S(1)} %collective-permute-done.15.refs_1_, f32[65,8,128]{2,1,0:T(8,128)S(1)} %get-tuple-element.115.refs_2_, ...), custom_call_target="tpu_custom_call", output_to_operand_aliasing={{0}: (3, {}), {1}: (4, {})} | custom-call | tf_op jit(solution)/shard_map/store_kernel/pallas_call | solution.py:64
  38.9 0.6 %collective-permute-done.14.refs_1_ = f32[65,8,128]{2,1,0:T(8,128)S(1)} collective-permute-done((f32[65,8,128]{2,1,0:T(8,128)S(1)}, f32[65,8,128]{2,1,0:T(8,128)S(1)}, u32[]{:S(2)}, u32[]{:S(2)}) %collective-permute-start.14) | collective-permute-done | bytes 266272 | tf_op jit(solution)/shard_map/ppermute | solution.py:300
  39.5 0.7 %store_kernel.5 = (f32[256,8,128]{2,1,0:T(8,128)}, f32[8,512]{1,0:T(8,128)}, f32[8,128]{1,0:T(8,128)S(1)}) custom-call(s32[1]{0:T(128)} %bitcast.refs_0_, f32[65,8,128]{2,1,0:T(8,128)S(1)} %collective-permute-done.14.refs_1_, f32[8,512]{1,0:T(8,128)S(1)} %get-tuple-element.116.refs_2_, ...), custom_call_target="tpu_custom_call", output_to_operand_aliasing={{0}: (4, {}), {2}: (5, {})} | custom-call | tf_op jit(solution)/shard_map/store_kernel/pallas_call | solution.py:64
  (28 shorter events, 1.5 us)
Async XLA Ops:
  0.6 0.7 %copy-start.2 = (f32[8,512]{1,0:T(8,128)S(1)}, f32[8,512]{1,0:T(8,128)}, u32[]{:S(2)}) copy-start(f32[8,512]{1,0:T(8,128)} %refs_3_.5) | copy-start | bytes 49156
  0.6 1.2 %copy-start = (f32[256,8,128]{2,1,0:T(8,128)S(1)}, f32[256,8,128]{2,1,0:T(8,128)}, u32[]{:S(2)}) copy-start(f32[256,8,128]{2,1,0:T(8,128)} %refs_4_.3) | copy-start | bytes 3145732
  0.7 1.4 %copy-start.1 = (f32[256,512]{1,0:T(8,128)S(1)}, f32[256,512]{1,0:T(8,128)}, u32[]{:S(2)}) copy-start(f32[256,512]{1,0:T(8,128)} %refs_2_.1) | copy-start | bytes 1572868
  1.4 6.9 %collective-permute-start = (f32[8,512]{1,0:T(8,128)S(1)}, f32[8,512]{1,0:T(8,128)S(1)}, u32[]{:S(2)}, u32[]{:S(2)}) collective-permute-start(f32[8,512]{1,0:T(8,128)S(1)} %copy-done.2), channel_id=1, source_target_pairs={{0,1},{1,2},{2,3},{3,4},{4,5},{5,6},{6,7},{7,8},{8,9},{9,10},{10,1... | collective-permute-start | bytes 49160 | tf_op jit(solution)/shard_map/ppermute | solution.py:308
  9.5 1.6 %collective-permute-start.2 = (f32[65,8,128]{2,1,0:T(8,128)S(1)}, f32[65,8,128]{2,1,0:T(8,128)S(1)}, u32[]{:S(2)}, u32[]{:S(2)}) collective-permute-start(f32[65,8,128]{2,1,0:T(8,128)S(1)} %bitcast.9), channel_id=1, source_target_pairs={{0,1},{1,0},{2,3},{3,2},{4,5},{5,4},{6,7},{7,6},{8,9},{9,8},{10,11... | collective-permute-start | bytes 798728 | tf_op jit(solution)/shard_map/ppermute | solution.py:300
  10.0 1.7 %collective-permute-start.1 = (f32[64,8,128]{2,1,0:T(8,128)S(1)}, f32[64,8,128]{2,1,0:T(8,128)S(1)}, u32[]{:S(2)}, u32[]{:S(2)}) collective-permute-start(f32[64,8,128]{2,1,0:T(8,128)S(1)} %bitcast.10), channel_id=1, source_target_pairs={{0,1},{1,0},{2,3},{3,2},{4,5},{5,4},{6,7},{7,6},{8,9},{9,8},{10,11... | collective-permute-start | bytes 786440 | tf_op jit(solution)/shard_map/ppermute | solution.py:300
  11.1 5.1 %collective-permute-start.4 = (f32[33,8,128]{2,1,0:T(8,128)S(1)}, f32[33,8,128]{2,1,0:T(8,128)S(1)}, u32[]{:S(2)}, u32[]{:S(2)}) collective-permute-start(f32[33,8,128]{2,1,0:T(8,128)S(1)} %get-tuple-element.85), channel_id=1, source_target_pairs={{0,2},{1,9},{2,0},{3,11},{4,6},{5,13},{6,4},{7,15},{8,10},{9,1},{1... | collective-permute-start | bytes 405512 | tf_op jit(solution)/shard_map/ppermute | solution.py:300
  11.7 5.9 %collective-permute-start.3 = (f32[32,8,128]{2,1,0:T(8,128)S(1)}, f32[32,8,128]{2,1,0:T(8,128)S(1)}, u32[]{:S(2)}, u32[]{:S(2)}) collective-permute-start(f32[32,8,128]{2,1,0:T(8,128)S(1)} %get-tuple-element.83), channel_id=1, source_target_pairs={{0,2},{1,9},{2,0},{3,11},{4,6},{5,13},{6,4},{7,15},{8,10},{9,1},{1... | collective-permute-start | bytes 393224 | tf_op jit(solution)/shard_map/ppermute | solution.py:300
  16.2 4.7 %collective-permute-start.7 = (f32[17,8,128]{2,1,0:T(8,128)S(1)}, f32[17,8,128]{2,1,0:T(8,128)S(1)}, u32[]{:S(2)}, u32[]{:S(2)}) collective-permute-start(f32[17,8,128]{2,1,0:T(8,128)S(1)} %get-tuple-element.95), channel_id=1, source_target_pairs={{0,4},{1,3},{2,6},{3,1},{4,0},{5,7},{6,2},{7,5},{8,12},{9,11},{10,... | collective-permute-start | bytes 208904 | tf_op jit(solution)/shard_map/ppermute | solution.py:300
  17.6 4.9 %collective-permute-start.5 = (f32[16,8,128]{2,1,0:T(8,128)S(1)}, f32[16,8,128]{2,1,0:T(8,128)S(1)}, u32[]{:S(2)}, u32[]{:S(2)}) collective-permute-start(f32[16,8,128]{2,1,0:T(8,128)S(1)} %get-tuple-element.92), channel_id=1, source_target_pairs={{0,4},{1,3},{2,6},{3,1},{4,0},{5,7},{6,2},{7,5},{8,12},{9,11},{10,... | collective-permute-start | bytes 196616 | tf_op jit(solution)/shard_map/ppermute | solution.py:300
  18.4 3.8 %collective-permute-start.6 = (f32[8,768]{1,0:T(8,128)S(1)}, f32[8,768]{1,0:T(8,128)S(1)}, u32[]{:S(2)}, u32[]{:S(2)}) collective-permute-start(f32[8,768]{1,0:T(8,128)S(1)} %get-tuple-element.93.refs_1_), channel_id=1, source_target_pairs={{0,16},{16,0},{1,17},{17,1},{2,18},{18,2},{3,19},{19,3},{4,20},{20... | collective-permute-start | bytes 73736 | tf_op jit(solution)/shard_map/ppermute | solution.py:358
  20.9 5.9 %collective-permute-start.9 = (f32[18,8,128]{2,1,0:T(8,128)S(1)}, f32[18,8,128]{2,1,0:T(8,128)S(1)}, u32[]{:S(2)}, u32[]{:S(2)}) collective-permute-start(f32[18,8,128]{2,1,0:T(8,128)S(1)} %get-tuple-element.101.refs_1_), channel_id=1, source_target_pairs={{0,8},{1,5},{2,10},{3,7},{4,12},{5,1},{6,14},{7,3},{8,0},{9,13},{1... | collective-permute-start | bytes 221192 | tf_op jit(solution)/shard_map/ppermute | solution.py:300
  22.5 5.4 %collective-permute-start.8 = (f32[17,8,128]{2,1,0:T(8,128)S(1)}, f32[17,8,128]{2,1,0:T(8,128)S(1)}, u32[]{:S(2)}, u32[]{:S(2)}) collective-permute-start(f32[17,8,128]{2,1,0:T(8,128)S(1)} %get-tuple-element.100.refs_1_), channel_id=1, source_target_pairs={{0,8},{1,5},{2,10},{3,7},{4,12},{5,1},{6,14},{7,3},{8,0},{9,13},{1... | collective-permute-start | bytes 208904 | tf_op jit(solution)/shard_map/ppermute | solution.py:300
  26.9 4.4 %collective-permute-start.11 = (f32[18,8,128]{2,1,0:T(8,128)S(1)}, f32[18,8,128]{2,1,0:T(8,128)S(1)}, u32[]{:S(2)}, u32[]{:S(2)}) collective-permute-start(f32[18,8,128]{2,1,0:T(8,128)S(1)} %get-tuple-element.106.refs_1_), channel_id=1, source_target_pairs={{0,2},{1,9},{2,0},{3,11},{4,6},{5,13},{6,4},{7,15},{8,10},{9,1},{1... | collective-permute-start | bytes 221192 | tf_op jit(solution)/shard_map/ppermute | solution.py:300
  27.9 4.4 %collective-permute-start.10 = (f32[17,8,128]{2,1,0:T(8,128)S(1)}, f32[17,8,128]{2,1,0:T(8,128)S(1)}, u32[]{:S(2)}, u32[]{:S(2)}) collective-permute-start(f32[17,8,128]{2,1,0:T(8,128)S(1)} %get-tuple-element.105.refs_1_), channel_id=1, source_target_pairs={{0,2},{1,9},{2,0},{3,11},{4,6},{5,13},{6,4},{7,15},{8,10},{9,1},{1... | collective-permute-start | bytes 208904 | tf_op jit(solution)/shard_map/ppermute | solution.py:300
  31.3 5.1 %collective-permute-start.13 = (f32[34,8,128]{2,1,0:T(8,128)S(1)}, f32[34,8,128]{2,1,0:T(8,128)S(1)}, u32[]{:S(2)}, u32[]{:S(2)}) collective-permute-start(f32[34,8,128]{2,1,0:T(8,128)S(1)} %get-tuple-element.110.refs_1_), channel_id=1, source_target_pairs={{0,4},{1,3},{2,6},{3,1},{4,0},{5,7},{6,2},{7,5},{8,12},{9,11},{10,... | collective-permute-start | bytes 417800 | tf_op jit(solution)/shard_map/ppermute | solution.py:300
  32.3 5.6 %collective-permute-start.12 = (f32[33,8,128]{2,1,0:T(8,128)S(1)}, f32[33,8,128]{2,1,0:T(8,128)S(1)}, u32[]{:S(2)}, u32[]{:S(2)}) collective-permute-start(f32[33,8,128]{2,1,0:T(8,128)S(1)} %get-tuple-element.109.refs_1_), channel_id=1, source_target_pairs={{0,4},{1,3},{2,6},{3,1},{4,0},{5,7},{6,2},{7,5},{8,12},{9,11},{10,... | collective-permute-start | bytes 405512 | tf_op jit(solution)/shard_map/ppermute | solution.py:300
  36.5 1.6 %collective-permute-start.15 = (f32[66,8,128]{2,1,0:T(8,128)S(1)}, f32[66,8,128]{2,1,0:T(8,128)S(1)}, u32[]{:S(2)}, u32[]{:S(2)}) collective-permute-start(f32[66,8,128]{2,1,0:T(8,128)S(1)} %get-tuple-element.112.refs_1_), channel_id=1, source_target_pairs={{0,1},{1,0},{2,3},{3,2},{4,5},{5,4},{6,7},{7,6},{8,9},{9,8},{10,11... | collective-permute-start | bytes 811016 | tf_op jit(solution)/shard_map/ppermute | solution.py:300
  37.9 1.6 %collective-permute-start.14 = (f32[65,8,128]{2,1,0:T(8,128)S(1)}, f32[65,8,128]{2,1,0:T(8,128)S(1)}, u32[]{:S(2)}, u32[]{:S(2)}) collective-permute-start(f32[65,8,128]{2,1,0:T(8,128)S(1)} %get-tuple-element.115.refs_2_), channel_id=1, source_target_pairs={{0,1},{1,0},{2,3},{3,2},{4,5},{5,4},{6,7},{7,6},{8,9},{9,8},{10,11... | collective-permute-start | bytes 798728 | tf_op jit(solution)/shard_map/ppermute | solution.py:300
